TPU v7x, 32 devices: a whole 2x2x4 slice. The times are simulated.
32 devices in a mesh: clip: 4 (over x, core), tube: 2 (over y), head: 4 (over z).
Axes of the slice: x: 2, y: 2, z: 4, core: 2. Of those that a mesh axis runs over, the one named last changes fastest.
Arguments:
- tokens: bfloat16 [4, 16, 16, 16, 768], P('clip', None, 'tube'), may hold values from -6 to 6
- token_mask: int32 [4, 16, 16, 16], P('clip', None, 'tube'), may hold values from 0 to 1, as said below
- mask_embed: float32 [768], replicated, may hold values from -5 to 5
- norm_gains: float32 [2, 2, 768], replicated, may hold values from 0.5 to 1.5
- norm_shifts: float32 [2, 2, 768], replicated, may hold values from -2 to 2
- w_qkv: bfloat16 [2, 768, 3, 768], P(None, None, None, 'head'), may hold values from -0.21875 to 0.21875
- b_qv: float32 [2, 2, 768], P(None, None, 'head'), may hold values from -2 to 2
- w_out: bfloat16 [2, 768, 768], P(None, 'head'), may hold values from -0.875 to 0.875
- b_out: float32 [2, 768], replicated, may hold values from -2 to 2
- w_up: bfloat16 [2, 768, 3072], P(None, None, 'head'), may hold values from -0.21875 to 0.21875
- b_up: float32 [2, 3072], P(None, 'head'), may hold values from -2 to 2
- w_down: bfloat16 [2, 3072, 768], P(None, 'head'), may hold values from -0.109375 to 0.109375
- b_down: float32 [2, 768], replicated, may hold values from -2 to 2
- cotangent: bfloat16 [4, 16, 16, 16, 768], P('clip', None, 'tube'), may hold values from -6 to 6
Outputs:
- result: bfloat16 [4, 16, 16, 16, 768], P('clip', None, 'tube')
- grad_tokens: bfloat16 [4, 16, 16, 16, 768], P('clip', None, 'tube')
- grad_mask_embed: float32 [768], replicated
- grad_norm_gains: float32 [2, 2, 768], replicated
- grad_norm_shifts: float32 [2, 2, 768], replicated
- grad_w_qkv: float32 [2, 768, 3, 768], P(None, None, None, 'head')
- grad_b_qv: float32 [2, 2, 768], P(None, None, 'head')
- grad_w_out: float32 [2, 768, 768], P(None, 'head')
- grad_b_out: float32 [2, 768], replicated
- grad_w_up: float32 [2, 768, 3072], P(None, None, 'head')
- grad_b_up: float32 [2, 3072], P(None, 'head')
- grad_w_down: float32 [2, 3072, 768], P(None, 'head')
- grad_b_down: float32 [2, 768], replicated
Inputs may be any that keep to these rules, and one draw needn't show every extreme that they name: token_mask is 1 where a token is masked; each clip masks its tokens at a rate of its own between one half and all.
All inputs are finite; a program needn't handle non-finite values.
Results may differ from a plain program's by a relative error of at most 0.03.
Values may be sent and summed in bfloat16 or wider, within the bound.
A program may use at most 256 MiB of HBM per device.

v0:
```python
import jax
import jax.numpy as jnp
from jax import lax
from jax.sharding import PartitionSpec as P

HD = 64


EPS = 1e-05


def norm_forward(values, gain_vector, shift_vector):
    centre = values - jnp.mean(values, -1, keepdims=True)
    inverse = lax.rsqrt(jnp.mean(centre * centre, -1, keepdims=True) + EPS)
    normal = centre * inverse
    return (normal * gain_vector + shift_vector, normal, inverse)


def norm_backward(grad_out, normal, inverse, gain_vector):
    grad_normal = grad_out * gain_vector
    grad_in = inverse * (
        grad_normal
        - jnp.mean(grad_normal, -1, keepdims=True)
        - normal * jnp.mean(grad_normal * normal, -1, keepdims=True)
    )
    return (grad_in, jnp.sum(grad_out * normal, 0), jnp.sum(grad_out, 0))


def row_total(partial_sum):
    return lax.psum(partial_sum.astype(jnp.bfloat16), "head").astype(jnp.float32)


def input_total(partial_sum):
    return lax.psum(partial_sum.astype(jnp.bfloat16), "head").astype(jnp.float32)


def split_heads(tensor, batch_count, length):
    return tensor.reshape(batch_count, length, tensor.shape[-1] // HD, HD)


def attend(queries, key_rows, value_rows):
    scores = jnp.einsum(
        "bshe,bthe->bhst", queries, key_rows, preferred_element_type=jnp.float32
    ) * HD ** (-0.5)
    maximum = jnp.max(scores, -1, keepdims=True)
    exponent = jnp.exp(scores - maximum)
    denominator = jnp.sum(exponent, -1, keepdims=True)
    weights_soft = (exponent / denominator).astype(jnp.bfloat16)
    mixture = jnp.einsum(
        "bhst,bthe->bshe", weights_soft, value_rows, preferred_element_type=jnp.float32
    )
    return (mixture.astype(jnp.bfloat16), maximum + jnp.log(denominator))


def attend_back(queries, key_rows, value_rows, log_total, grad_mixture):
    scaling = HD ** (-0.5)
    scores = (
        jnp.einsum("bshe,bthe->bhst", queries, key_rows, preferred_element_type=jnp.float32)
        * scaling
    )
    weights_soft = jnp.exp(scores - log_total)
    grad_weights = jnp.einsum(
        "bshe,bthe->bhst", grad_mixture, value_rows, preferred_element_type=jnp.float32
    )
    grad_values = jnp.einsum(
        "bhst,bshe->bthe",
        weights_soft.astype(jnp.bfloat16),
        grad_mixture,
        preferred_element_type=jnp.float32,
    )
    grad_scores = (
        weights_soft * (grad_weights - jnp.sum(weights_soft * grad_weights, -1, keepdims=True))
    ).astype(jnp.bfloat16)
    grad_queries = (
        jnp.einsum("bhst,bthe->bshe", grad_scores, key_rows, preferred_element_type=jnp.float32)
        * scaling
    )
    grad_keys = (
        jnp.einsum("bhst,bshe->bthe", grad_scores, queries, preferred_element_type=jnp.float32)
        * scaling
    )
    return (grad_queries, grad_keys, grad_values)


def mixer_forward(block_kind, queries, key_rows, value_rows):
    clip_count, frame_count, tube_count, patch_count, columns = queries.shape
    if block_kind == 1:
        reorder = (0, 2, 1, 3, 4)
        pieces = [
            split_heads(
                tensor.transpose(reorder), clip_count * tube_count, frame_count * patch_count
            )
            for tensor in (queries, key_rows, value_rows)
        ]
        mixture, log_total = attend(pieces[0], pieces[1], pieces[2])
        mixture = mixture.reshape(
            clip_count, tube_count, frame_count, patch_count, columns
        ).transpose(reorder)
        return (mixture, (pieces, log_total))
    key_all, value_all = (
        lax.all_gather(key_rows, "tube", axis=2, tiled=True),
        lax.all_gather(value_rows, "tube", axis=2, tiled=True),
    )
    tube_all = key_all.shape[2]
    pieces = [
        split_heads(queries, clip_count * frame_count, tube_count * patch_count),
        split_heads(key_all, clip_count * frame_count, tube_all * patch_count),
        split_heads(value_all, clip_count * frame_count, tube_all * patch_count),
    ]
    mixture, log_total = attend(pieces[0], pieces[1], pieces[2])
    return (
        mixture.reshape(clip_count, frame_count, tube_count, patch_count, columns),
        (pieces, log_total),
    )


def mixer_backward(block_kind, retained, grad_mixture):
    pieces, log_total = retained
    clip_count, frame_count, tube_count, patch_count, columns = grad_mixture.shape
    if block_kind == 1:
        reorder = (0, 2, 1, 3, 4)
        moved = split_heads(
            grad_mixture.transpose(reorder), clip_count * tube_count, frame_count * patch_count
        )
        gradients = attend_back(pieces[0], pieces[1], pieces[2], log_total, moved)
        return [
            grad.astype(jnp.bfloat16)
            .reshape(clip_count, tube_count, frame_count, patch_count, columns)
            .transpose(reorder)
            for grad in gradients
        ]
    gradients = attend_back(
        pieces[0],
        pieces[1],
        pieces[2],
        log_total,
        split_heads(grad_mixture, clip_count * frame_count, tube_count * patch_count),
    )
    tube_all = pieces[1].shape[1] // patch_count
    grad_keys = gradients[1].reshape(clip_count, frame_count, tube_all, patch_count, columns)
    grad_values = gradients[2].reshape(clip_count, frame_count, tube_all, patch_count, columns)
    grad_keys, grad_values = (
        lax.psum_scatter(
            grad_keys.astype(jnp.bfloat16), "tube", scatter_dimension=2, tiled=True
        ).astype(jnp.float32),
        lax.psum_scatter(
            grad_values.astype(jnp.bfloat16), "tube", scatter_dimension=2, tiled=True
        ).astype(jnp.float32),
    )
    grad_queries = (
        gradients[0]
        .astype(jnp.bfloat16)
        .reshape(clip_count, frame_count, tube_count, patch_count, columns)
    )
    return [grad_queries, grad_keys.astype(jnp.bfloat16), grad_values.astype(jnp.bfloat16)]


def block_forward(block_kind, residual, layout, weights):
    gains, shifts, w_qkv, b_qv, w_out, b_out, w_up, b_up, w_down, b_down = weights
    columns = w_qkv.shape[-1]
    grid_shape = layout[:-1] + (columns,)
    normed_share, first_normal, first_inverse = norm_forward(residual, gains[0], shifts[0])
    normed = normed_share.astype(jnp.bfloat16)
    projected = jnp.einsum("rd,dcj->rcj", normed, w_qkv, preferred_element_type=jnp.float32)
    queries = (projected[:, 0] + b_qv[0]).astype(jnp.bfloat16).reshape(grid_shape)
    key_rows = projected[:, 1].astype(jnp.bfloat16).reshape(grid_shape)
    value_rows = (projected[:, 2] + b_qv[1]).astype(jnp.bfloat16).reshape(grid_shape)
    mixture, retained = mixer_forward(block_kind, queries, key_rows, value_rows)
    mixture = mixture.reshape(-1, columns)
    middle = (
        residual + row_total(jnp.dot(mixture, w_out, preferred_element_type=jnp.float32)) + b_out
    )
    second_share, second_normal, second_inverse = norm_forward(middle, gains[1], shifts[1])
    normed_two = second_share.astype(jnp.bfloat16)
    hidden = jnp.dot(normed_two, w_up, preferred_element_type=jnp.float32) + b_up
    active = jax.nn.gelu(hidden).astype(jnp.bfloat16)
    stored = (
        normed,
        first_normal,
        first_inverse,
        retained,
        mixture,
        normed_two,
        second_normal,
        second_inverse,
        hidden,
    )
    return (middle, active, stored)


def block_output(middle, active, w_down, b_down):
    return middle + row_total(jnp.dot(active, w_down, preferred_element_type=jnp.float32)) + b_down


def block_backward(block_kind, residual, layout, weights, grad_rows):
    gains, shifts, w_qkv, b_qv, w_out, b_out, w_up, b_up, w_down, b_down = weights
    middle, active, stored = block_forward(block_kind, residual, layout, weights)
    (
        normed,
        first_normal,
        first_inverse,
        retained,
        mixture,
        normed_two,
        second_normal,
        second_inverse,
        hidden,
    ) = stored
    columns = w_qkv.shape[-1]
    grad_low = grad_rows.astype(jnp.bfloat16)
    grad_wdown = jnp.dot(active.T, grad_low, preferred_element_type=jnp.float32)
    grad_bdown = jnp.sum(grad_rows, 0)
    grad_active = jnp.dot(grad_low, w_down.T, preferred_element_type=jnp.float32)
    gelu_pull = jax.vjp(jax.nn.gelu, hidden)[1]
    grad_hidden = gelu_pull(grad_active)[0].astype(jnp.bfloat16)
    grad_bup = jnp.sum(grad_hidden.astype(jnp.float32), 0)
    grad_wup = jnp.dot(normed_two.T, grad_hidden, preferred_element_type=jnp.float32)
    grad_normed_two = input_total(jnp.dot(grad_hidden, w_up.T, preferred_element_type=jnp.float32))
    grad_norm, grad_gain_two, grad_shift_two = norm_backward(
        grad_normed_two, second_normal, second_inverse, gains[1]
    )
    grad_middle = grad_rows + grad_norm
    grad_bout = jnp.sum(grad_middle, 0)
    grad_mid_low = grad_middle.astype(jnp.bfloat16)
    grad_wout = jnp.dot(mixture.T, grad_mid_low, preferred_element_type=jnp.float32)
    grad_mixture = jnp.dot(grad_mid_low, w_out.T, preferred_element_type=jnp.float32).astype(
        jnp.bfloat16
    )
    grad_parts = mixer_backward(
        block_kind, retained, grad_mixture.reshape(layout[:-1] + (columns,))
    )
    grad_flat = [grad.reshape(-1, columns) for grad in grad_parts]
    grad_project = jnp.stack(grad_flat, 1)
    grad_bqv = jnp.stack(
        [jnp.sum(grad_flat[0].astype(jnp.float32), 0), jnp.sum(grad_flat[2].astype(jnp.float32), 0)]
    )
    grad_wqkv = jnp.einsum("rd,rcj->dcj", normed, grad_project, preferred_element_type=jnp.float32)
    grad_normed = input_total(
        jnp.einsum("rcj,dcj->rd", grad_project, w_qkv, preferred_element_type=jnp.float32)
    )
    grad_input, grad_gain_one, grad_shift_one = norm_backward(
        grad_normed, first_normal, first_inverse, gains[0]
    )
    gradients = (
        jnp.stack([grad_gain_one, grad_gain_two]),
        jnp.stack([grad_shift_one, grad_shift_two]),
        grad_wqkv,
        grad_bqv,
        grad_wout,
        grad_bout,
        grad_wup,
        grad_bup,
        grad_wdown,
        grad_bdown,
    )
    return (grad_middle + grad_input, gradients)


def on_device(
    tokens,
    token_mask,
    mask_embed,
    norm_gains,
    norm_shifts,
    w_qkv,
    b_qv,
    w_out,
    b_out,
    w_up,
    b_up,
    w_down,
    b_down,
    cotangent,
):
    layout = tokens.shape
    width = layout[-1]
    masked = (token_mask == 1).reshape(-1, 1)
    initial = jnp.where(masked, mask_embed[None, :], tokens.reshape(-1, width).astype(jnp.float32))
    upstream = cotangent.reshape(-1, width).astype(jnp.float32)

    def weights_of(block_kind):
        return (
            norm_gains[block_kind],
            norm_shifts[block_kind],
            w_qkv[block_kind],
            b_qv[block_kind],
            w_out[block_kind],
            b_out[block_kind],
            w_up[block_kind],
            b_up[block_kind],
            w_down[block_kind],
            b_down[block_kind],
        )

    middle, active, unused_first = block_forward(0, initial, layout, weights_of(0))
    second = block_output(middle, active, w_down[0], b_down[0])
    middle, active, unused_second = block_forward(1, second, layout, weights_of(1))
    output_rows = block_output(middle, active, w_down[1], b_down[1])
    grad_second, grads_later = block_backward(1, second, layout, weights_of(1), upstream)
    grad_initial, grads_earlier = block_backward(0, initial, layout, weights_of(0), grad_second)
    stacked = [
        jnp.stack([first_grad, later_grad])
        for first_grad, later_grad in zip(grads_earlier, grads_later)
    ]
    grad_embed = jnp.sum(jnp.where(masked, grad_initial, 0.0), 0)
    output_low = output_rows.astype(jnp.bfloat16)
    grad_low = jnp.where(masked, 0.0, grad_initial).astype(jnp.bfloat16)
    shares = (
        lax.psum_scatter(stacked[2], ("clip", "tube"), scatter_dimension=1, tiled=True),
        lax.psum_scatter(stacked[4], ("clip", "tube"), scatter_dimension=2, tiled=True),
        lax.psum_scatter(stacked[6], ("clip", "tube"), scatter_dimension=1, tiled=True),
        lax.psum_scatter(stacked[8], ("clip", "tube"), scatter_dimension=2, tiled=True),
    )
    whole = (
        lax.all_gather(shares[0].astype(jnp.bfloat16), ("clip", "tube"), axis=1, tiled=True).astype(
            jnp.float32
        ),
        lax.all_gather(shares[1].astype(jnp.bfloat16), ("clip", "tube"), axis=2, tiled=True).astype(
            jnp.float32
        ),
        lax.all_gather(shares[2].astype(jnp.bfloat16), ("clip", "tube"), axis=1, tiled=True).astype(
            jnp.float32
        ),
        lax.all_gather(shares[3].astype(jnp.bfloat16), ("clip", "tube"), axis=2, tiled=True).astype(
            jnp.float32
        ),
    )
    column_part = (
        grad_embed,
        stacked[0],
        stacked[1],
        stacked[5],
        stacked[9],
        stacked[3],
        stacked[7],
    )
    small = lax.psum(
        (
            column_part[0],
            column_part[1],
            column_part[2],
            column_part[3],
            column_part[4],
            column_part[5],
            column_part[6],
        ),
        ("clip", "tube"),
    )
    embed_grad, gain_grad, shift_grad, bout_grad, bdown_grad = (
        small[0],
        small[1],
        small[2],
        small[3],
        small[4],
    )
    bqv_grad, bup_grad = (small[5], small[6])
    return (
        output_low.reshape(layout),
        grad_low.reshape(layout),
        embed_grad,
        gain_grad,
        shift_grad,
        whole[0],
        bqv_grad,
        whole[1],
        bout_grad,
        whole[2],
        bup_grad,
        whole[3],
        bdown_grad,
    )


def solution(mesh):
    return jax.shard_map(
        on_device,
        mesh=mesh,
        in_specs=(
            P("clip", None, "tube", None, None),
            P("clip", None, "tube", None),
            P(),
            P(),
            P(),
            P(None, None, None, "head"),
            P(None, None, "head"),
            P(None, "head", None),
            P(),
            P(None, None, "head"),
            P(None, "head"),
            P(None, "head", None),
            P(),
            P("clip", None, "tube", None, None),
        ),
        out_specs=(
            P("clip", None, "tube", None, None),
            P("clip", None, "tube", None, None),
            P(),
            P(),
            P(),
            P(None, None, None, "head"),
            P(None, None, "head"),
            P(None, "head", None),
            P(),
            P(None, None, "head"),
            P(None, "head"),
            P(None, "head", None),
            P(),
        ),
        check_vma=False,
    )
```

profile of v0, /device:TPU:1, one launch (start us, length us, event | category | flops | bytes accessed | tf_op | source)
XLA Modules:
  0.0 1748.2 jit_solution(1111980832249639431)
XLA Ops:
  37.5 22.3 %all-gather.8.cloned.1.call-done = bf16[1,16,16,16,192]{4,3,2,1,0:T(8,128)(2,1)} async-done(((bf16[1,16,8,16,192]{4,3,2,1,0:T(8,128)(2,1)}), bf16[1,16,16,16,192]{4,3,2,1,0:T(8,128)(2,1)}) %all-gather.8.cloned.1.call-update) | async-done | bytes 1572880 | tf_op jit(solution)/shard_map/all_gather | solution.py:101
  59.9 8.5 reshape.413
  75.1 20.1 %all-gather.6.cloned.1.call-done = bf16[1,16,16,16,192]{4,3,2,1,0:T(8,128)(2,1)} async-done(((bf16[1,16,8,16,192]{4,3,2,1,0:T(8,128)(2,1)}), bf16[1,16,16,16,192]{4,3,2,1,0:T(8,128)(2,1)}) %all-gather.6.cloned.1.call-update) | async-done | bytes 1572880 | tf_op jit(solution)/shard_map/all_gather | solution.py:102
  95.1 8.5 reshape.412
  124.2 120.3 %all-reduce.12.cloned.1.call-done = bf16[2048,768]{1,0:T(8,128)(2,1)} async-done(((bf16[2048,768]{1,0:T(8,128)(2,1)}), bf16[2048,768]{1,0:T(8,128)(2,1)}) %all-reduce.12.cloned.1.call-update) | async-done | bytes 3145744 | tf_op jit(solution)/shard_map/psum | solution.py:30
  264.7 119.4 %all-reduce.14.cloned.1.call-done = bf16[2048,768]{1,0:T(8,128)(2,1)} async-done(((bf16[2048,768]{1,0:T(8,128)(2,1)}), bf16[2048,768]{1,0:T(8,128)(2,1)}) %all-reduce.14.cloned.1.call-update) | async-done | bytes 3145744 | tf_op jit(solution)/shard_map/psum | solution.py:30
  429.8 120.2 %all-reduce.16.cloned.1.call-done = bf16[2048,768]{1,0:T(8,128)(2,1)} async-done(((bf16[2048,768]{1,0:T(8,128)(2,1)}), bf16[2048,768]{1,0:T(8,128)(2,1)}) %all-reduce.16.cloned.1.call-update) | async-done | bytes 3145744 | tf_op jit(solution)/shard_map/psum | solution.py:30
  575.2 120.2 %all-reduce.18.cloned.1.call-done = bf16[2048,768]{1,0:T(8,128)(2,1)} async-done(((bf16[2048,768]{1,0:T(8,128)(2,1)}), bf16[2048,768]{1,0:T(8,128)(2,1)}) %all-reduce.18.cloned.1.call-update) | async-done | bytes 3145744 | tf_op jit(solution)/shard_map/psum | solution.py:34
  758.6 120.2 %all-reduce.20.cloned.1.call-done = bf16[2048,768]{1,0:T(8,128)(2,1)} async-done(((bf16[2048,768]{1,0:T(8,128)(2,1)}), bf16[2048,768]{1,0:T(8,128)(2,1)}) %all-reduce.20.cloned.1.call-update) | async-done | bytes 3145744 | tf_op jit(solution)/shard_map/psum | solution.py:34
  891.8 8.1 convert_reduce_fusion.6
  905.9 120.1 %all-reduce.22.cloned.1.call-done = bf16[2048,768]{1,0:T(8,128)(2,1)} async-done(((bf16[2048,768]{1,0:T(8,128)(2,1)}), bf16[2048,768]{1,0:T(8,128)(2,1)}) %all-reduce.22.cloned.1.call-update) | async-done | bytes 3145744 | tf_op jit(solution)/shard_map/psum | solution.py:34
  1054.4 8.5 convert_element_type.392
  1092.8 8.5 convert_element_type.388
  1109.1 9.0 convolution_convert_fusion.2
  1169.1 203.0 %all-reduce.24.cloned.1.call-done = (bf16[2048,768]{1,0:T(8,128)(2,1)}, bf16[2048,768]{1,0:T(8,128)(2,1)}) async-done(((bf16[2048,768]{1,0:T(8,128)(2,1)}, bf16[2048,768]{1,0:T(8,128)(2,1)}), (bf16[2048,768]{1,0:T(8,128)(2,1)}, bf16[2048,768]{1,0:T(8,128)(2,1)})) %all-reduce.24.cloned.1.call-update) | async-done | bytes 6291472 | tf_op jit(solution)/shard_map/psum | solution.py:34
  1378.2 7.9 select_reduce_fusion
  1393.3 8.3 reshape.442
  1419.6 7.8 convolution_bitcast_fusion
  1430.8 7.3 convolution_bitcast_fusion.1
  1440.7 8.4 copy.139
  1449.8 217.8 %all-reduce.25 = (bf16[2,768,768]{1,0,2:T(2,128)(2,1)S(1)}, f32[768]{0:T(1024)}, f32[2,2,768]{2,1,0:T(2,128)}, f32[2,2,768]{2,1,0:T(2,128)}, f32[2,2,192]{2,1,0:...) all-reduce(f32[2,768,768]{1,0,2:T(2,128)} %copy.139, ...), channel_id=7, replica_groups=mesh['clip'=4,'tube'=2,'head'=4] {'clip','tube'}, use_global_device_ids=true, to_apply=%region_58.59.clone | all-reduce | flops 1191936 | bytes 7176192
  1674.4 24.5 %all_gather.23 = bf16[2,192,768]{1,0,2:T(2,128)(2,1)} all-gather(bf16[2,192,96]{1,0,2:T(2,128)(2,1)S(1)} %copy.138), channel_id=1, replica_groups=mesh['clip'=4,'tube'=2,'head'=4] {'clip','tube'}, dimensions={2}, use_global_device_ids=true | all-gather | bytes 663552 | tf_op jit(solution)/shard_map/all_gather | solution.py:318
  1713.7 7.5 copy.142
  1721.2 12.8 all-gather.10.cloned.1.call-done
  (488 shorter events, 411.7 us)
Async XLA Ops:
  7.2 52.6 %all-gather.8.cloned.1.call-start = ((), (), s32[]{:S(2)}) async-start(), calls=%async_computation.6 | async-start | bytes 3145728 | tf_op jit(solution)/shard_map/all_gather | solution.py:101
  15.4 235.0 %copy-start.74 = (f32[768]{0:T(1024)}, f32[768]{0:T(1024)S(1)}, u32[]{:S(2)}) copy-start(f32[768]{0:T(1024)S(1)} %get-tuple-element.105) | copy-start | bytes 9220
  24.5 70.6 %all-gather.6.cloned.1.call-start = ((), (), s32[]{:S(2)}) async-start(), calls=%async_computation.5 | async-start | bytes 3145728 | tf_op jit(solution)/shard_map/all_gather | solution.py:102
  34.1 210.4 %all-reduce.12.cloned.1.call-start = ((), (), s32[]{:S(2)}) async-start(), calls=%async_computation.7 | async-start | bytes 6291456 | tf_op jit(solution)/shard_map/psum | solution.py:30
  123.3 260.8 %all-reduce.14.cloned.1.call-start = ((), (), s32[]{:S(2)}) async-start(), calls=%async_computation.8 | async-start | bytes 6291456 | tf_op jit(solution)/shard_map/psum | solution.py:30
  124.1 260.0 %copy-start.66 = (pred[2048]{0:T(1024)(128)(4,1)}, pred[2048]{0:T(1024)(128)(4,1)S(1)}, u32[]{:S(2)}) copy-start(pred[2048]{0:T(1024)(128)(4,1)S(1)} %broadcast_in_dim.32) | copy-start | bytes 6148
  124.1 260.0 %copy-start.68 = (f32[768]{0:T(1024)}, f32[768]{0:T(1024)S(1)}, u32[]{:S(2)}) copy-start(f32[768]{0:T(1024)S(1)} %get-tuple-element.55) | copy-start | bytes 9220
  124.2 767.6 %copy-start.98 = (f32[768]{0:T(1024)}, f32[768]{0:T(1024)S(1)}, u32[]{:S(2)}) copy-start(f32[768]{0:T(1024)S(1)} %get-tuple-element.53) | copy-start | bytes 9220
  124.2 984.9 %copy-start.100 = (f32[768]{0:T(1024)}, f32[768]{0:T(1024)S(1)}, u32[]{:S(2)}) copy-start(f32[768]{0:T(1024)S(1)} %get-tuple-element.52) | copy-start | bytes 9220
  263.8 286.2 %all-reduce.16.cloned.1.call-start = ((), (), s32[]{:S(2)}) async-start(), calls=%async_computation.9 | async-start | bytes 6291456 | tf_op jit(solution)/shard_map/psum | solution.py:30
  429.8 265.6 %all-reduce.18.cloned.1.call-start = ((), (), s32[]{:S(2)}) async-start(), calls=%async_computation.10 | async-start | bytes 6291456 | tf_op jit(solution)/shard_map/psum | solution.py:34
  575.1 303.7 %all-reduce.20.cloned.1.call-start = ((), (), s32[]{:S(2)}) async-start(), calls=%async_computation.11 | async-start | bytes 6291456 | tf_op jit(solution)/shard_map/psum | solution.py:34
  758.6 267.5 %all-reduce.22.cloned.1.call-start = ((), (), s32[]{:S(2)}) async-start(), calls=%async_computation.12 | async-start | bytes 6291456 | tf_op jit(solution)/shard_map/psum | solution.py:34
  905.8 217.8 %reduce-scatter.18.cloned.1.call-start = ((), (), s32[]{:S(2)}) async-start(), calls=%async_computation.18 | async-start | bytes 2359296
  1070.7 64.0 %reduce-scatter.16.cloned.1.call-start = ((), (), s32[]{:S(2)}) async-start(), calls=%async_computation.17 | async-start | bytes 2359296
  1109.0 263.1 %all-reduce.24.cloned.1.call-start = ((), (), s32[]{:S(2)}) async-start(), calls=%async_computation.21 | async-start | bytes 12582912 | tf_op jit(solution)/shard_map/psum | solution.py:34
  1148.7 280.1 %reduce-scatter.14.cloned.1.call-start = ((), (), s32[]{:S(2)}) async-start(), calls=%async_computation.14 | async-start | bytes 5308416 | tf_op jit(solution)/shard_map/reduce_scatter | solution.py:311
  1159.8 508.8 %reduce-scatter.20.cloned.1.call-start = ((), (), s32[]{:S(2)}) async-start(), calls=%async_computation.19 | async-start | bytes 3981312
  1162.1 210.0 %copy-start.77 = (f32[768]{0:T(1024)S(1)}, f32[768]{0:T(1024)}, u32[]{:S(2)}) copy-start(f32[768]{0:T(1024)} %copy-done.76) | copy-start | bytes 9220
  1167.4 210.8 %copy-start.79 = (f32[768]{0:T(1024)S(1)}, f32[768]{0:T(1024)}, u32[]{:S(2)}) copy-start(f32[768]{0:T(1024)} %copy-done.78) | copy-start | bytes 9220
  1401.7 271.4 %reduce-scatter.22.cloned.1.call-start = ((), (), s32[]{:S(2)}) async-start(), calls=%async_computation.20 | async-start | bytes 1327104
  1417.4 284.7 %all-gather.12.cloned.1.call-start = ((), (), s32[]{:S(2)}) async-start(), calls=%async_computation.15 | async-start | bytes 2654208 | tf_op jit(solution)/shard_map/all_gather | solution.py:321
  1430.7 283.0 %all-gather.14.cloned.1.call-start = ((), (), s32[]{:S(2)}) async-start(), calls=%async_computation.16 | async-start | bytes 2654208 | tf_op jit(solution)/shard_map/all_gather | solution.py:324
  1668.5 65.4 %all-gather.10.cloned.1.call-start = ((), (), s32[]{:S(2)}) async-start(), calls=%async_computation.13 | async-start | bytes 2654208 | tf_op jit(solution)/shard_map/all_gather | solution.py:315
  (116 other events, 1641.3 us)
Sparse Core Ops, SparseCore 0:
  24.6 35.1 all-gather.7
  62.0 33.1 all-gather.5
  123.4 121.0 all-reduce.11
  264.0 120.0 all-reduce.13
  429.9 120.0 all-reduce.15
  575.2 120.0 all-reduce.17
  758.7 120.0 all-reduce.19
  906.0 120.0 all-reduce.21
  1070.8 25.1 reduce-scatter.17
  1109.1 25.5 reduce-scatter.15
  1148.9 223.1 all-reduce.23
  1376.0 52.8 reduce-scatter.13
  1433.3 68.3 reduce-scatter.19
  1505.6 44.4 reduce-scatter.21
  1551.9 40.3 all-gather.11
  1668.7 33.7 all-gather.13
  1704.7 29.2 all-gather.9
where the time goes:
time: 1760 us; the launch traced here: 1750 us
  waiting for transfers between devices  983 us (56%)
  blocking collectives  242 us (14%)
  local copies, waits for them, and re-layouts  241 us (14%)
  matrix products  141 us (8%)
  other arithmetic  121 us (7%)
    psum x4, waiting for transfers between devices, input_total(): lax.psum(partial_sum.astype(jnp.bfloat16), 'head').astype(jnp.float32)  564 us
    psum x3, waiting for transfers between devices, row_total(): lax.psum(partial_sum.astype(jnp.bfloat16), 'head').astype(jnp.float32)  360 us
    unnamed x1, blocking collectives  218 us
    unnamed x269, local copies, waits for them, and re-layouts  99.9 us
    reshape x12, local copies, waits for them, and re-layouts, split_heads(): return tensor.reshape(batch_count, length, tensor.shape[-1] // HD, HD)  48.7 us
  transfers between devices with their start and end apart: 17, of which 12 were waited for; matrix products, arithmetic and copies ran while one was open for 12% of the time, Pallas kernels for 0%

commit v1 on v0

--- a/solution.py
+++ b/solution.py
@@ -1,3 +1,5 @@
+from functools import partial
+
 import jax
 import jax.numpy as jnp
 from jax import lax
@@ -256,7 +258,7 @@
     return (grad_middle + grad_input, gradients)
 
 
-def on_device(
+def on_device_sums(
     tokens,
     token_mask,
     mask_embed,
@@ -371,7 +373,279 @@
     )
 
 
+AXES = ("head", "tube", "clip")
+
+
+def gather_shards(shard, parts):
+    rows = shard.shape[0] // parts
+    index = lax.axis_index("tube") * lax.axis_size("clip") + lax.axis_index("clip")
+    piece = lax.dynamic_slice_in_dim(shard, index * rows, rows, 0)
+    return lax.all_gather(piece, AXES, axis=0, tiled=True)
+
+
+def shard_sum(partial_sum):
+    share = lax.psum_scatter(
+        partial_sum.astype(jnp.bfloat16), AXES, scatter_dimension=0, tiled=True
+    )
+    return lax.all_gather(share, ("tube", "clip"), axis=0, tiled=True)
+
+
+def local_block_forward(residual, sequences, weights):
+    gains, shifts, w_qkv, b_qv, w_out, b_out, w_up, b_up, w_down, b_down = weights
+    shards, width, columns3 = w_qkv.shape
+    columns = columns3 // 3
+    rows = residual.shape[0]
+    first, first_normal, first_inverse = norm_forward(residual, gains[0], shifts[0])
+    normed = first.astype(jnp.bfloat16)
+    projected = jnp.einsum("rd,hdc->hrc", normed, w_qkv, preferred_element_type=jnp.float32)
+    projected = projected.reshape(shards, rows, 3, columns)
+    queries = (projected[:, :, 0] + b_qv[0][:, None]).astype(jnp.bfloat16)
+    key_rows = projected[:, :, 1].astype(jnp.bfloat16)
+    value_rows = (projected[:, :, 2] + b_qv[1][:, None]).astype(jnp.bfloat16)
+    pieces = [
+        split_heads(tensor, shards * sequences, rows // sequences)
+        for tensor in (queries, key_rows, value_rows)
+    ]
+    mixture, log_total = attend(*pieces)
+    mixture = mixture.reshape(shards, rows, columns)
+    middle = (
+        residual
+        + jnp.einsum("hrc,hcd->rd", mixture, w_out, preferred_element_type=jnp.float32)
+        + b_out
+    )
+    second, second_normal, second_inverse = norm_forward(middle, gains[1], shifts[1])
+    normed_two = second.astype(jnp.bfloat16)
+    hidden = (
+        jnp.einsum("rd,hdf->hrf", normed_two, w_up, preferred_element_type=jnp.float32)
+        + b_up[:, None]
+    )
+    active = jax.nn.gelu(hidden).astype(jnp.bfloat16)
+    result = (
+        middle
+        + jnp.einsum("hrf,hfd->rd", active, w_down, preferred_element_type=jnp.float32)
+        + b_down
+    )
+    stored = (
+        normed,
+        first_normal,
+        first_inverse,
+        pieces,
+        log_total,
+        mixture,
+        normed_two,
+        second_normal,
+        second_inverse,
+        hidden,
+        active,
+    )
+    return (result, stored)
+
+
+def local_block_backward(weights, stored, grad_rows):
+    gains, shifts, w_qkv, b_qv, w_out, b_out, w_up, b_up, w_down, b_down = weights
+    (
+        normed,
+        first_normal,
+        first_inverse,
+        pieces,
+        log_total,
+        mixture,
+        normed_two,
+        second_normal,
+        second_inverse,
+        hidden,
+        active,
+    ) = stored
+    shards, rows, columns = mixture.shape
+    low = jnp.bfloat16
+    grad_low = grad_rows.astype(low)
+    dot = partial(jnp.einsum, preferred_element_type=jnp.float32)
+    grad_wdown = dot("hrf,rd->hfd", active, grad_low)
+    grad_bdown = jnp.sum(grad_rows, 0)
+    grad_active = dot("rd,hfd->hrf", grad_low, w_down)
+    gelu_pull = jax.vjp(jax.nn.gelu, hidden)[1]
+    grad_hidden = gelu_pull(grad_active)[0].astype(low)
+    grad_bup = jnp.sum(grad_hidden.astype(jnp.float32), 1)
+    grad_wup = dot("rd,hrf->hdf", normed_two, grad_hidden)
+    grad_normed_two = dot("hrf,hdf->rd", grad_hidden, w_up)
+    grad_norm, grad_gain_two, grad_shift_two = norm_backward(
+        grad_normed_two, second_normal, second_inverse, gains[1]
+    )
+    grad_middle = grad_rows + grad_norm
+    grad_bout = jnp.sum(grad_middle, 0)
+    grad_mid_low = grad_middle.astype(low)
+    grad_wout = dot("hrc,rd->hcd", mixture, grad_mid_low)
+    grad_mixture = dot("rd,hcd->hrc", grad_mid_low, w_out).astype(low)
+    count, length = pieces[0].shape[:2]
+    gradients = attend_back(*pieces, log_total, split_heads(grad_mixture, count, length))
+    grad_flat = [grad.astype(low).reshape(shards, rows, columns) for grad in gradients]
+    grad_bqv = jnp.stack(
+        [jnp.sum(grad_flat[i].astype(jnp.float32), 1) for i in (0, 2)]
+    )
+    grad_project = jnp.concatenate(grad_flat, -1)
+    grad_wqkv = dot("rd,hrc->hdc", normed, grad_project)
+    grad_normed = dot("hrc,hdc->rd", grad_project, w_qkv)
+    grad_input, grad_gain_one, grad_shift_one = norm_backward(
+        grad_normed, first_normal, first_inverse, gains[0]
+    )
+    small = (
+        jnp.stack([grad_gain_one, grad_gain_two]),
+        jnp.stack([grad_shift_one, grad_shift_two]),
+        grad_bqv,
+        grad_bout,
+        grad_bup,
+        grad_bdown,
+    )
+    large = (grad_wqkv, grad_wout, grad_wup, grad_wdown)
+    return (grad_middle + grad_input, small, large)
+
+
+def on_device_local(
+    tokens,
+    token_mask,
+    mask_embed,
+    norm_gains,
+    norm_shifts,
+    w_qkv,
+    b_qv,
+    w_out,
+    b_out,
+    w_up,
+    b_up,
+    w_down,
+    b_down,
+    cotangent,
+):
+    low = jnp.bfloat16
+    _, frames, tubes, patches, width = tokens.shape
+    tube_size, head_size = lax.axis_size("tube"), lax.axis_size("head")
+    head = lax.axis_index("head")
+    parts = lax.axis_size("clip") * tube_size
+    frame_share = frames // (tube_size * head_size)
+    tube_share = tubes // head_size
+    rows = frame_share * tube_size * tubes * patches
+
+    def to_frames(array):
+        mine = lax.dynamic_slice_in_dim(
+            array[0], head * frame_share * tube_size, frame_share * tube_size, 0
+        )
+        return lax.all_to_all(mine, "tube", 0, 1, tiled=True)
+
+    def frames_to_tubes(array):
+        array = lax.all_to_all(array, ("tube", "head"), 1, 0, tiled=True)
+        order = array.reshape(
+            tube_size, head_size, frame_share, tube_share, patches, width
+        ).transpose(3, 1, 0, 2, 4, 5)
+        return order.reshape(rows, width)
+
+    def tubes_to_frames(array):
+        order = array.reshape(
+            tube_share, head_size, tube_size, frame_share, patches, width
+        ).transpose(2, 1, 3, 0, 4, 5)
+        order = order.reshape(frames, tube_share, patches, width)
+        return lax.all_to_all(order, ("tube", "head"), 0, 1, tiled=True).reshape(rows, width)
+
+    columns = w_qkv.shape[-1]
+    hidden_share = w_up.shape[-1]
+
+    def weights_of(b):
+        whole_bqv = lax.all_gather(b_qv[b], "head", axis=0)
+        return (
+            norm_gains[b],
+            norm_shifts[b],
+            gather_shards(w_qkv[b].reshape(width, 3 * columns), parts).reshape(
+                head_size, width, 3 * columns
+            ),
+            whole_bqv.transpose(1, 0, 2),
+            gather_shards(w_out[b], parts).reshape(head_size, columns, width),
+            b_out[b],
+            gather_shards(w_up[b], parts).reshape(head_size, width, hidden_share),
+            lax.all_gather(b_up[b], "head", axis=0),
+            gather_shards(w_down[b], parts).reshape(head_size, hidden_share, width),
+            b_down[b],
+        )
+
+    masked = to_frames(token_mask[..., None]).reshape(-1, 1) == 1
+    initial = jnp.where(
+        masked,
+        mask_embed[None, :],
+        to_frames(tokens).reshape(rows, width).astype(jnp.float32),
+    )
+    sequences = frame_share
+    weights = [weights_of(b) for b in range(2)]
+    first, stored_first = local_block_forward(initial, frame_share, weights[0])
+    second = frames_to_tubes(
+        first.astype(low).reshape(frame_share, tube_size * tubes, patches, width)
+    ).astype(jnp.float32)
+    output, stored_second = local_block_forward(second, tube_share, weights[1])
+    output = output.astype(low).reshape(tube_share, frames, patches, width).transpose(1, 0, 2, 3)
+    output = lax.all_gather(output, "head", axis=1, tiled=True)[None]
+    upstream = lax.dynamic_slice_in_dim(cotangent[0], head * tube_share, tube_share, 1)
+    upstream = upstream.transpose(1, 0, 2, 3).reshape(rows, width).astype(jnp.float32)
+    grad_second, small_second, large_second = local_block_backward(
+        weights[1], stored_second, upstream
+    )
+    grad_first = tubes_to_frames(grad_second.astype(low)).astype(jnp.float32)
+    grad_initial, small_first, large_first = local_block_backward(
+        weights[0], stored_first, grad_first
+    )
+    grad_embed = jnp.sum(jnp.where(masked, grad_initial, 0.0), 0)
+    grad_tokens = jnp.where(masked, 0.0, grad_initial).astype(low)
+    grad_tokens = grad_tokens.reshape(frame_share, tube_size * tubes, patches, width)
+    grad_tokens = lax.all_to_all(grad_tokens, "tube", 1, 0, tiled=True)
+    grad_tokens = lax.all_gather(grad_tokens, "head", axis=0, tiled=True)[None]
+    shapes = (w_qkv.shape[1:], w_out.shape[1:], w_up.shape[1:], w_down.shape[1:])
+    whole = [
+        jnp.stack(
+            [
+                shard_sum(part.reshape(-1, part.shape[-1])).reshape(shape)
+                for part in (first_part, second_part)
+            ]
+        ).astype(jnp.float32)
+        for first_part, second_part, shape in zip(large_first, large_second, shapes)
+    ]
+    small = [jnp.stack(pair) for pair in zip(small_first, small_second)]
+    small = lax.psum((grad_embed, *small), AXES)
+    embed_grad, gain_grad, shift_grad, bqv_grad, bout_grad, bup_grad, bdown_grad = small
+    bqv_grad = lax.dynamic_index_in_dim(bqv_grad, head, 2, False)
+    bup_grad = lax.dynamic_index_in_dim(bup_grad, head, 1, False)
+    return (
+        output,
+        grad_tokens,
+        embed_grad,
+        gain_grad,
+        shift_grad,
+        whole[0],
+        bqv_grad,
+        whole[1],
+        bout_grad,
+        whole[2],
+        bup_grad,
+        whole[3],
+        bdown_grad,
+    )
+
+
+def fits_local(tokens, clip_size, tube_size, head_size):
+    clips, frames, tubes = tokens.shape[:3]
+    return (
+        clips == clip_size
+        and frames % (tube_size * head_size) == 0
+        and tubes % (tube_size * head_size) == 0
+    )
+
+
 def solution(mesh):
+    sizes = [mesh.shape[name] for name in ("clip", "tube", "head")]
+
+    def run(tokens, *others):
+        on_device = on_device_local if fits_local(tokens, *sizes) else on_device_sums
+        return on_mesh(on_device, mesh)(tokens, *others)
+
+    return run
+
+
+def on_mesh(on_device, mesh):
     return jax.shard_map(
         on_device,
         mesh=mesh,

time: 1760 us -> 1810 us (1.028)
  waiting for transfers between devices: 983 us -> 1290 us
  local copies, waits for them, and re-layouts: 241 us -> 122 us
  blocking collectives: 242 us -> 155 us
  other arithmetic: 121 us -> 41.7 us
  matrix products: 141 us -> 161 us
    psum x7 -> x1, waiting for transfers between devices: 923 us -> 132 us  [on_device_local(): small = lax.psum((grad_embed, *small), AXES)]
    reduce_scatter x1 -> x8, waiting for transfers between devices: 0.79 us -> 637 us  [shard_sum(): lax.psum_scatter(partial_sum.astype(jnp.bfloat16), AXES, scatter_dimensio...]
    all_gather x5 -> x14, waiting for transfers between devices: 55.2 us -> 519 us  [the longest x8 316 us: gather_shards(): return lax.all_gather(piece, AXES, axis=0, tiled=True)]
    unnamed x1 -> x0, blocking collectives: 218 us -> none
    all_gather x1 -> x8, blocking collectives: 24.5 us -> 106 us  [the longest x4 49.4 us: shard_sum(): return lax.all_gather(share, ('tube', 'clip'), axis=0, tiled=True)]
    all_to_all x0 -> x2, blocking collectives: none -> 49.2 us  [the longest x1 33.2 us: tubes_to_frames(): lax.all_to_all(order, ('tube', 'head'), 0, 1, tiled=True)]
    reshape x12 -> x2, local copies, waits for them, and re-layouts: 48.7 us -> 0.36 us  [split_heads(): return tensor.reshape(batch_count, length, tensor.shape[-1] // HD, HD)]
    reduce_sum x12 -> x9, other arithmetic: 54.1 us -> 6.62 us  [the longest x2 2.98 us: local_block_backward(): grad_bout = jnp.sum(grad_middle, 0)]
  transfers between devices with their start and end apart: 17 -> 26, of which waited for: 12 -> 22; matrix products, arithmetic and copies ran while one was open for 12% -> 15% of each run, Pallas kernels for 0% -> 0%
where the time goes in v1:
time: 1810 us; the launch traced here: 1800 us
  waiting for transfers between devices  1290 us (71%)
  matrix products  161 us (9%)
  blocking collectives  155 us (9%)
  local copies, waits for them, and re-layouts  122 us (7%)
  other arithmetic  41.7 us (2%)
    reduce_scatter x8, waiting for transfers between devices, shard_sum(): lax.psum_scatter(partial_sum.astype(jnp.bfloat16), AXES, scatter_dimensio...  637 us
    all_gather x8, waiting for transfers between devices, gather_shards(): return lax.all_gather(piece, AXES, axis=0, tiled=True)  316 us
    psum x1, waiting for transfers between devices, on_device_local(): small = lax.psum((grad_embed, *small), AXES)  132 us
    all_gather x4, waiting for transfers between devices, shard_sum(): return lax.all_gather(share, ('tube', 'clip'), axis=0, tiled=True)  99.4 us
    all_gather x1, waiting for transfers between devices, on_device_local(): output = lax.all_gather(output, 'head', axis=1, tiled=True)[None]  52.9 us
    unnamed x181, local copies, waits for them, and re-layouts  52.7 us
    all_gather x1, waiting for transfers between devices, on_device_local(): grad_tokens = lax.all_gather(grad_tokens, 'head', axis=0, tiled=True)[None]  50.7 us
    all_gather x4, blocking collectives, shard_sum(): return lax.all_gather(share, ('tube', 'clip'), axis=0, tiled=True)  49.4 us
  transfers between devices with their start and end apart: 26, of which 22 were waited for; matrix products, arithmetic and copies ran while one was open for 15% of the time, Pallas kernels for 0%

profile of v1, /device:TPU:1, one launch (start us, length us, event | category | flops | bytes accessed | tf_op | source)
XLA Modules:
  0.0 1797.1 jit_solution(6485954288284658308)
XLA Ops:
  104.0 27.4 %all-gather.39.cloned.1.call-done = bf16[1,768,768]{2,1,0:T(8,128)(2,1)} async-done(((bf16[1,24,768]{2,1,0:T(8,128)(2,1)}), bf16[1,768,768]{2,1,0:T(8,128)(2,1)}) %all-gather.39.cloned.1.call-update) | async-done | bytes 1179664 | tf_op jit(solution)/shard_map/all_gather | solution.py:383
  134.5 62.5 %all-gather.41.cloned.1.call-done = bf16[1,3072,768]{2,1,0:T(8,128)(2,1)} async-done(((bf16[1,96,768]{2,1,0:T(8,128)(2,1)}), bf16[1,3072,768]{2,1,0:T(8,128)(2,1)}) %all-gather.41.cloned.1.call-update) | async-done | bytes 4718608 | tf_op jit(solution)/shard_map/all_gather | solution.py:383
  206.2 56.5 %all-gather.43.cloned.1.call-done = bf16[1,3072,768]{2,1,0:T(8,128)(2,1)} async-done(((bf16[1,96,768]{2,1,0:T(8,128)(2,1)}), bf16[1,3072,768]{2,1,0:T(8,128)(2,1)}) %all-gather.43.cloned.1.call-update) | async-done | bytes 4718608 | tf_op jit(solution)/shard_map/all_gather | solution.py:383
  275.6 25.6 %all_gather.73 = f32[4,2,192]{2,1,0:T(2,128)S(1)} all-gather(f32[1,2,192]{2,1,0:T(2,128)S(1)} %get-tuple-element.76), channel_id=1, replica_groups=mesh['clip'=4,'tube'=2,'head'=4] {'head'}, dimensions={0}, use_global_device_ids=true | all-gather | bytes 7680 | tf_op jit(solution)/shard_map/all_gather | solution.py:552
  318.8 13.6 all-gather.25.cloned.1.call-done
  361.2 26.7 %all-gather.45.cloned.1.call-done = bf16[1,768,768]{2,1,0:T(8,128)(2,1)} async-done(((bf16[1,24,768]{2,1,0:T(8,128)(2,1)}), bf16[1,768,768]{2,1,0:T(8,128)(2,1)}) %all-gather.45.cloned.1.call-update) | async-done | bytes 1179664 | tf_op jit(solution)/shard_map/all_gather | solution.py:383
  390.7 62.7 %all-gather.47.cloned.1.call-done = bf16[1,3072,768]{2,1,0:T(8,128)(2,1)} async-done(((bf16[1,96,768]{2,1,0:T(8,128)(2,1)}), bf16[1,3072,768]{2,1,0:T(8,128)(2,1)}) %all-gather.47.cloned.1.call-update) | async-done | bytes 4718608 | tf_op jit(solution)/shard_map/all_gather | solution.py:383
  462.7 56.0 %all-gather.49.cloned.1.call-done = bf16[1,3072,768]{2,1,0:T(8,128)(2,1)} async-done(((bf16[1,96,768]{2,1,0:T(8,128)(2,1)}), bf16[1,3072,768]{2,1,0:T(8,128)(2,1)}) %all-gather.49.cloned.1.call-update) | async-done | bytes 4718608 | tf_op jit(solution)/shard_map/all_gather | solution.py:383
  576.3 33.2 %all_to_all.63 = bf16[16,2,16,768]{3,2,1,0:T(8,128)(2,1)S(1)} all-to-all(bf16[16,2,16,768]{3,2,1,0:T(8,128)(2,1)S(1)} %bitcast.477), channel_id=1, replica_groups=mesh['clip'=4,'tube'=2,'head'=4] {'tube','head'}, dimensions={0} | all-to-all | bytes 1572864 | tf_op jit(solution)/shard_map/all_to_all | solution.py:546
  728.2 16.0 all_to_all.64
  745.8 20.3 %reduce-scatter.21.cloned.1.call-done = bf16[96,768]{1,0:T(8,128)(2,1)} async-done(((bf16[3072,768]{1,0:T(8,128)(2,1)}), bf16[96,768]{1,0:T(8,128)(2,1)}) %reduce-scatter.21.cloned.1.call-update) | async-done | bytes 147472 | tf_op jit(solution)/shard_map/reduce_scatter | solution.py:387
  766.1 112.1 %reduce-scatter.19.cloned.1.call-done = bf16[96,768]{1,0:T(8,128)(2,1)} async-done(((bf16[3072,768]{1,0:T(8,128)(2,1)}), bf16[96,768]{1,0:T(8,128)(2,1)}) %reduce-scatter.19.cloned.1.call-update) | async-done | bytes 147472 | tf_op jit(solution)/shard_map/reduce_scatter | solution.py:387
  878.3 112.8 %reduce-scatter.17.cloned.1.call-done = bf16[96,768]{1,0:T(8,128)(2,1)} async-done(((bf16[3072,768]{1,0:T(8,128)(2,1)}), bf16[96,768]{1,0:T(8,128)(2,1)}) %reduce-scatter.17.cloned.1.call-update) | async-done | bytes 147472 | tf_op jit(solution)/shard_map/reduce_scatter | solution.py:387
  991.2 131.8 %all-reduce.3.cloned.1.call-done = (f32[768]{0:T(1024)}, f32[2,2,768]{2,1,0:T(2,128)}, f32[2,2,768]{2,1,0:T(2,128)}, f32[2,2,4,192]{3,1,0,2:T(2,128)}, f32[2,768...) async-done(((f32[768]{0:T(1024)}, f32[2,2,768]{2,1,0:T(2,128)}, f32[2,2,768]{2,1,0:T(2,128)}, f32[2,2,4,192]{3,1,0,2:T(2,128)}, f32[2,768]{1,0:T(2,128)}, ...) | async-done | bytes 76816 | tf_op jit(solution)/shard_map/psum | solution.py:608
  1125.5 99.8 %reduce-scatter.15.cloned.1.call-done = bf16[24,768]{1,0:T(8,128)(2,1)} async-done(((bf16[768,768]{1,0:T(8,128)(2,1)}), bf16[24,768]{1,0:T(8,128)(2,1)}) %reduce-scatter.15.cloned.1.call-update) | async-done | bytes 36880 | tf_op jit(solution)/shard_map/reduce_scatter | solution.py:387
  1237.0 89.3 %reduce-scatter.13.cloned.1.call-done = bf16[24,768]{1,0:T(8,128)(2,1)} async-done(((bf16[768,768]{1,0:T(8,128)(2,1)}), bf16[24,768]{1,0:T(8,128)(2,1)}) %reduce-scatter.13.cloned.1.call-update) | async-done | bytes 36880 | tf_op jit(solution)/shard_map/reduce_scatter | solution.py:387
  1339.1 52.9 %all-gather.27.cloned.1.call-done = bf16[16,8,16,768]{3,2,1,0:T(8,128)(2,1)} async-done(((bf16[16,2,16,768]{3,2,1,0:T(8,128)(2,1)}), bf16[16,8,16,768]{3,2,1,0:T(8,128)(2,1)}) %all-gather.27.cloned.1.call-update) | async-done | bytes 3145744 | tf_op jit(solution)/shard_map/all_gather | solution.py:582
  1392.0 107.1 %reduce-scatter.27.cloned.1.call-done = bf16[96,576]{1,0:T(8,128)(2,1)} async-done(((bf16[3072,576]{1,0:T(8,128)(2,1)}), bf16[96,576]{1,0:T(8,128)(2,1)}) %reduce-scatter.27.cloned.1.call-update) | async-done | bytes 110608 | tf_op jit(solution)/shard_map/reduce_scatter | solution.py:387
  1512.8 95.6 %reduce-scatter.25.cloned.1.call-done = bf16[96,576]{1,0:T(8,128)(2,1)} async-done(((bf16[3072,576]{1,0:T(8,128)(2,1)}), bf16[96,576]{1,0:T(8,128)(2,1)}) %reduce-scatter.25.cloned.1.call-update) | async-done | bytes 110608 | tf_op jit(solution)/shard_map/reduce_scatter | solution.py:387
  1623.9 50.7 %all-gather.29.cloned.1.call-done = bf16[16,8,16,768]{3,2,1,0:T(8,128)(2,1)} async-done(((bf16[4,8,16,768]{3,2,1,0:T(8,128)(2,1)}), bf16[16,8,16,768]{3,2,1,0:T(8,128)(2,1)}) %all-gather.29.cloned.1.call-update) | async-done | bytes 3145744 | tf_op jit(solution)/shard_map/all_gather | solution.py:596
  1674.6 25.1 %all-gather.37.cloned.1.call-done = bf16[768,768]{1,0:T(8,128)(2,1)} async-done(((bf16[96,768]{1,0:T(8,128)(2,1)}), bf16[768,768]{1,0:T(8,128)(2,1)}) %all-gather.37.cloned.1.call-update) | async-done | bytes 1179664 | tf_op jit(solution)/shard_map/all_gather | solution.py:390
  1699.8 26.1 %all-gather.35.cloned.1.call-done = bf16[768,768]{1,0:T(8,128)(2,1)} async-done(((bf16[96,768]{1,0:T(8,128)(2,1)}), bf16[768,768]{1,0:T(8,128)(2,1)}) %all-gather.35.cloned.1.call-update) | async-done | bytes 1179664 | tf_op jit(solution)/shard_map/all_gather | solution.py:390
  1730.0 22.0 %all-gather.33.cloned.1.call-done = bf16[768,768]{1,0:T(8,128)(2,1)} async-done(((bf16[96,768]{1,0:T(8,128)(2,1)}), bf16[768,768]{1,0:T(8,128)(2,1)}) %all-gather.33.cloned.1.call-update) | async-done | bytes 1179664 | tf_op jit(solution)/shard_map/all_gather | solution.py:390
  1752.0 26.1 %all-gather.31.cloned.1.call-done = bf16[768,768]{1,0:T(8,128)(2,1)} async-done(((bf16[96,768]{1,0:T(8,128)(2,1)}), bf16[768,768]{1,0:T(8,128)(2,1)}) %all-gather.31.cloned.1.call-update) | async-done | bytes 1179664 | tf_op jit(solution)/shard_map/all_gather | solution.py:390
  (463 shorter events, 428.9 us)
Async XLA Ops:
  7.2 68.6 %all-gather.23.cloned.1.call-start = ((), (), s32[]{:S(2)}) async-start(), calls=%async_computation.13 | async-start | bytes 4055040 | tf_op jit(solution)/shard_map/all_gather | solution.py:383
  12.0 119.4 %all-gather.39.cloned.1.call-start = ((), (), s32[]{:S(2)}) async-start(), calls=%async_computation.27 | async-start | bytes 1216512 | tf_op jit(solution)/shard_map/all_gather | solution.py:383
  14.5 182.4 %all-gather.41.cloned.1.call-start = ((), (), s32[]{:S(2)}) async-start(), calls=%async_computation.28 | async-start | bytes 4866048 | tf_op jit(solution)/shard_map/all_gather | solution.py:383
  18.1 244.7 %all-gather.43.cloned.1.call-start = ((), (), s32[]{:S(2)}) async-start(), calls=%async_computation.29 | async-start | bytes 4866048 | tf_op jit(solution)/shard_map/all_gather | solution.py:383
  21.7 310.7 %all-gather.25.cloned.1.call-start = ((), (), s32[]{:S(2)}) async-start(), calls=%async_computation.14 | async-start | bytes 4055040 | tf_op jit(solution)/shard_map/all_gather | solution.py:383
  23.6 364.2 %all-gather.45.cloned.1.call-start = ((), (), s32[]{:S(2)}) async-start(), calls=%async_computation.30 | async-start | bytes 1216512 | tf_op jit(solution)/shard_map/all_gather | solution.py:383
  25.1 428.3 %all-gather.47.cloned.1.call-start = ((), (), s32[]{:S(2)}) async-start(), calls=%async_computation.31 | async-start | bytes 4866048 | tf_op jit(solution)/shard_map/all_gather | solution.py:383
  31.5 487.3 %all-gather.49.cloned.1.call-start = ((), (), s32[]{:S(2)}) async-start(), calls=%async_computation.32 | async-start | bytes 4866048 | tf_op jit(solution)/shard_map/all_gather | solution.py:383
  271.6 42.6 %all-to-all-start.2 = ((bf16[2,16,16,768]{3,2,0,1:T(8,128)(2,1)}), bf16[2,16,16,768]{3,2,0,1:T(8,128)(2,1)S(1)}, u32[]{:S(2)}, u32[]{:S(2)}) async-start(bf16[2,16,16,768]{3,2,0,1:T(8,128)(2,1)} %copy.332), calls=%async_computation.2 | async-start | bytes 1572864 | tf_op jit(solution)/shard_map/all_to_all | solution.py:535
  275.6 469.6 %reduce-scatter.23.cloned.1.call-start = ((), (), s32[]{:S(2)}) async-start(), calls=%async_computation.25 | async-start | bytes 4866048 | tf_op jit(solution)/shard_map/reduce_scatter | solution.py:387
  541.9 224.2 %reduce-scatter.21.cloned.1.call-start = ((), (), s32[]{:S(2)}) async-start(), calls=%async_computation.23 | async-start | bytes 4866048 | tf_op jit(solution)/shard_map/reduce_scatter | solution.py:387
  613.9 264.4 %reduce-scatter.19.cloned.1.call-start = ((), (), s32[]{:S(2)}) async-start(), calls=%async_computation.21 | async-start | bytes 4866048 | tf_op jit(solution)/shard_map/reduce_scatter | solution.py:387
  621.7 369.4 %reduce-scatter.17.cloned.1.call-start = ((), (), s32[]{:S(2)}) async-start(), calls=%async_computation.19 | async-start | bytes 4866048 | tf_op jit(solution)/shard_map/reduce_scatter | solution.py:387
  645.8 477.2 %all-reduce.3.cloned.1.call-start = ((), (), s32[]{:S(2)}) async-start(), calls=%async_computation.35 | async-start | bytes 163840 | tf_op jit(solution)/shard_map/psum | solution.py:608
  686.7 538.6 %reduce-scatter.15.cloned.1.call-start = ((), (), s32[]{:S(2)}) async-start(), calls=%async_computation.18 | async-start | bytes 1216512 | tf_op jit(solution)/shard_map/reduce_scatter | solution.py:387
  689.7 636.6 %reduce-scatter.13.cloned.1.call-start = ((), (), s32[]{:S(2)}) async-start(), calls=%async_computation.17 | async-start | bytes 1216512 | tf_op jit(solution)/shard_map/reduce_scatter | solution.py:387
  692.9 699.1 %all-gather.27.cloned.1.call-start = ((), (), s32[]{:S(2)}) async-start(), calls=%async_computation.15 | async-start | bytes 3932160 | tf_op jit(solution)/shard_map/all_gather | solution.py:582
  702.1 797.1 %reduce-scatter.27.cloned.1.call-start = ((), (), s32[]{:S(2)}) async-start(), calls=%async_computation.34 | async-start | bytes 4055040 | tf_op jit(solution)/shard_map/reduce_scatter | solution.py:387
  713.9 894.5 %reduce-scatter.25.cloned.1.call-start = ((), (), s32[]{:S(2)}) async-start(), calls=%async_computation.33 | async-start | bytes 4055040 | tf_op jit(solution)/shard_map/reduce_scatter | solution.py:387
  726.8 947.9 %all-gather.29.cloned.1.call-start = ((), (), s32[]{:S(2)}) async-start(), calls=%async_computation.16 | async-start | bytes 3932160 | tf_op jit(solution)/shard_map/all_gather | solution.py:596
  745.1 954.6 %all-gather.37.cloned.1.call-start = ((), (), s32[]{:S(2)}) async-start(), calls=%async_computation.26 | async-start | bytes 1327104 | tf_op jit(solution)/shard_map/all_gather | solution.py:390
  745.7 980.2 %all-gather.35.cloned.1.call-start = ((), (), s32[]{:S(2)}) async-start(), calls=%async_computation.24 | async-start | bytes 1327104 | tf_op jit(solution)/shard_map/all_gather | solution.py:390
  766.1 985.9 %all-gather.33.cloned.1.call-start = ((), (), s32[]{:S(2)}) async-start(), calls=%async_computation.22 | async-start | bytes 1327104 | tf_op jit(solution)/shard_map/all_gather | solution.py:390
  878.3 899.9 %all-gather.31.cloned.1.call-start = ((), (), s32[]{:S(2)}) async-start(), calls=%async_computation.20 | async-start | bytes 1327104 | tf_op jit(solution)/shard_map/all_gather | solution.py:390
  (79 other events, 883.0 us)
Sparse Core Ops, SparseCore 0:
  12.2 63.5 all-gather.22
  78.7 52.7 all-gather.38
  134.3 62.5 all-gather.40
  200.3 62.4 all-gather.42
  265.5 66.8 all-gather.24
  335.1 52.6 all-gather.44
  390.7 62.5 all-gather.46
  456.2 62.4 all-gather.48
  542.0 108.3 reduce-scatter.22
  656.6 109.4 reduce-scatter.20
  772.1 106.0 reduce-scatter.18
  885.0 106.0 reduce-scatter.16
  998.7 124.2 all-reduce.2
  1129.3 95.9 reduce-scatter.14
  1231.0 95.2 reduce-scatter.12
  1327.8 64.1 all-gather.26
  1398.2 100.9 reduce-scatter.26
  1505.3 103.0 reduce-scatter.24
  1610.6 63.9 all-gather.28
  1676.5 23.1 all-gather.36
  1701.8 24.0 all-gather.34
  1727.9 24.0 all-gather.32
  1754.1 24.0 all-gather.30

commit v2 on v0

--- a/solution.py
+++ b/solution.py
@@ -1,7 +1,13 @@
 import jax
 import jax.numpy as jnp
 from jax import lax
+from jax.experimental import pallas as pl
+from jax.experimental.pallas import tpu as pltpu
 from jax.sharding import PartitionSpec as P
+
+F32 = jnp.float32
+LOW = jnp.bfloat16
+MESH = pl.DeviceIdType.MESH
 
 HD = 64
 
@@ -256,7 +262,7 @@
     return (grad_middle + grad_input, gradients)
 
 
-def on_device(
+def on_device_sums(
     tokens,
     token_mask,
     mask_embed,
@@ -371,7 +377,775 @@
     )
 
 
+GELU_A = 0.7978845608028654
+GELU_B = 0.044715
+
+
+def dot(left, right, dims):
+    return lax.dot_general(left, right, (dims, ((), ())), preferred_element_type=F32)
+
+
+NN, NT, TN = ((1,), (0,)), ((1,), (1,)), ((0,), (0,))
+
+
+def standardize(values):
+    centre = values - jnp.mean(values, -1, keepdims=True)
+    inverse = lax.rsqrt(jnp.mean(centre * centre, -1, keepdims=True) + EPS)
+    return centre * inverse, inverse
+
+
+def head_masks(columns, scale):
+    lane = lax.broadcasted_iota(jnp.int32, (1, columns), 1)
+    return [
+        jnp.where((lane >= j * HD) & (lane < (j + 1) * HD), scale, 0.0).astype(LOW)
+        for j in range(columns // HD)
+    ]
+
+
+def gelu_pair(hidden):
+    square = hidden * hidden
+    tanh = jnp.tanh(GELU_A * hidden * (1.0 + GELU_B * square))
+    half = 0.5 * (1.0 + tanh)
+    slope = half + hidden * (0.5 * GELU_A) * (1.0 - tanh * tanh) * (1.0 + 3.0 * GELU_B * square)
+    return hidden * half, slope
+
+
+class Sizes:
+    def __init__(self, rows, width, shards, columns, units, length):
+        self.rows, self.width, self.shards = rows, width, shards
+        self.columns, self.units, self.length = columns, units, length
+        self.sequences = rows // length
+        self.heads = columns // HD
+        self.out_row = 3 * columns
+        self.up_row = 4 * columns
+        self.down_row = 4 * columns + width
+        self.block_rows = 4 * columns + width + units
+
+
+def norm_rows(sz, x_ref, gain, shift, n_ref, chunk=128):
+    @pl.loop(0, sz.rows, step=chunk)
+    def _(start):
+        at = pl.ds(pl.multiple_of(start, chunk), chunk)
+        normal, _ = standardize(x_ref[at, :].astype(F32))
+        n_ref[at, :] = (normal * gain + shift).astype(LOW)
+
+
+def forward_attention(sz, shard, w_ref, bqv, n_ref, q_ref, k_ref, v_ref, p_ref, o_ref, m_ref):
+    cols, length = sz.columns, sz.length
+    normed = n_ref[...]
+    q_ref[shard] = (dot(normed, w_ref[shard, 0:cols, :], NT) + bqv[0:1, :]).astype(LOW)
+    k_ref[shard] = dot(normed, w_ref[shard, cols : 2 * cols, :], NT).astype(LOW)
+    v_ref[shard] = (dot(normed, w_ref[shard, 2 * cols : 3 * cols, :], NT) + bqv[1:2, :]).astype(LOW)
+    scaled = head_masks(cols, HD**-0.5)
+    masks = head_masks(cols, 1.0)
+    for seq in range(sz.sequences):
+        at = slice(seq * length, (seq + 1) * length)
+        queries, keys, values = q_ref[shard, at, :], k_ref[shard, at, :], v_ref[shard, at, :]
+        mixture = jnp.zeros((length, cols), F32)
+        for head in range(sz.heads):
+            scores = dot(queries * scaled[head], keys, NT)
+            exponent = jnp.exp(scores - jnp.max(scores, -1, keepdims=True))
+            weights = (exponent / jnp.sum(exponent, -1, keepdims=True)).astype(LOW)
+            p_ref[shard, seq * sz.heads + head] = weights
+            mixture += dot(weights, values * masks[head], NN)
+        o_ref[shard, at, :] = mixture.astype(LOW)
+    m_ref[...] += dot(o_ref[shard], w_ref[shard, sz.out_row : sz.out_row + cols, :], NN)
+
+
+def forward_mlp(sz, shard, w_ref, b_up, n2_ref, a_ref, s_ref, y_ref):
+    hidden = (
+        dot(n2_ref[...], w_ref[shard, sz.up_row : sz.up_row + sz.width, :], NN) + b_up
+    )
+    active, slope = gelu_pair(hidden)
+    a_ref[shard] = active.astype(LOW)
+    s_ref[shard] = slope.astype(LOW)
+    y_ref[...] += dot(a_ref[shard], w_ref[shard, sz.down_row : sz.down_row + sz.units, :], NN)
+
+
+def forward_block(sz, x_ref, gains_ref, shifts_ref, w_ref, bqv_ref, bout_ref, bup_ref, bdown_ref,
+                  n_ref, q_ref, k_ref, v_ref, p_ref, o_ref, m_ref, n2_ref, a_ref, s_ref, y_ref):
+    norm_rows(sz, x_ref, gains_ref[0:1, :], shifts_ref[0:1, :], n_ref)
+    m_ref[...] = x_ref[...].astype(F32) + bout_ref[...]
+
+    @pl.loop(0, sz.shards)
+    def _(shard):
+        forward_attention(sz, shard, w_ref, bqv_ref[shard], n_ref, q_ref, k_ref, v_ref, p_ref, o_ref, m_ref)
+
+    norm_rows(sz, m_ref, gains_ref[1:2, :], shifts_ref[1:2, :], n2_ref)
+    y_ref[...] = m_ref[...] + bdown_ref[...]
+
+    @pl.loop(0, sz.shards)
+    def _(shard):
+        forward_mlp(sz, shard, w_ref, bup_ref[shard], n2_ref, a_ref, s_ref, y_ref)
+
+
+def backward_mlp(sz, shard, w_ref, gl_ref, n2_ref, a_ref, s_ref, du_ref, dn_ref, g_ref, gbup_ref):
+    low = gl_ref[...]
+    grad_active = dot(low, w_ref[shard, sz.down_row : sz.down_row + sz.units, :], NT)
+    du_ref[...] = (grad_active * s_ref[shard].astype(F32)).astype(LOW)
+    gbup_ref[shard] = jnp.sum(du_ref[...].astype(F32), 0, keepdims=True)
+    g_ref[shard, sz.down_row : sz.down_row + sz.units, :] = dot(a_ref[shard], low, TN).astype(LOW)
+    g_ref[shard, sz.up_row : sz.up_row + sz.width, :] = dot(n2_ref[...], du_ref[...], TN).astype(LOW)
+    dn_ref[...] += dot(du_ref[...], w_ref[shard, sz.up_row : sz.up_row + sz.width, :], NT)
+
+
+def norm_back_rows(sz, x_ref, gain, dn_ref, g_ref, out_ref, gain_ref, shift_ref, at_row, sum_ref, low_ref, chunk=128):
+    gain_ref[at_row : at_row + 1, :] = jnp.zeros((1, sz.width), F32)
+    shift_ref[at_row : at_row + 1, :] = jnp.zeros((1, sz.width), F32)
+    if sum_ref is not None:
+        sum_ref[...] = jnp.zeros_like(sum_ref)
+
+    @pl.loop(0, sz.rows, step=chunk)
+    def _(start):
+        at = pl.ds(pl.multiple_of(start, chunk), chunk)
+        normal, inverse = standardize(x_ref[at, :].astype(F32))
+        dn = dn_ref[at, :]
+        dy = dn * gain
+        part = inverse * (
+            dy - jnp.mean(dy, -1, keepdims=True) - normal * jnp.mean(dy * normal, -1, keepdims=True)
+        )
+        total = g_ref[at, :].astype(F32) + part
+        out_ref[at, :] = total.astype(out_ref.dtype)
+        if low_ref is not None:
+            low_ref[at, :] = total.astype(LOW)
+        gain_ref[at_row : at_row + 1, :] += jnp.sum(dn * normal, 0, keepdims=True)
+        shift_ref[at_row : at_row + 1, :] += jnp.sum(dn, 0, keepdims=True)
+        if sum_ref is not None:
+            sum_ref[...] += jnp.sum(total, 0, keepdims=True)
+
+
+def backward_attention(sz, shard, w_ref, dml_ref, n_ref, q_ref, k_ref, v_ref, p_ref, o_ref,
+                       do_ref, dq_ref, dk_ref, dv_ref, dn_ref, g_ref, gbqv_ref):
+    cols, length = sz.columns, sz.length
+    low = dml_ref[...]
+    w_out = w_ref[shard, sz.out_row : sz.out_row + cols, :]
+    do_ref[...] = dot(low, w_out, NT).astype(LOW)
+    g_ref[shard, sz.out_row : sz.out_row + cols, :] = dot(o_ref[shard], low, TN).astype(LOW)
+    scaled = head_masks(cols, HD**-0.5)
+    masks = head_masks(cols, 1.0)
+    for seq in range(sz.sequences):
+        at = slice(seq * length, (seq + 1) * length)
+        queries, keys, values = q_ref[shard, at, :], k_ref[shard, at, :], v_ref[shard, at, :]
+        grad_o = do_ref[at, :]
+        dq = jnp.zeros((length, cols), F32)
+        dk = jnp.zeros((length, cols), F32)
+        dv = jnp.zeros((length, cols), F32)
+        for head in range(sz.heads):
+            weights = p_ref[shard, seq * sz.heads + head]
+            grad_head = grad_o * masks[head]
+            dp = dot(grad_head, values, NT)
+            dv += dot(weights, grad_head, TN)
+            wide = weights.astype(F32)
+            ds = (wide * (dp - jnp.sum(wide * dp, -1, keepdims=True))).astype(LOW)
+            dq += dot(ds, keys * scaled[head], NN)
+            dk += dot(ds, queries * scaled[head], TN)
+        dq_ref[at, :] = dq.astype(LOW)
+        dk_ref[at, :] = dk.astype(LOW)
+        dv_ref[at, :] = dv.astype(LOW)
+    normed = n_ref[...]
+    gbqv_ref[shard, 0:1, :] = jnp.sum(dq_ref[...].astype(F32), 0, keepdims=True)
+    gbqv_ref[shard, 1:2, :] = jnp.sum(dv_ref[...].astype(F32), 0, keepdims=True)
+    for i, part in enumerate((dq_ref, dk_ref, dv_ref)):
+        g_ref[shard, i * cols : (i + 1) * cols, :] = dot(part[...], normed, TN).astype(LOW)
+        dn_ref[...] += dot(part[...], w_ref[shard, i * cols : (i + 1) * cols, :], NN)
+
+
+def backward_block(sz, up_ref, x_ref, gains_ref, w_ref, n_ref, q_ref, k_ref, v_ref, p_ref, o_ref, m_ref, n2_ref, a_ref, s_ref,
+                   gl_ref, du_ref, dn_ref, dm_ref, do_ref, dq_ref, dk_ref, dv_ref,
+                   dx_ref, g_ref, ggain_ref, gshift_ref, gbqv_ref, gbout_ref, gbup_ref, gbdown_ref):
+    gl_ref[...] = up_ref[...].astype(LOW)
+    gbdown_ref[...] = jnp.sum(up_ref[...].astype(F32), 0, keepdims=True)
+    dn_ref[...] = jnp.zeros_like(dn_ref)
+
+    @pl.loop(0, sz.shards)
+    def _(shard):
+        backward_mlp(sz, shard, w_ref, gl_ref, n2_ref, a_ref, s_ref, du_ref, dn_ref, g_ref, gbup_ref)
+
+    norm_back_rows(sz, m_ref, gains_ref[1:2, :], dn_ref, up_ref, dm_ref, ggain_ref, gshift_ref, 1, gbout_ref, gl_ref)
+    dn_ref[...] = jnp.zeros_like(dn_ref)
+
+    @pl.loop(0, sz.shards)
+    def _(shard):
+        backward_attention(sz, shard, w_ref, gl_ref, n_ref, q_ref, k_ref, v_ref, p_ref, o_ref,
+                           do_ref, dq_ref, dk_ref, dv_ref, dn_ref, g_ref, gbqv_ref)
+
+    norm_back_rows(sz, x_ref, gains_ref[0:1, :], dn_ref, dm_ref, dx_ref, ggain_ref, gshift_ref, 0, None, None)
+
+
+def saved_shapes(sz):
+    s, r, c = sz.shards, sz.rows, sz.columns
+    return [
+        ((r, sz.width), LOW),
+        ((s, r, c), LOW),
+        ((s, r, c), LOW),
+        ((s, r, c), LOW),
+        ((s, sz.sequences * sz.heads, sz.length, sz.length), LOW),
+        ((s, r, c), LOW),
+        ((r, sz.width), F32),
+        ((r, sz.width), LOW),
+        ((s, r, sz.units), LOW),
+        ((s, r, sz.units), LOW),
+    ]
+
+
+def work_shapes(sz):
+    r, c = sz.rows, sz.columns
+    return [
+        ((r, sz.width), LOW),
+        ((r, sz.units), LOW),
+        ((r, sz.width), F32),
+        ((r, sz.width), F32),
+        ((r, c), LOW),
+        ((r, c), LOW),
+        ((r, c), LOW),
+        ((r, c), LOW),
+    ]
+
+
+def grad_shapes(sz):
+    return [
+        ((sz.shards, sz.block_rows, sz.width), LOW),
+        ((2, sz.width), F32),
+        ((2, sz.width), F32),
+        ((sz.shards, 2, sz.columns), F32),
+        ((1, sz.width), F32),
+        ((sz.shards, 1, sz.units), F32),
+        ((1, sz.width), F32),
+    ]
+
+
+def structs(shapes):
+    return [jax.ShapeDtypeStruct(s, d) for s, d in shapes]
+
+
+def vmems(shapes):
+    return [pltpu.VMEM(s, d) for s, d in shapes]
+
+
+PARAMS = pltpu.CompilerParams(vmem_limit_bytes=62 * 2**20)
+
+
+def run_forward(sz, x, weights):
+    def kernel(*refs):
+        forward_block(sz, *refs[:-1], refs[-1])
+    out = pl.pallas_call(
+        kernel, name="forward_first",
+        out_shape=structs(saved_shapes(sz) + [((sz.rows, sz.width), F32)]),
+        compiler_params=PARAMS,
+    )(x, *weights)
+    return out[-1], out[:-1]
+
+
+def run_backward(sz, up, x, weights, saved):
+    nw = len(work_shapes(sz))
+    ng = len(grad_shapes(sz))
+    def kernel(*refs):
+        ins = refs[: 4 + 10]
+        dx, grads = refs[14], refs[15 : 15 + ng]
+        work = refs[15 + ng :]
+        backward_block(sz, *ins, *work, dx, *grads)
+    return pl.pallas_call(
+        kernel, name="backward_first",
+        out_shape=structs([((sz.rows, sz.width), F32)] + grad_shapes(sz)),
+        scratch_shapes=vmems(work_shapes(sz)),
+        compiler_params=PARAMS,
+    )(up, x, weights[0], weights[2], *saved)
+
+
+def run_both(sz, x, up, weights):
+    ns, nw, ng = len(saved_shapes(sz)), len(work_shapes(sz)), len(grad_shapes(sz))
+    def kernel(*refs):
+        x_ref, up_ref = refs[:2]
+        w = refs[2:9]
+        y_ref, dx_ref = refs[9:11]
+        grads = refs[11 : 11 + ng]
+        acc, *rest = refs[11 + ng :]
+        saved, work = rest[:ns], rest[ns:]
+        forward_block(sz, x_ref, *w, *saved, acc)
+        y_ref[...] = acc[...].astype(LOW)
+        backward_block(sz, up_ref, x_ref, w[0], w[2], *saved, *work, dx_ref, *grads)
+    return pl.pallas_call(
+        kernel, name="both_second",
+        out_shape=structs([((sz.rows, sz.width), LOW), ((sz.rows, sz.width), LOW)] + grad_shapes(sz)),
+        scratch_shapes=vmems([((sz.rows, sz.width), F32)] + saved_shapes(sz) + work_shapes(sz)),
+        compiler_params=PARAMS,
+    )(x, up, *weights)
+
+
+class Place:
+    def __init__(self, heads, zs=None):
+        self.clip, self.y, self.z = (lax.axis_index(n) for n in ("clip", "tube", "head"))
+        self.heads = heads
+        self.core, self.x = lax.rem(self.clip, 2), lax.div(self.clip, 2)
+        c, x, y = self.core, self.x, self.y
+        self.first = (c + 2 * (x + (1 - c) * (1 - 2 * x)), y + c * (1 - 2 * y), self.z)
+        self.second = (c + 2 * (x + c * (1 - 2 * x)), y + (1 - c) * (1 - 2 * y), self.z)
+        self.other = (1 - c + 2 * x, y, self.z)
+        self.i = (1 - c) * x + c * y
+        self.j = (1 - c) * y + c * x
+
+    def head(self, step):
+        return (self.clip, self.y, lax.rem(self.z + step + self.heads, self.heads))
+
+    def peers(self):
+        return [self.first, self.second, self.other] + [self.head(d) for d in range(1, self.heads)]
+
+
+def greet(peers):
+    barrier = pltpu.get_barrier_semaphore()
+    for peer in peers:
+        pl.semaphore_signal(barrier, inc=1, device_id=peer, device_id_type=MESH)
+    pl.semaphore_wait(barrier, len(peers))
+
+
+class Moves:
+    def __init__(self, send_sem, recv_sem):
+        self.send_sem, self.recv_sem, self.count, self.sent = send_sem, recv_sem, 0, []
+
+    def phase(self, copies):
+        made = []
+        for src, dst, landing, target in copies:
+            n = self.count
+            self.count += 1
+            made.append((src, dst, landing, target, n))
+        return made
+
+    def start(self, made):
+        for src, dst, _, target, n in made:
+            copy = pltpu.make_async_remote_copy(
+                src, dst, self.send_sem.at[n], self.recv_sem.at[n], device_id=target, device_id_type=MESH
+            )
+            copy.start()
+            self.sent.append(copy)
+
+    def arrive(self, made):
+        for src, _, landing, target, n in made:
+            pltpu.make_async_remote_copy(
+                src, landing, self.send_sem.at[n], self.recv_sem.at[n], device_id=target, device_id_type=MESH
+            ).wait_recv()
+
+    def finish(self):
+        for copy in self.sent:
+            copy.wait_send()
+        self.sent = []
+
+
+PIECES = 3
+
+
+def gather_phases(place, moves, shard, full, base, offset, rows):
+    q = rows // 8
+    c, i, j, z, heads = place.core, place.i, place.j, place.z, place.heads
+
+    def at(ref, head, start, size):
+        return ref.at[head, pl.ds(pl.multiple_of(offset + start * q, q), size * q), :]
+
+    def other(d):
+        return lax.rem(z + d, heads)
+
+    mine = 4 * c + 2 * j + i
+    near = 4 * c + 2 * j + (1 - i)
+    pair = 4 * c + 2 * j
+    pair_far = 4 * c + 2 * (1 - j)
+    src = shard.at[pl.ds(pl.multiple_of(base + offset + mine * q, q), q), :]
+    steps = range(1, heads)
+    return [
+        moves.phase(
+            [(src, at(full, z, mine, 1), at(full, lax.rem(z + heads - d, heads), mine, 1), place.head(d)) for d in steps]
+        ),
+        moves.phase(
+            [(at(full, other(d), mine, 1), at(full, other(d), mine, 1), at(full, other(d), near, 1), place.first) for d in steps]
+        ),
+        moves.phase(
+            [(at(full, other(d), pair, 2), at(full, other(d), pair, 2), at(full, other(d), pair_far, 2), place.second) for d in steps]
+        ),
+        moves.phase(
+            [(at(full, other(d), 4 * c, 4), at(full, other(d), 4 * c, 4), at(full, other(d), 4 * (1 - c), 4), place.other) for d in steps]
+        ),
+    ]
+
+
+def gather_kernel(heads, block_rows, blocks, shard, biases, tokens, marks, *refs):
+    fulls, whole_bias, frames, frame_marks = refs[:blocks], *refs[blocks : blocks + 3]
+    held, send_sem, recv_sem, local_sem, held_sem = refs[blocks + 3 :]
+    place = Place(heads)
+    moves = Moves(send_sem, recv_sem)
+    rows = block_rows // PIECES
+    y, z = place.y, place.z
+    count, tubes = frames.shape[0], tokens.shape[1]
+    greet(place.peers())
+    owned = pl.ds((2 * z + y) * count, count)
+    asked = pl.ds((2 * z + 1 - y) * count, count)
+    here, there = pl.ds(y * tubes, tubes), pl.ds((1 - y) * tubes, tubes)
+    across = (place.clip, 1 - y, z)
+    exchange = moves.phase(
+        [
+            (src.at[asked], dst.at[:, here], dst.at[:, there], across)
+            for src, dst in ((tokens, frames), (marks, frame_marks))
+        ]
+        + [
+            (biases, whole_bias.at[z], whole_bias.at[lax.rem(z + heads - d, heads)], place.head(d))
+            for d in range(1, heads)
+        ]
+    )
+    moves.start(exchange)
+    local = [
+        pltpu.make_async_copy(tokens.at[owned], frames.at[:, here], local_sem.at[0]),
+        pltpu.make_async_copy(marks.at[owned], frame_marks.at[:, here], local_sem.at[1]),
+        pltpu.make_async_copy(biases, whole_bias.at[z], local_sem.at[2]),
+    ]
+    hold = [
+        (
+            pltpu.make_async_copy(shard.at[pl.ds(b * block_rows, block_rows), :], held.at[b], held_sem.at[b]),
+            pltpu.make_async_copy(held.at[b], fulls[b].at[z], local_sem.at[3 + b]),
+        )
+        for b in range(blocks)
+    ]
+    for copy in local:
+        copy.start()
+    for fetch, _ in hold:
+        fetch.start()
+    work = [
+        gather_phases(place, moves, shard, fulls[b], b * block_rows, i * rows, rows)
+        for b in range(blocks)
+        for i in range(PIECES)
+    ]
+    moves.start(work[0][0])
+    for fetch, store in hold:
+        fetch.wait()
+        store.start()
+    for n, phases in enumerate(work):
+        moves.arrive(phases[0])
+        if n + 1 < len(work):
+            moves.start(work[n + 1][0])
+        moves.start(phases[1])
+        if n:
+            moves.arrive(work[n - 1][2])
+            moves.start(work[n - 1][3])
+        moves.arrive(phases[1])
+        moves.start(phases[2])
+    moves.arrive(work[-1][2])
+    moves.start(work[-1][3])
+    for phases in work:
+        moves.arrive(phases[3])
+    moves.arrive(exchange)
+    moves.finish()
+    for copy in local:
+        copy.wait()
+    for _, store in hold:
+        store.wait()
+
+
+def gather_weights(heads, shard, blocks, biases, tokens, marks, frame_share):
+    total, width = shard.shape
+    block_rows = total // blocks
+    count = blocks * PIECES * 4 * (heads - 1) + 2 + heads - 1
+    hbm = pl.BlockSpec(memory_space=pl.ANY)
+    whole = lambda array: jax.ShapeDtypeStruct(
+        (frame_share, 2 * array.shape[1]) + array.shape[2:], array.dtype
+    )
+    out = pl.pallas_call(
+        lambda *refs: gather_kernel(heads, block_rows, blocks, *refs),
+        name="gather_weights",
+        out_shape=[jax.ShapeDtypeStruct((heads, block_rows, width), LOW)] * blocks
+        + [jax.ShapeDtypeStruct((heads,) + biases.shape, F32), whole(tokens), whole(marks)],
+        in_specs=[hbm] * 4,
+        out_specs=[hbm] * (blocks + 3),
+        scratch_shapes=[
+            pltpu.VMEM((blocks, block_rows, width), LOW),
+            pltpu.SemaphoreType.DMA((count,)),
+            pltpu.SemaphoreType.DMA((count,)),
+            pltpu.SemaphoreType.DMA((3 + blocks,)),
+            pltpu.SemaphoreType.DMA((blocks,)),
+        ],
+        compiler_params=pltpu.CompilerParams(
+            collective_id=0, has_side_effects=True, vmem_limit_bytes=60 * 2**20
+        ),
+    )(shard, biases, tokens, marks)
+    return out[:blocks], *out[blocks:]
+
+
+class Reduction:
+    def __init__(self, place, moves, grads, out, offset, out_row, rows, own, core_buf, first_buf, second_buf, head_buf, local_sem):
+        q = rows // 8
+        self.q, self.place, self.moves = q, place, moves
+        self.grads, self.out, self.out_row = grads, out, out_row
+        self.own, self.core_buf, self.first_buf, self.second_buf, self.head_buf = own, core_buf, first_buf, second_buf, head_buf
+        c, i, j, z, heads = place.core, place.i, place.j, place.z, place.heads
+        cut = lambda ref, start, size: ref.at[:, pl.ds(pl.multiple_of(start * q, q), size * q), :]
+        half = lambda core: grads.at[:, pl.ds(pl.multiple_of(offset + core * 4 * q, q), 4 * q), :]
+        row = lambda start, size: out.at[pl.ds(pl.multiple_of(out_row + start * q, q), size * q), :]
+        self.load = pltpu.make_async_copy(half(c), own, local_sem)
+        self.core = moves.phase([(half(1 - c), core_buf, core_buf, place.other)])
+        self.first = moves.phase([(cut(own, 2 * (1 - i), 2), first_buf, first_buf, place.first)])
+        self.second = moves.phase([(cut(own, 2 * i + 1 - j, 1), second_buf, second_buf, place.second)])
+        mine = 2 * i + j
+        at = pl.ds(pl.multiple_of(mine * q, q), q)
+        self.mine = at
+        self.heads = moves.phase(
+            [(own.at[lax.rem(z + d, heads), at, :], head_buf.at[d - 1], head_buf.at[d - 1], place.head(d)) for d in range(1, heads)]
+        )
+        a = 4 * c
+        self.share_second = moves.phase([(row(a + mine, 1), row(a + mine, 1), row(a + 2 * i + 1 - j, 1), place.second)])
+        self.share_first = moves.phase([(row(a + 2 * i, 2), row(a + 2 * i, 2), row(a + 2 * (1 - i), 2), place.first)])
+        self.share_core = moves.phase([(row(a, 4), row(a, 4), row(4 - a, 4), place.other)])
+        self.final_row = row(a + mine, 1)
+
+    def begin(self):
+        self.load.start()
+        self.moves.start(self.core)
+
+    def add(self, buf, start, size):
+        q = self.q
+        shards = self.own.shape[0]
+        at = pl.ds(pl.multiple_of(start * q, q), size * q)
+
+        @pl.loop(0, shards)
+        def _(s):
+            self.own[s, at, :] = self.own[s, at, :] + buf[s]
+
+    def step_first(self):
+        self.load.wait()
+        self.moves.arrive(self.core)
+        self.add(self.core_buf, 0, 4)
+        self.moves.start(self.first)
+
+    def step_second(self):
+        self.moves.arrive(self.first)
+        self.add(self.first_buf, 2 * self.place.i, 2)
+        self.moves.start(self.second)
+
+    def step_heads(self):
+        self.moves.arrive(self.second)
+        self.add(self.second_buf, 2 * self.place.i + self.place.j, 1)
+        self.moves.start(self.heads)
+
+    def step_share(self, final_buf, sem):
+        self.moves.arrive(self.heads)
+        total = self.own[self.place.z, self.mine, :].astype(F32)
+        for d in range(self.place.heads - 1):
+            total += self.head_buf[d].astype(F32)
+        final_buf[...] = total.astype(LOW)
+        copy = pltpu.make_async_copy(final_buf, self.final_row, sem)
+        copy.start()
+        copy.wait()
+        self.moves.start(self.share_second)
+
+    def step_share_first(self):
+        self.moves.arrive(self.share_second)
+        self.moves.start(self.share_first)
+
+    def step_share_core(self):
+        self.moves.arrive(self.share_first)
+        self.moves.start(self.share_core)
+
+    def end(self):
+        self.moves.arrive(self.share_core)
+
+
+def reduce_kernel(heads, block_rows, blocks, *refs):
+    grads, out = refs[:blocks], refs[blocks]
+    own, core_buf, first_buf, second_buf, head_buf, final_buf, send_sem, recv_sem, local_sem, final_sem = refs[blocks + 1 :]
+    place = Place(heads)
+    moves = Moves(send_sem, recv_sem)
+    rows = block_rows // PIECES
+    greet(place.peers())
+    work = []
+    for n in range(blocks * PIECES):
+        b, i = blocks - 1 - n // PIECES, PIECES - 1 - n % PIECES
+        work.append(
+            Reduction(
+                place, moves, grads[b], out, i * rows, b * block_rows + i * rows, rows,
+                own.at[n], core_buf.at[n], first_buf.at[n], second_buf.at[n], head_buf.at[n], local_sem.at[n],
+            )
+        )
+    count = len(work)
+    work[0].begin()
+    for tick in range(count + 6):
+        if tick + 1 < count:
+            work[tick + 1].begin()
+        if tick < count:
+            work[tick].step_first()
+        if 0 <= tick - 1 < count:
+            work[tick - 1].step_second()
+        if 0 <= tick - 2 < count:
+            work[tick - 2].step_heads()
+        if 0 <= tick - 3 < count:
+            work[tick - 3].step_share(final_buf.at[tick - 3], final_sem.at[tick - 3])
+        if 0 <= tick - 4 < count:
+            work[tick - 4].step_share_first()
+        if 0 <= tick - 5 < count:
+            work[tick - 5].step_share_core()
+        if 0 <= tick - 6 < count:
+            work[tick - 6].end()
+    moves.finish()
+
+
+def reduce_grads(heads, grads):
+    blocks = len(grads)
+    _, block_rows, width = grads[0].shape
+    rows = block_rows // PIECES
+    n = blocks * PIECES
+    q = rows // 8
+    count = n * (6 + heads - 1)
+    hbm = pl.BlockSpec(memory_space=pl.ANY)
+    return pl.pallas_call(
+        lambda *refs: reduce_kernel(heads, block_rows, blocks, *refs),
+        name="reduce_grads",
+        out_shape=jax.ShapeDtypeStruct((blocks * block_rows, width), LOW),
+        in_specs=[hbm] * blocks,
+        out_specs=hbm,
+        scratch_shapes=[
+            pltpu.VMEM((n, heads, 4 * q, width), LOW),
+            pltpu.VMEM((n, heads, 4 * q, width), LOW),
+            pltpu.VMEM((n, heads, 2 * q, width), LOW),
+            pltpu.VMEM((n, heads, q, width), LOW),
+            pltpu.VMEM((n, heads - 1, q, width), LOW),
+            pltpu.VMEM((n, q, width), LOW),
+            pltpu.SemaphoreType.DMA((count,)),
+            pltpu.SemaphoreType.DMA((count,)),
+            pltpu.SemaphoreType.DMA((n,)),
+            pltpu.SemaphoreType.DMA((n,)),
+        ],
+        compiler_params=pltpu.CompilerParams(collective_id=1, has_side_effects=True, vmem_limit_bytes=60 * 2**20),
+    )(*grads)
+
+
+AXES = ("head", "tube", "clip")
+
+
+def fits_local(arrays, clip_size, tube_size, head_size):
+    clips, frames, tubes = arrays[0].shape[:3]
+    width = arrays[0].shape[-1]
+    columns, units = arrays[5].shape[3] // head_size, arrays[9].shape[2] // head_size
+    devices = tube_size * head_size
+    return (
+        (clips, clip_size, tube_size) == (4, 4, 2)
+        and frames % devices == 0
+        and tubes % devices == 0
+        and width == 4 * columns == units
+        and width % 384 == 0
+        and columns % HD == 0
+    )
+
+
+def on_device_local(
+    tokens,
+    token_mask,
+    mask_embed,
+    norm_gains,
+    norm_shifts,
+    w_qkv,
+    b_qv,
+    w_out,
+    b_out,
+    w_up,
+    b_up,
+    w_down,
+    b_down,
+    cotangent,
+):
+    _, frames, tubes, patches, width = tokens.shape
+    tube_size, heads = lax.axis_size("tube"), lax.axis_size("head")
+    head = lax.axis_index("head")
+    blocks, columns, units = w_qkv.shape[0], w_qkv.shape[-1], w_up.shape[-1]
+    frame_share = frames // (tube_size * heads)
+    tube_share = tubes // heads
+    rows = frame_share * tube_size * tubes * patches
+    sz = Sizes(rows, width, heads, columns, units, rows // frame_share)
+    pair = Sizes(rows, width, heads, columns, units, rows // tube_share)
+
+    shard = jnp.concatenate(
+        [w_qkv.transpose(0, 2, 3, 1).reshape(blocks, 3 * columns, width), w_out, w_up, w_down], 1
+    ).reshape(blocks * sz.block_rows, width)
+    marks = jnp.broadcast_to(token_mask[0][..., None], (frames, tubes, patches, 128)).astype(LOW)
+    biases = jnp.concatenate([b_qv.reshape(-1), b_up.reshape(-1)]).reshape(-1, 128)
+    full, whole_bias, x_frames, mark_frames = gather_weights(
+        heads, shard, blocks, biases, tokens[0], marks, frame_share
+    )
+    whole_bias = whole_bias.reshape(heads, -1)
+    cut = blocks * 2 * columns
+    whole_bqv = whole_bias[:, :cut].reshape(heads, blocks, 2, columns)
+    whole_bup = whole_bias[:, cut:].reshape(heads, blocks, 1, units)
+
+    def weights_of(b):
+        return (
+            norm_gains[b],
+            norm_shifts[b],
+            full[b],
+            whole_bqv[:, b],
+            b_out[b][None],
+            whole_bup[:, b],
+            b_down[b][None],
+        )
+
+    def frames_to_tubes(array):
+        array = array.reshape(frame_share, tube_size * tubes, patches, width)
+        array = lax.all_to_all(array, ("tube", "head"), 1, 0, tiled=True)
+        order = array.reshape(tube_size, heads, frame_share, tube_share, patches, width)
+        return order.transpose(3, 1, 0, 2, 4, 5).reshape(rows, width)
+
+    def tubes_to_frames(array):
+        order = array.reshape(tube_share, heads, tube_size, frame_share, patches, width)
+        order = order.transpose(2, 1, 3, 0, 4, 5).reshape(frames, tube_share, patches, width)
+        return lax.all_to_all(order, ("tube", "head"), 0, 1, tiled=True).reshape(rows, width)
+
+    masked = mark_frames[..., :1].reshape(rows, 1) > 0.5
+    initial = jnp.where(masked, mask_embed[None, :], x_frames.reshape(rows, width).astype(F32))
+    first, saved = run_forward(sz, initial, weights_of(0))
+    second = frames_to_tubes(first.astype(LOW))
+    upstream = lax.dynamic_slice_in_dim(cotangent[0], head * tube_share, tube_share, 1)
+    upstream = upstream.transpose(1, 0, 2, 3).reshape(rows, width)
+    output, grad_second, grads_second, *small_second = run_both(
+        pair, second, upstream, weights_of(1)
+    )
+    output = output.reshape(tube_share, frames, patches, width).transpose(1, 0, 2, 3)
+    output = lax.all_gather(output, "head", axis=1, tiled=True)[None]
+    grad_first = tubes_to_frames(grad_second)
+    grad_initial, grads_first, *small_first = run_backward(
+        sz, grad_first, initial, weights_of(0), saved
+    )
+    grad_embed = jnp.sum(jnp.where(masked, grad_initial, 0.0), 0)
+    grad_tokens = jnp.where(masked, 0.0, grad_initial).astype(LOW)
+    grad_tokens = grad_tokens.reshape(frame_share, tube_size * tubes, patches, width)
+    grad_tokens = lax.all_to_all(grad_tokens, "tube", 1, 0, tiled=True)
+    grad_tokens = lax.all_gather(grad_tokens, "head", axis=0, tiled=True)[None]
+    small = [jnp.stack(two) for two in zip(small_first, small_second)]
+    small = lax.psum((grad_embed, *small), AXES)
+    embed_grad, gain_grad, shift_grad, bqv_grad, bout_grad, bup_grad, bdown_grad = small
+    bqv_grad = lax.dynamic_index_in_dim(bqv_grad, head, 1, False)
+    bup_grad = lax.dynamic_index_in_dim(bup_grad, head, 1, False).reshape(blocks, units)
+    whole = reduce_grads(heads, [grads_first, grads_second]).astype(F32)
+    whole = whole.reshape(blocks, sz.block_rows, width)
+    qkv_grad = whole[:, : sz.out_row].reshape(blocks, 3, columns, width).transpose(0, 3, 1, 2)
+    return (
+        output,
+        grad_tokens,
+        embed_grad,
+        gain_grad,
+        shift_grad,
+        qkv_grad,
+        bqv_grad,
+        whole[:, sz.out_row : sz.up_row],
+        bout_grad[:, 0],
+        whole[:, sz.up_row : sz.down_row],
+        bup_grad,
+        whole[:, sz.down_row :],
+        bdown_grad[:, 0],
+    )
+
+
 def solution(mesh):
+    sizes = [mesh.shape[name] for name in ("clip", "tube", "head")]
+
+    def run(*arrays):
+        on_device = on_device_local if fits_local(arrays, *sizes) else on_device_sums
+        return on_mesh(on_device, mesh)(*arrays)
+
+    return run
+
+
+def on_mesh(on_device, mesh):
     return jax.shard_map(
         on_device,
         mesh=mesh,

time: 1760 us -> 643 us (0.37)
  waiting for transfers between devices: 983 us -> 72.7 us
  Pallas kernels: 0 us -> 449 us
  blocking collectives: 242 us -> 33.9 us
  local copies, waits for them, and re-layouts: 241 us -> 36.1 us
  matrix products: 141 us -> 0 us
  other arithmetic: 121 us -> 23.7 us
    psum x7 -> x1, waiting for transfers between devices: 923 us -> 54.2 us  [on_device_local(): small = lax.psum((grad_embed, *small), AXES)]
    pallas_call x0 -> x5, Pallas kernels: none -> 449 us  [the longest x1 190 us: reduce_grads(): pl.pallas_call(lambda *refs: reduce_kernel(heads, block_rows, blocks, *re...]
    unnamed x1 -> x0, blocking collectives: 218 us -> none
    dot_general x32 -> x0, matrix products: 130 us -> none  [the longest x2 15.1 us: block_backward(): grad_wdown = jnp.dot(active.T, grad_low, preferred_element_type=jnp.float32)]
    unnamed x269 -> x49, local copies, waits for them, and re-layouts: 99.9 us -> 11.2 us
    reduce_sum x22 -> x1, other arithmetic: 79.4 us -> 2.31 us  [on_device_local(): grad_embed = jnp.sum(jnp.where(masked, grad_initial, 0.0), 0)]
    all_gather x5 -> x2, waiting for transfers between devices: 55.2 us -> 0.01 us  [the longest x1 0.01 us: on_device_local(): output = lax.all_gather(output, 'head', axis=1, tiled=True)[None]]
    reshape x16 -> x8, local copies, waits for them, and re-layouts: 59.6 us -> 4.82 us  [the longest x1 1.21 us: tubes_to_frames(): array.reshape(tube_share, heads, tube_size, frame_share, patches, width)]
  transfers between devices with their start and end apart: 17 -> 4, of which waited for: 12 -> 2; matrix products, arithmetic and copies ran while one was open for 12% -> 3% of each run, Pallas kernels for 0% -> 30%
where the time goes in v2:
time: 643 us; the launch traced here: 640 us
  Pallas kernels  449 us (70%)
  waiting for transfers between devices  72.7 us (11%)
  local copies, waits for them, and re-layouts  36.1 us (6%)
  blocking collectives  33.9 us (5%)
  other arithmetic  23.7 us (4%)
  between operations  15.7 us (2%)
  starting transfers between devices  9.15 us (1%)
    pallas_call x1, Pallas kernels, reduce_grads(): pl.pallas_call(lambda *refs: reduce_kernel(heads, block_rows, blocks, *re...  190 us
    pallas_call x1, Pallas kernels, gather_weights(): pl.pallas_call(lambda *refs: gather_kernel(heads, block_rows, blocks, *re...  124 us
    pallas_call x1, Pallas kernels, run_both(): pl.pallas_call(kernel, name='both_second', out_shape=structs([((sz.rows,...  60 us
    psum x1, waiting for transfers between devices, on_device_local(): small = lax.psum((grad_embed, *small), AXES)  54.2 us
    pallas_call x1, Pallas kernels, run_backward(): pl.pallas_call(kernel, name='backward_first', out_shape=structs([((sz.row...  44.1 us
    pallas_call x1, Pallas kernels, run_forward(): pl.pallas_call(kernel, name='forward_first', out_shape=structs(saved_shap...  31.1 us
    all_to_all x1, blocking collectives, tubes_to_frames(): lax.all_to_all(order, ('tube', 'head'), 0, 1, tiled=True)  22.3 us
    all_to_all x1, waiting for transfers between devices, frames_to_tubes(): array = lax.all_to_all(array, ('tube', 'head'), 1, 0, tiled=True)  18.4 us
  transfers between devices with their start and end apart: 4, of which 2 were waited for; matrix products, arithmetic and copies ran while one was open for 3% of the time, Pallas kernels for 30%

profile of v2, /device:TPU:1, one launch (start us, length us, event | category | flops | bytes accessed | tf_op | source)
XLA Modules:
  0.0 640.2 jit_solution(8546021772193923446)
XLA Ops:
  10.9 6.4 %pad_maximum_fusion = bf16[2,2304,768]{2,1,0:T(8,128)(2,1)} fusion(bf16[2,768,768]{2,1,0:T(8,128)(2,1)} %param.25, bf16[2,768,768]{2,1,0:T(8,128)(2,1)} %param.23, bf16[2,192,768]{2,1,0:T(8,128)(2,1)} %param.21, bf16[2,576,768]{2,1,0:T(8,128)(2,1)} %bitcast.114), kind=kLoop, calls=%fused_computation | loop fusion | flops 28311552 | bytes 14155776 | tf_op jit(solution)/shard_map/concatenate | solution.py:1058
  18.5 123.8 %gather_weights.1 = (bf16[4,2304,768]{2,1,0:T(8,128)(2,1)}, bf16[4,2304,768]{2,1,0:T(8,128)(2,1)}, f32[4,18,128]{2,1,0:T(8,128)}, bf16[2,16,16,768]{3,2,1,0:T(8,128)(2,1)}, bf16[2,16,16,128]{3,2,1,0:T(8,128)(2,1)}) custom-call(bf16[4608,768]{1,0:T(8,128)(2,1)} %bitcast.98, f32[18,128]{1,0:T(8,128)} %maximum_bitcast_fusion.refs_1_, ...), custom_call_target="tpu_custom_call" | custom-call | tf_op jit(solution)/shard_map/gather_weights/pallas_call | solution.py:847
  143.2 1.5 compare_reduce_fusion
  147.4 2.5 convert_select_fusion.refs_0_.refs_1_
  149.9 31.1 %forward_first.1 = (bf16[512,768]{1,0:T(8,128)(2,1)}, bf16[4,512,192]{2,1,0:T(8,128)(2,1)}, bf16[4,512,192]{2,1,0:T(8,128)(2,1)}, bf16[4,512,192]{2,1,0:T(8,128)...) custom-call(f32[512,768]{1,0:T(8,128)} %convert_select_fusion.refs_0, ...), custom_call_target="tpu_custom_call" | custom-call | tf_op jit(solution)/shard_map/forward_first/pallas_call | solution.py:631
  181.0 1.5 convert_element_type.22
  183.5 8.8 %all-to-all-start = ((bf16[2,16,16,768]{3,2,0,1:T(8,128)(2,1)}), bf16[2,16,16,768]{3,2,0,1:T(8,128)(2,1)S(1)}, u32[]{:S(2)}, u32[]{:S(2)}) async-start(bf16[2,16,16,768]{3,2,0,1:T(8,128)(2,1)} %copy.47), calls=%async_computation | async-start | bytes 1572864 | tf_op jit(solution)/shard_map/all_to_all | solution.py:1084
  194.7 18.4 %all-to-all-done = bf16[2,16,16,768]{3,2,0,1:T(8,128)(2,1)S(1)} async-done(((bf16[2,16,16,768]{3,2,0,1:T(8,128)(2,1)}), bf16[2,16,16,768]{3,2,0,1:T(8,128)(2,1)S(1)}, u32[]{:S(2)}, u32[]{:S(2)}) %all-to-all-start) | async-done | bytes 786464 | tf_op jit(solution)/shard_map/all_to_all | solution.py:1084
  214.1 60.0 %both_second.1 = (bf16[512,768]{1,0:T(8,128)(2,1)}, bf16[512,768]{1,0:T(8,128)(2,1)}, bf16[4,2304,768]{2,1,0:T(8,128)(2,1)}, f32[2,768]{1,0:T(2,128)}, f32[2,768...) custom-call(bf16[512,768]{1,0:T(8,128)(2,1)} %bitcast.101, ...), custom_call_target="tpu_custom_call" | custom-call | tf_op jit(solution)/shard_map/both_second/pallas_call | solution.py:667
  275.3 22.3 %all_to_all.48 = bf16[16,2,16,768]{3,2,1,0:T(8,128)(2,1)S(1)} all-to-all(bf16[16,2,16,768]{3,2,1,0:T(8,128)(2,1)S(1)} %bitcast.108), channel_id=1, replica_groups=mesh['clip'=4,'tube'=2,'head'=4] {'tube','head'}, dimensions={0} | all-to-all | bytes 1572864 | tf_op jit(solution)/shard_map/all_to_all | solution.py:1091
  298.7 44.1 %backward_first.1 = (f32[512,768]{1,0:T(8,128)}, bf16[4,2304,768]{2,1,0:T(8,128)(2,1)}, f32[2,768]{1,0:T(2,128)}, f32[2,768]{1,0:T(2,128)}, f32[4,2,192]{2,1,0:T...) custom-call(bf16[512,768]{1,0:T(8,128)(2,1)} %bitcast.113, ...), custom_call_target="tpu_custom_call" | custom-call | tf_op jit(solution)/shard_map/backward_first/pallas_call | solution.py:647
  342.7 2.3 select_reduce_fusion
  346.3 1.3 pad_maximum_fusion.1
  348.9 1.3 pad_maximum_fusion.2
  350.2 1.3 pad_maximum_fusion.4
  351.5 1.3 pad_maximum_fusion.3
  354.2 11.6 %all_to_all.49 = bf16[2,16,16,768]{3,2,0,1:T(8,128)(2,1)S(1)} all-to-all(bf16[2,16,16,768]{3,2,0,1:T(8,128)(2,1)S(1)} %copy.56), channel_id=1, replica_groups=mesh['clip'=4,'tube'=2,'head'=4] {'tube'}, dimensions={1} | all-to-all | bytes 1572864 | tf_op jit(solution)/shard_map/all_to_all | solution.py:1111
  366.8 190.1 %reduce_grads.1 = bf16[4608,768]{1,0:T(8,128)(2,1)} custom-call(bf16[4,2304,768]{2,1,0:T(8,128)(2,1)} %get-tuple-element.69.refs_0_, bf16[4,2304,768]{2,1,0:T(8,128)(2,1)} %get-tuple-element.70.refs_1_), custom_call_target="tpu_custom_call" | custom-call | tf_op jit(solution)/shard_map/reduce_grads/pallas_call | solution.py:992
  556.9 3.7 slice.83
  562.8 4.6 fusion
  567.3 54.2 %all-reduce.3.cloned.1.call-done = (f32[768]{0:T(1024)}, f32[2,2,768]{2,1,0:T(2,128)}, f32[2,2,768]{2,1,0:T(2,128)}, f32[2,4,2,192]{3,2,1,0:T(2,128)}, f32[2,768...) async-done(((f32[768]{0:T(1024)}, f32[2,2,768]{2,1,0:T(2,128)}, f32[2,2,768]{2,1,0:T(2,128)}, f32[2,4,2,192]{3,2,1,0:T(2,128)}, f32[2,768]{1,0:T(2,128)}, ...) | async-done | bytes 76816 | tf_op jit(solution)/shard_map/psum | solution.py:1114
  622.8 1.3 dynamic-slice_bitcast_fusion.1
  624.1 4.0 copy.79
  628.1 1.7 copy.80
  (83 shorter events, 25.4 us)
Async XLA Ops:
  18.5 127.7 %copy-start.6 = (f32[2,2,768]{2,1,0:T(2,128)S(1)}, f32[2,2,768]{2,1,0:T(2,128)}, u32[]{:S(2)}) copy-start(f32[2,2,768]{2,1,0:T(2,128)} %param.18) | copy-start | bytes 36868
  18.5 127.7 %copy-start.7 = (f32[2,2,768]{2,1,0:T(2,128)S(1)}, f32[2,2,768]{2,1,0:T(2,128)}, u32[]{:S(2)}) copy-start(f32[2,2,768]{2,1,0:T(2,128)} %param.17) | copy-start | bytes 36868
  18.5 128.3 %copy-start.12 = (f32[2,768]{1,0:T(2,128)S(1)}, f32[2,768]{1,0:T(2,128)}, u32[]{:S(2)}) copy-start(f32[2,768]{1,0:T(2,128)} %param.26) | copy-start | bytes 18436
  18.5 128.3 %copy-start.13 = (f32[2,768]{1,0:T(2,128)S(1)}, f32[2,768]{1,0:T(2,128)}, u32[]{:S(2)}) copy-start(f32[2,768]{1,0:T(2,128)} %param.22) | copy-start | bytes 18436
  18.5 128.9 %copy-start.17 = (f32[768]{0:T(1024)S(1)}, f32[768]{0:T(1024)}, u32[]{:S(2)}) copy-start(f32[768]{0:T(1024)} %param.16) | copy-start | bytes 9220
  183.5 29.7 %all-to-all-start = ((bf16[2,16,16,768]{3,2,0,1:T(8,128)(2,1)}), bf16[2,16,16,768]{3,2,0,1:T(8,128)(2,1)S(1)}, u32[]{:S(2)}, u32[]{:S(2)}) async-start(bf16[2,16,16,768]{3,2,0,1:T(8,128)(2,1)} %copy.47), calls=%async_computation | async-start | bytes 1572864 | tf_op jit(solution)/shard_map/all_to_all | solution.py:1084
  192.3 429.2 %all-reduce.3.cloned.1.call-start = ((), (), s32[]{:S(2)}) async-start(), calls=%async_computation.5 | async-start | bytes 163840 | tf_op jit(solution)/shard_map/psum | solution.py:1114
  298.6 46.4 %copy-start.19 = (f32[1,768]{1,0:T(1,128)S(1)}, f32[1,768]{1,0:T(1,128)}, u32[]{:S(2)}) copy-start(f32[1,768]{1,0:T(1,128)} %get-tuple-element.78) | copy-start | bytes 9220
  298.6 47.7 %copy-start.8 = (f32[4,1,768]{2,1,0:T(1,128)S(1)}, f32[4,1,768]{2,1,0:T(1,128)}, u32[]{:S(2)}) copy-start(f32[4,1,768]{2,1,0:T(1,128)} %get-tuple-element.76) | copy-start | bytes 36868
  298.6 49.0 %copy-start.18 = (f32[1,768]{1,0:T(1,128)S(1)}, f32[1,768]{1,0:T(1,128)}, u32[]{:S(2)}) copy-start(f32[1,768]{1,0:T(1,128)} %get-tuple-element.74) | copy-start | bytes 9220
  298.6 50.3 %copy-start.9 = (f32[4,2,192]{2,1,0:T(2,128)S(1)}, f32[4,2,192]{2,1,0:T(2,128)}, u32[]{:S(2)}) copy-start(f32[4,2,192]{2,1,0:T(2,128)} %get-tuple-element.72) | copy-start | bytes 18436
  298.6 51.6 %copy-start.15 = (f32[2,768]{1,0:T(2,128)S(1)}, f32[2,768]{1,0:T(2,128)}, u32[]{:S(2)}) copy-start(f32[2,768]{1,0:T(2,128)} %get-tuple-element.68) | copy-start | bytes 18436
  298.6 52.9 %copy-start.14 = (f32[2,768]{1,0:T(2,128)S(1)}, f32[2,768]{1,0:T(2,128)}, u32[]{:S(2)}) copy-start(f32[2,768]{1,0:T(2,128)} %get-tuple-element.66) | copy-start | bytes 18436
  298.6 54.3 %copy-start.3 = (bf16[512,768]{1,0:T(8,128)(2,1)S(1)}, bf16[512,768]{1,0:T(8,128)(2,1)}, u32[]{:S(2)}) copy-start(bf16[512,768]{1,0:T(8,128)(2,1)} %get-tuple-element.52) | copy-start | bytes 2359300
  342.7 11.3 %copy-start.1 = (f32[512,768]{1,0:T(8,128)S(1)}, f32[512,768]{1,0:T(8,128)}, u32[]{:S(2)}) copy-start(f32[512,768]{1,0:T(8,128)} %get-tuple-element.64) | copy-start | bytes 4718596
  352.9 271.2 %all-gather.3.cloned.1.call-start = ((), (), s32[]{:S(2)}) async-start(), calls=%async_computation.3 | async-start | bytes 3932160 | tf_op jit(solution)/shard_map/all_gather | solution.py:1103
  353.9 270.2 %all-gather.5.cloned.1.call-start = ((), (), s32[]{:S(2)}) async-start(), calls=%async_computation.4 | async-start | bytes 3932160 | tf_op jit(solution)/shard_map/all_gather | solution.py:1112
  556.9 4.8 copy-start
  624.1 4.0 copy-start.2
  628.1 1.7 copy-start.16
  628.1 2.3 copy-start.5
  628.1 2.9 copy-start.4
  628.1 3.5 copy-start.11
  628.1 4.1 copy-start.10
Sparse Core Ops, SparseCore 0:
  353.0 268.5 all-reduce.2
Sparse Core Ops, SparseCore 1:
  355.5 70.5 all-gather.2
  428.1 113.5 all-gather.4

commit v3 on v2

--- a/solution.py
+++ b/solution.py
@@ -430,17 +430,18 @@
         n_ref[at, :] = (normal * gain + shift).astype(LOW)
 
 
-def forward_attention(sz, shard, w_ref, bqv, n_ref, q_ref, k_ref, v_ref, p_ref, o_ref, m_ref):
+def forward_attention(sz, shard, w_ref, b_query, b_value, n_ref, t_ref, p_ref, m_ref):
     cols, length = sz.columns, sz.length
     normed = n_ref[...]
-    q_ref[shard] = (dot(normed, w_ref[shard, 0:cols, :], NT) + bqv[0:1, :]).astype(LOW)
-    k_ref[shard] = dot(normed, w_ref[shard, cols : 2 * cols, :], NT).astype(LOW)
-    v_ref[shard] = (dot(normed, w_ref[shard, 2 * cols : 3 * cols, :], NT) + bqv[1:2, :]).astype(LOW)
+    q_ref, k_ref, v_ref, o_ref = (t_ref.at[shard, i] for i in range(4))
+    q_ref[...] = (dot(normed, w_ref[shard, 0:cols, :], NT) + b_query).astype(LOW)
+    k_ref[...] = dot(normed, w_ref[shard, cols : 2 * cols, :], NT).astype(LOW)
+    v_ref[...] = (dot(normed, w_ref[shard, 2 * cols : 3 * cols, :], NT) + b_value).astype(LOW)
     scaled = head_masks(cols, HD**-0.5)
     masks = head_masks(cols, 1.0)
     for seq in range(sz.sequences):
         at = slice(seq * length, (seq + 1) * length)
-        queries, keys, values = q_ref[shard, at, :], k_ref[shard, at, :], v_ref[shard, at, :]
+        queries, keys, values = q_ref[at, :], k_ref[at, :], v_ref[at, :]
         mixture = jnp.zeros((length, cols), F32)
         for head in range(sz.heads):
             scores = dot(queries * scaled[head], keys, NT)
@@ -448,43 +449,27 @@
             weights = (exponent / jnp.sum(exponent, -1, keepdims=True)).astype(LOW)
             p_ref[shard, seq * sz.heads + head] = weights
             mixture += dot(weights, values * masks[head], NN)
-        o_ref[shard, at, :] = mixture.astype(LOW)
-    m_ref[...] += dot(o_ref[shard], w_ref[shard, sz.out_row : sz.out_row + cols, :], NN)
-
-
-def forward_mlp(sz, shard, w_ref, b_up, n2_ref, a_ref, s_ref, y_ref):
-    hidden = (
-        dot(n2_ref[...], w_ref[shard, sz.up_row : sz.up_row + sz.width, :], NN) + b_up
-    )
+        o_ref[at, :] = mixture.astype(LOW)
+    m_ref[...] += dot(o_ref[...], w_ref[shard, sz.out_row : sz.out_row + cols, :], NN)
+
+
+def forward_up(sz, shard, w_ref, b_up, n2_ref, as_ref):
+    hidden = dot(n2_ref[...], w_ref[shard, sz.up_row : sz.up_row + sz.width, :], NN) + b_up
     active, slope = gelu_pair(hidden)
-    a_ref[shard] = active.astype(LOW)
-    s_ref[shard] = slope.astype(LOW)
-    y_ref[...] += dot(a_ref[shard], w_ref[shard, sz.down_row : sz.down_row + sz.units, :], NN)
-
-
-def forward_block(sz, x_ref, gains_ref, shifts_ref, w_ref, bqv_ref, bout_ref, bup_ref, bdown_ref,
-                  n_ref, q_ref, k_ref, v_ref, p_ref, o_ref, m_ref, n2_ref, a_ref, s_ref, y_ref):
-    norm_rows(sz, x_ref, gains_ref[0:1, :], shifts_ref[0:1, :], n_ref)
-    m_ref[...] = x_ref[...].astype(F32) + bout_ref[...]
-
-    @pl.loop(0, sz.shards)
-    def _(shard):
-        forward_attention(sz, shard, w_ref, bqv_ref[shard], n_ref, q_ref, k_ref, v_ref, p_ref, o_ref, m_ref)
-
-    norm_rows(sz, m_ref, gains_ref[1:2, :], shifts_ref[1:2, :], n2_ref)
-    y_ref[...] = m_ref[...] + bdown_ref[...]
-
-    @pl.loop(0, sz.shards)
-    def _(shard):
-        forward_mlp(sz, shard, w_ref, bup_ref[shard], n2_ref, a_ref, s_ref, y_ref)
-
-
-def backward_mlp(sz, shard, w_ref, gl_ref, n2_ref, a_ref, s_ref, du_ref, dn_ref, g_ref, gbup_ref):
+    as_ref[shard, 0] = active.astype(LOW)
+    as_ref[shard, 1] = slope.astype(LOW)
+
+
+def forward_down(sz, shard, w_ref, as_ref, y_ref):
+    y_ref[...] += dot(as_ref[shard, 0], w_ref[shard, sz.down_row : sz.down_row + sz.units, :], NN)
+
+
+def backward_mlp(sz, shard, w_ref, gl_ref, n2_ref, as_ref, du_ref, dn_ref, g_ref, gbup_ref):
     low = gl_ref[...]
     grad_active = dot(low, w_ref[shard, sz.down_row : sz.down_row + sz.units, :], NT)
-    du_ref[...] = (grad_active * s_ref[shard].astype(F32)).astype(LOW)
+    du_ref[...] = (grad_active * as_ref[shard, 1].astype(F32)).astype(LOW)
     gbup_ref[shard] = jnp.sum(du_ref[...].astype(F32), 0, keepdims=True)
-    g_ref[shard, sz.down_row : sz.down_row + sz.units, :] = dot(a_ref[shard], low, TN).astype(LOW)
+    g_ref[shard, sz.down_row : sz.down_row + sz.units, :] = dot(as_ref[shard, 0], low, TN).astype(LOW)
     g_ref[shard, sz.up_row : sz.up_row + sz.width, :] = dot(n2_ref[...], du_ref[...], TN).astype(LOW)
     dn_ref[...] += dot(du_ref[...], w_ref[shard, sz.up_row : sz.up_row + sz.width, :], NT)
 
@@ -514,18 +499,19 @@
             sum_ref[...] += jnp.sum(total, 0, keepdims=True)
 
 
-def backward_attention(sz, shard, w_ref, dml_ref, n_ref, q_ref, k_ref, v_ref, p_ref, o_ref,
+def backward_attention(sz, shard, w_ref, dml_ref, n_ref, t_ref, p_ref,
                        do_ref, dq_ref, dk_ref, dv_ref, dn_ref, g_ref, gbqv_ref):
     cols, length = sz.columns, sz.length
     low = dml_ref[...]
+    q_ref, k_ref, v_ref, o_ref = (t_ref.at[shard, i] for i in range(4))
     w_out = w_ref[shard, sz.out_row : sz.out_row + cols, :]
     do_ref[...] = dot(low, w_out, NT).astype(LOW)
-    g_ref[shard, sz.out_row : sz.out_row + cols, :] = dot(o_ref[shard], low, TN).astype(LOW)
+    g_ref[shard, sz.out_row : sz.out_row + cols, :] = dot(o_ref[...], low, TN).astype(LOW)
     scaled = head_masks(cols, HD**-0.5)
     masks = head_masks(cols, 1.0)
     for seq in range(sz.sequences):
         at = slice(seq * length, (seq + 1) * length)
-        queries, keys, values = q_ref[shard, at, :], k_ref[shard, at, :], v_ref[shard, at, :]
+        queries, keys, values = q_ref[at, :], k_ref[at, :], v_ref[at, :]
         grad_o = do_ref[at, :]
         dq = jnp.zeros((length, cols), F32)
         dk = jnp.zeros((length, cols), F32)
@@ -550,7 +536,7 @@
         dn_ref[...] += dot(part[...], w_ref[shard, i * cols : (i + 1) * cols, :], NN)
 
 
-def backward_block(sz, up_ref, x_ref, gains_ref, w_ref, n_ref, q_ref, k_ref, v_ref, p_ref, o_ref, m_ref, n2_ref, a_ref, s_ref,
+def backward_block(sz, up_ref, x_ref, gains_ref, w_ref, n_ref, t_ref, p_ref, m_ref, n2_ref, as_ref,
                    gl_ref, du_ref, dn_ref, dm_ref, do_ref, dq_ref, dk_ref, dv_ref,
                    dx_ref, g_ref, ggain_ref, gshift_ref, gbqv_ref, gbout_ref, gbup_ref, gbdown_ref):
     gl_ref[...] = up_ref[...].astype(LOW)
@@ -559,14 +545,14 @@
 
     @pl.loop(0, sz.shards)
     def _(shard):
-        backward_mlp(sz, shard, w_ref, gl_ref, n2_ref, a_ref, s_ref, du_ref, dn_ref, g_ref, gbup_ref)
+        backward_mlp(sz, shard, w_ref, gl_ref, n2_ref, as_ref, du_ref, dn_ref, g_ref, gbup_ref)
 
     norm_back_rows(sz, m_ref, gains_ref[1:2, :], dn_ref, up_ref, dm_ref, ggain_ref, gshift_ref, 1, gbout_ref, gl_ref)
     dn_ref[...] = jnp.zeros_like(dn_ref)
 
     @pl.loop(0, sz.shards)
     def _(shard):
-        backward_attention(sz, shard, w_ref, gl_ref, n_ref, q_ref, k_ref, v_ref, p_ref, o_ref,
+        backward_attention(sz, shard, w_ref, gl_ref, n_ref, t_ref, p_ref,
                            do_ref, dq_ref, dk_ref, dv_ref, dn_ref, g_ref, gbqv_ref)
 
     norm_back_rows(sz, x_ref, gains_ref[0:1, :], dn_ref, dm_ref, dx_ref, ggain_ref, gshift_ref, 0, None, None)
@@ -576,15 +562,11 @@
     s, r, c = sz.shards, sz.rows, sz.columns
     return [
         ((r, sz.width), LOW),
-        ((s, r, c), LOW),
-        ((s, r, c), LOW),
-        ((s, r, c), LOW),
+        ((s, 4, r, c), LOW),
         ((s, sz.sequences * sz.heads, sz.length, sz.length), LOW),
-        ((s, r, c), LOW),
         ((r, sz.width), F32),
         ((r, sz.width), LOW),
-        ((s, r, sz.units), LOW),
-        ((s, r, sz.units), LOW),
+        ((s, 2, r, sz.units), LOW),
     ]
 
 
@@ -625,51 +607,20 @@
 PARAMS = pltpu.CompilerParams(vmem_limit_bytes=62 * 2**20)
 
 
-def run_forward(sz, x, weights):
+def run_backward(sz, up, x, gains, full, saved, name):
+    count = len(grad_shapes(sz))
+    inputs = 4 + len(saved)
+
     def kernel(*refs):
-        forward_block(sz, *refs[:-1], refs[-1])
-    out = pl.pallas_call(
-        kernel, name="forward_first",
-        out_shape=structs(saved_shapes(sz) + [((sz.rows, sz.width), F32)]),
-        compiler_params=PARAMS,
-    )(x, *weights)
-    return out[-1], out[:-1]
-
-
-def run_backward(sz, up, x, weights, saved):
-    nw = len(work_shapes(sz))
-    ng = len(grad_shapes(sz))
-    def kernel(*refs):
-        ins = refs[: 4 + 10]
-        dx, grads = refs[14], refs[15 : 15 + ng]
-        work = refs[15 + ng :]
-        backward_block(sz, *ins, *work, dx, *grads)
+        backward_block(sz, *refs[:inputs], *refs[inputs + 1 + count :], *refs[inputs : inputs + 1 + count])
+
     return pl.pallas_call(
-        kernel, name="backward_first",
+        kernel,
+        name=name,
         out_shape=structs([((sz.rows, sz.width), F32)] + grad_shapes(sz)),
         scratch_shapes=vmems(work_shapes(sz)),
         compiler_params=PARAMS,
-    )(up, x, weights[0], weights[2], *saved)
-
-
-def run_both(sz, x, up, weights):
-    ns, nw, ng = len(saved_shapes(sz)), len(work_shapes(sz)), len(grad_shapes(sz))
-    def kernel(*refs):
-        x_ref, up_ref = refs[:2]
-        w = refs[2:9]
-        y_ref, dx_ref = refs[9:11]
-        grads = refs[11 : 11 + ng]
-        acc, *rest = refs[11 + ng :]
-        saved, work = rest[:ns], rest[ns:]
-        forward_block(sz, x_ref, *w, *saved, acc)
-        y_ref[...] = acc[...].astype(LOW)
-        backward_block(sz, up_ref, x_ref, w[0], w[2], *saved, *work, dx_ref, *grads)
-    return pl.pallas_call(
-        kernel, name="both_second",
-        out_shape=structs([((sz.rows, sz.width), LOW), ((sz.rows, sz.width), LOW)] + grad_shapes(sz)),
-        scratch_shapes=vmems([((sz.rows, sz.width), F32)] + saved_shapes(sz) + work_shapes(sz)),
-        compiler_params=PARAMS,
-    )(x, up, *weights)
+    )(up, x, gains, full, *saved)
 
 
 class Place:
@@ -687,8 +638,20 @@
     def head(self, step):
         return (self.clip, self.y, lax.rem(self.z + step + self.heads, self.heads))
 
+    def across(self, step):
+        return (self.clip, 1 - self.y, lax.rem(self.z + step + self.heads, self.heads))
+
     def peers(self):
         return [self.first, self.second, self.other] + [self.head(d) for d in range(1, self.heads)]
+
+    def clip_peers(self):
+        return [self.head(d) for d in range(1, self.heads)] + [self.across(d) for d in range(self.heads)]
+
+    def all_peers(self):
+        return [
+            (self.first[0] * (1 - self.core) + self.second[0] * self.core, self.y, self.z),
+            self.other,
+        ] + self.clip_peers()
 
 
 def greet(peers):
@@ -765,104 +728,234 @@
     ]
 
 
-def gather_kernel(heads, block_rows, blocks, shard, biases, tokens, marks, *refs):
-    fulls, whole_bias, frames, frame_marks = refs[:blocks], *refs[blocks : blocks + 3]
-    held, send_sem, recv_sem, local_sem, held_sem = refs[blocks + 3 :]
+class Saves:
+    def __init__(self, sem):
+        self.sem, self.count = sem, 0
+
+    def start(self, src, dst):
+        copy = pltpu.make_async_copy(src, dst, self.sem.at[self.count])
+        self.count += 1
+        copy.start()
+        return copy
+
+
+def forward_kernel(sz, blocks, frame_share, tube_share, *refs):
+    (shard, tokens, marks, b_qv, b_up, embed, gains, shifts, b_out, b_down), refs = refs[:10], refs[10:]
+    fulls, refs = refs[:blocks], refs[blocks:]
+    saved, refs = [refs[7 * b : 7 * b + 7] for b in range(blocks)], refs[7 * blocks :]
+    (result, frame_marks), refs = refs[:2], refs[2:]
+    w = refs[:blocks]
+    (
+        frames, bqv, bup, x, n, t, p, m, n2, act, y, y_low, second, send_sem, recv_sem, local_sem, save_sem,
+    ) = refs[blocks:]
+    heads, block_rows, length = sz.shards, sz.block_rows, sz.length
     place = Place(heads)
     moves = Moves(send_sem, recv_sem)
+    local, saves = Saves(local_sem), Saves(save_sem)
     rows = block_rows // PIECES
-    y, z = place.y, place.z
-    count, tubes = frames.shape[0], tokens.shape[1]
-    greet(place.peers())
-    owned = pl.ds((2 * z + y) * count, count)
-    asked = pl.ds((2 * z + 1 - y) * count, count)
-    here, there = pl.ds(y * tubes, tubes), pl.ds((1 - y) * tubes, tubes)
-    across = (place.clip, 1 - y, z)
+    yy, z = place.y, place.z
+    tubes = tokens.shape[1]
+    greet(place.all_peers())
+
+    owned = pl.ds((2 * z + yy) * frame_share, frame_share)
+    asked = pl.ds((2 * z + 1 - yy) * frame_share, frame_share)
+    here, there = pl.ds(yy * tubes, tubes), pl.ds((1 - yy) * tubes, tubes)
     exchange = moves.phase(
         [
-            (src.at[asked], dst.at[:, here], dst.at[:, there], across)
+            (src.at[asked], dst.at[:, here], dst.at[:, there], place.across(0))
             for src, dst in ((tokens, frames), (marks, frame_marks))
         ]
         + [
-            (biases, whole_bias.at[z], whole_bias.at[lax.rem(z + heads - d, heads)], place.head(d))
+            (src, dst.at[z], dst.at[lax.rem(z + heads - d, heads)], place.head(d))
+            for src, dst in ((b_qv, bqv), (b_up, bup))
             for d in range(1, heads)
         ]
     )
-    moves.start(exchange)
-    local = [
-        pltpu.make_async_copy(tokens.at[owned], frames.at[:, here], local_sem.at[0]),
-        pltpu.make_async_copy(marks.at[owned], frame_marks.at[:, here], local_sem.at[1]),
-        pltpu.make_async_copy(biases, whole_bias.at[z], local_sem.at[2]),
-    ]
-    hold = [
-        (
-            pltpu.make_async_copy(shard.at[pl.ds(b * block_rows, block_rows), :], held.at[b], held_sem.at[b]),
-            pltpu.make_async_copy(held.at[b], fulls[b].at[z], local_sem.at[3 + b]),
-        )
-        for b in range(blocks)
-    ]
-    for copy in local:
-        copy.start()
-    for fetch, _ in hold:
-        fetch.start()
+    spread = moves.phase(
+        [
+            (
+                y_low.at[:, pl.ds((heads * ty + tz) * tube_share, tube_share)],
+                second.at[pl.ds((2 * z + yy) * frame_share, frame_share)],
+                second.at[pl.ds((2 * fz + ty) * frame_share, frame_share)],
+                target,
+            )
+            for ty, tz, fz, target in [
+                (yy, lax.rem(z + d, heads), lax.rem(z + heads - d, heads), place.head(d)) for d in range(1, heads)
+            ]
+            + [
+                (1 - yy, lax.rem(z + d, heads), lax.rem(z + heads - d, heads), place.across(d)) for d in range(heads)
+            ]
+        ]
+    )
     work = [
-        gather_phases(place, moves, shard, fulls[b], b * block_rows, i * rows, rows)
+        gather_phases(place, moves, shard, w[b], b * block_rows, i * rows, rows)
         for b in range(blocks)
         for i in range(PIECES)
     ]
+    moves.start(exchange)
     moves.start(work[0][0])
-    for fetch, store in hold:
-        fetch.wait()
-        store.start()
-    for n, phases in enumerate(work):
-        moves.arrive(phases[0])
-        if n + 1 < len(work):
-            moves.start(work[n + 1][0])
-        moves.start(phases[1])
-        if n:
-            moves.arrive(work[n - 1][2])
-            moves.start(work[n - 1][3])
-        moves.arrive(phases[1])
-        moves.start(phases[2])
-    moves.arrive(work[-1][2])
-    moves.start(work[-1][3])
-    for phases in work:
-        moves.arrive(phases[3])
-    moves.arrive(exchange)
+    owns = [
+        local.start(tokens.at[owned], frames.at[:, here]),
+        local.start(marks.at[owned], frame_marks.at[:, here]),
+        local.start(b_qv, bqv.at[z]),
+        local.start(b_up, bup.at[z]),
+    ] + [local.start(shard.at[pl.ds(b * block_rows, block_rows), :], w[b].at[z]) for b in range(blocks)]
+
+    def save(b, index, src, part=None):
+        dst = saved[b][index]
+        return saves.start(src, dst if part is None else dst.at[part])
+
+    def begin_block(b):
+        norm_rows(sz, x, gains[b, 0:1, :], shifts[b, 0:1, :], n)
+        m[...] = x[...] + b_out[b]
+        return [save(b, 0, x), save(b, 1, n)]
+
+    def attention(b, low, high):
+        @pl.loop(low, high)
+        def _(s):
+            forward_attention(sz, s, w[b], bqv[s, 2 * b : 2 * b + 1, :], bqv[s, 2 * b + 1 : 2 * b + 2, :], n, t, p, m)
+
+        at = pl.ds(low, high - low)
+        return [save(b, 2, t.at[at], at), save(b, 3, p.at[at], at)]
+
+    def middle(b):
+        norm_rows(sz, m, gains[b, 1:2, :], shifts[b, 1:2, :], n2)
+        y[...] = m[...] + b_down[b]
+        return [save(b, 4, m), save(b, 5, n2)]
+
+    def up(b, low, high):
+        @pl.loop(low, high)
+        def _(s):
+            forward_up(sz, s, w[b], bup[s, b : b + 1, :], n2, act)
+
+        at = pl.ds(low, high - low)
+        return [save(b, 6, act.at[at], at)]
+
+    def down(b):
+        @pl.loop(0, heads)
+        def _(s):
+            forward_down(sz, s, w[b], act, y)
+
+    def keep(piece):
+        b, i = piece // PIECES, piece % PIECES
+        at = pl.ds(i * rows, rows)
+        return [saves.start(w[b].at[:, at], fulls[b].at[:, at])]
+
+    def arrived(piece):
+        moves.arrive(work[piece][3])
+        return keep(piece)
+
+    def settle(copies):
+        for copy in copies:
+            copy.wait()
+
+    half = heads // 2
+    kept = []
+    early = []
+    for tick in range(6):
+        moves.arrive(work[tick][0])
+        if tick + 1 < 6:
+            moves.start(work[tick + 1][0])
+        moves.start(work[tick][1])
+        if tick:
+            moves.arrive(work[tick - 1][2])
+            moves.start(work[tick - 1][3])
+        if tick == 0:
+            settle(owns)
+            moves.arrive(exchange)
+            tok = frames[...].astype(F32).reshape(sz.rows, sz.width)
+            mark = frame_marks[...].astype(F32).reshape(sz.rows, 128)[:, 0:1]
+            x[...] = jnp.where(mark > 0.5, embed[...], tok)
+            early += begin_block(0)
+        if tick == 2:
+            kept += arrived(0)
+            early += attention(0, 0, half)
+        if tick == 3:
+            kept += arrived(1)
+            early += middle(0)
+            early += up(0, 0, half)
+        if tick == 4:
+            kept += arrived(2)
+            down(0)
+            y_low[...] = y[...].astype(LOW).reshape(y_low.shape)
+            moves.start(spread)
+            mine = local.start(
+                y_low.at[:, pl.ds((heads * yy + z) * tube_share, tube_share)],
+                second.at[pl.ds((2 * z + yy) * frame_share, frame_share)],
+            )
+        if tick == 5:
+            kept += arrived(3)
+            kept += attention(1, 0, half)
+        moves.arrive(work[tick][1])
+        moves.start(work[tick][2])
+        if tick == 2:
+            early += attention(0, half, heads)
+        if tick == 3:
+            early += up(0, half, heads)
+        if tick == 4:
+            moves.arrive(spread)
+            mine.wait()
+            settle(early)
+            for j in range(tube_share):
+                x[j * length : (j + 1) * length, :] = second[:, j].astype(F32).reshape(length, sz.width)
+            kept += begin_block(1)
+        if tick == 5:
+            kept += attention(1, half, heads)
+    kept += middle(1)
+    kept += arrived(4)
+    kept += up(1, 0, heads)
+    moves.arrive(work[5][2])
+    moves.start(work[5][3])
+    kept += arrived(5)
+    down(1)
     moves.finish()
-    for copy in local:
-        copy.wait()
-    for _, store in hold:
-        store.wait()
-
-
-def gather_weights(heads, shard, blocks, biases, tokens, marks, frame_share):
-    total, width = shard.shape
-    block_rows = total // blocks
-    count = blocks * PIECES * 4 * (heads - 1) + 2 + heads - 1
-    hbm = pl.BlockSpec(memory_space=pl.ANY)
-    whole = lambda array: jax.ShapeDtypeStruct(
-        (frame_share, 2 * array.shape[1]) + array.shape[2:], array.dtype
-    )
+    y_low[...] = y[...].astype(LOW).reshape(y_low.shape)
+    kept.append(saves.start(y_low, result))
+    settle(kept)
+
+
+def run_forward(sz, blocks, frame_share, tube_share, shard, tokens, marks, b_qv, b_up, embed, gains, shifts, b_out, b_down):
+    heads, width, rows = sz.shards, sz.width, sz.rows
+    tubes, patches = 2 * tokens.shape[1], tokens.shape[2]
+    frames = tokens.shape[0]
+    saved = [((rows, width), F32)] + saved_shapes(sz)
+    whole_frames = (frame_share, tubes, patches)
+    count = blocks * PIECES * 4 * (heads - 1) + 2 + 2 * (heads - 1) + 2 * heads - 1
+    hbm, vmem = pl.BlockSpec(memory_space=pl.ANY), pl.BlockSpec(memory_space=pltpu.VMEM)
+    full = ((heads, sz.block_rows, width), LOW)
     out = pl.pallas_call(
-        lambda *refs: gather_kernel(heads, block_rows, blocks, *refs),
-        name="gather_weights",
-        out_shape=[jax.ShapeDtypeStruct((heads, block_rows, width), LOW)] * blocks
-        + [jax.ShapeDtypeStruct((heads,) + biases.shape, F32), whole(tokens), whole(marks)],
-        in_specs=[hbm] * 4,
-        out_specs=[hbm] * (blocks + 3),
-        scratch_shapes=[
-            pltpu.VMEM((blocks, block_rows, width), LOW),
+        lambda *refs: forward_kernel(sz, blocks, frame_share, tube_share, *refs),
+        name="forward_both",
+        out_shape=structs([full] * blocks + saved * blocks + [(whole_frames + (width,), LOW), (whole_frames + (128,), LOW)]),
+        in_specs=[hbm] * 5 + [vmem] * 5,
+        out_specs=[hbm] * (blocks + 7 * blocks + 1) + [vmem],
+        scratch_shapes=vmems(
+            [full] * blocks
+            + [
+                (whole_frames + (width,), LOW),
+                ((heads,) + b_qv.shape, F32),
+                ((heads,) + b_up.shape, F32),
+            ]
+            + saved
+            + [
+                ((rows, width), F32),
+                (whole_frames + (width,), LOW),
+                ((frames, tube_share, patches, width), LOW),
+            ]
+        )
+        + [
             pltpu.SemaphoreType.DMA((count,)),
             pltpu.SemaphoreType.DMA((count,)),
-            pltpu.SemaphoreType.DMA((3 + blocks,)),
-            pltpu.SemaphoreType.DMA((blocks,)),
+            pltpu.SemaphoreType.DMA((8,)),
+            pltpu.SemaphoreType.DMA((32,)),
         ],
         compiler_params=pltpu.CompilerParams(
-            collective_id=0, has_side_effects=True, vmem_limit_bytes=60 * 2**20
+            collective_id=0, has_side_effects=True, vmem_limit_bytes=62 * 2**20
         ),
-    )(shard, biases, tokens, marks)
-    return out[:blocks], *out[blocks:]
+    )(shard, tokens, marks, b_qv, b_up, embed, gains, shifts, b_out, b_down)
+    fulls, out = out[:blocks], out[blocks:]
+    saved = [out[7 * b : 7 * b + 7] for b in range(blocks)]
+    return fulls, saved, out[-2], out[-1]
 
 
 class Reduction:
@@ -1022,7 +1115,8 @@
     return (
         (clips, clip_size, tube_size) == (4, 4, 2)
         and frames % devices == 0
-        and tubes % devices == 0
+        and frames == tubes
+        and head_size % 2 == 0
         and width == 4 * columns == units
         and width % 384 == 0
         and columns % HD == 0
@@ -1053,37 +1147,29 @@
     tube_share = tubes // heads
     rows = frame_share * tube_size * tubes * patches
     sz = Sizes(rows, width, heads, columns, units, rows // frame_share)
-    pair = Sizes(rows, width, heads, columns, units, rows // tube_share)
 
     shard = jnp.concatenate(
         [w_qkv.transpose(0, 2, 3, 1).reshape(blocks, 3 * columns, width), w_out, w_up, w_down], 1
     ).reshape(blocks * sz.block_rows, width)
     marks = jnp.broadcast_to(token_mask[0][..., None], (frames, tubes, patches, 128)).astype(LOW)
-    biases = jnp.concatenate([b_qv.reshape(-1), b_up.reshape(-1)]).reshape(-1, 128)
-    full, whole_bias, x_frames, mark_frames = gather_weights(
-        heads, shard, blocks, biases, tokens[0], marks, frame_share
-    )
-    whole_bias = whole_bias.reshape(heads, -1)
-    cut = blocks * 2 * columns
-    whole_bqv = whole_bias[:, :cut].reshape(heads, blocks, 2, columns)
-    whole_bup = whole_bias[:, cut:].reshape(heads, blocks, 1, units)
-
-    def weights_of(b):
-        return (
-            norm_gains[b],
-            norm_shifts[b],
-            full[b],
-            whole_bqv[:, b],
-            b_out[b][None],
-            whole_bup[:, b],
-            b_down[b][None],
-        )
-
-    def frames_to_tubes(array):
-        array = array.reshape(frame_share, tube_size * tubes, patches, width)
-        array = lax.all_to_all(array, ("tube", "head"), 1, 0, tiled=True)
-        order = array.reshape(tube_size, heads, frame_share, tube_share, patches, width)
-        return order.transpose(3, 1, 0, 2, 4, 5).reshape(rows, width)
+    full, saved, output, mark_frames = run_forward(
+        sz,
+        blocks,
+        frame_share,
+        tube_share,
+        shard,
+        tokens[0],
+        marks,
+        b_qv.reshape(2 * blocks, columns),
+        b_up,
+        mask_embed[None],
+        norm_gains,
+        norm_shifts,
+        b_out[:, None],
+        b_down[:, None],
+    )
+    output = output.reshape(tube_share, frames, patches, width).transpose(1, 0, 2, 3)
+    output = lax.all_gather(output, "head", axis=1, tiled=True)[None]
 
     def tubes_to_frames(array):
         order = array.reshape(tube_share, heads, tube_size, frame_share, patches, width)
@@ -1091,19 +1177,14 @@
         return lax.all_to_all(order, ("tube", "head"), 0, 1, tiled=True).reshape(rows, width)
 
     masked = mark_frames[..., :1].reshape(rows, 1) > 0.5
-    initial = jnp.where(masked, mask_embed[None, :], x_frames.reshape(rows, width).astype(F32))
-    first, saved = run_forward(sz, initial, weights_of(0))
-    second = frames_to_tubes(first.astype(LOW))
     upstream = lax.dynamic_slice_in_dim(cotangent[0], head * tube_share, tube_share, 1)
     upstream = upstream.transpose(1, 0, 2, 3).reshape(rows, width)
-    output, grad_second, grads_second, *small_second = run_both(
-        pair, second, upstream, weights_of(1)
-    )
-    output = output.reshape(tube_share, frames, patches, width).transpose(1, 0, 2, 3)
-    output = lax.all_gather(output, "head", axis=1, tiled=True)[None]
-    grad_first = tubes_to_frames(grad_second)
+    grad_second, grads_second, *small_second = run_backward(
+        sz, upstream, saved[1][0], norm_gains[1], full[1], saved[1][1:], "backward_second"
+    )
+    grad_first = tubes_to_frames(grad_second.astype(LOW))
     grad_initial, grads_first, *small_first = run_backward(
-        sz, grad_first, initial, weights_of(0), saved
+        sz, grad_first, saved[0][0], norm_gains[0], full[0], saved[0][1:], "backward_first"
     )
     grad_embed = jnp.sum(jnp.where(masked, grad_initial, 0.0), 0)
     grad_tokens = jnp.where(masked, 0.0, grad_initial).astype(LOW)

time: 643 us -> 598 us (0.930)
  blocking collectives: 33.9 us -> 12.9 us
  Pallas kernels: 449 us -> 436 us
  other arithmetic: 23.7 us -> 16.6 us
    all_to_all x1 -> x0, blocking collectives: 22.3 us -> none  [tubes_to_frames(): lax.all_to_all(order, ('tube', 'head'), 0, 1, tiled=True)]
    pallas_call x4 -> x3, Pallas kernels: 259 us -> 247 us  [the longest x1 159 us: run_forward(): pl.pallas_call(lambda *refs: forward_kernel(sz, blocks, frame_share, tube...]
  transfers between devices with their start and end apart: 4 -> 4, of which waited for: 2 -> 2; matrix products, arithmetic and copies ran while one was open for 3% -> 3% of each run, Pallas kernels for 30% -> 32%
where the time goes in v3:
time: 598 us; the launch traced here: 596 us
  Pallas kernels  436 us (73%)
  waiting for transfers between devices  72.4 us (12%)
  local copies, waits for them, and re-layouts  36.6 us (6%)
  other arithmetic  16.6 us (3%)
  between operations  15.7 us (3%)
  blocking collectives  12.9 us (2%)
    pallas_call x1, Pallas kernels, reduce_grads(): pl.pallas_call(lambda *refs: reduce_kernel(heads, block_rows, blocks, *re...  188 us
    pallas_call x1, Pallas kernels, run_forward(): pl.pallas_call(lambda *refs: forward_kernel(sz, blocks, frame_share, tube...  159 us
    pallas_call x2, Pallas kernels, run_backward(): pl.pallas_call(kernel, name=name, out_shape=structs([((sz.rows, sz.width)...  88.4 us
    psum x1, waiting for transfers between devices, on_device_local(): small = lax.psum((grad_embed, *small), AXES)  53.8 us
    all_to_all x1, waiting for transfers between devices, tubes_to_frames(): lax.all_to_all(order, ('tube', 'head'), 0, 1, tiled=True)  18.1 us
    all_to_all x1, blocking collectives, on_device_local(): grad_tokens = lax.all_to_all(grad_tokens, 'tube', 1, 0, tiled=True)  12.9 us
    unnamed x40, local copies, waits for them, and re-layouts  12.5 us
  transfers between devices with their start and end apart: 4, of which 2 were waited for; matrix products, arithmetic and copies ran while one was open for 3% of the time, Pallas kernels for 32%

profile of v3, /device:TPU:1, one launch (start us, length us, event | category | flops | bytes accessed | tf_op | source)
XLA Modules:
  0.0 595.7 jit_solution(14344792789730735822)
XLA Ops:
  9.0 1.3 broadcast_in_dim.42.refs_8_
  10.3 1.3 broadcast_in_dim.43.refs_9_
  11.6 1.3 reshape.79.refs_3_
  16.3 1.3 slice_bitcast_fusion
  17.6 5.7 pad_maximum_fusion
  24.5 159.0 %forward_both.1 = (bf16[4,2304,768]{2,1,0:T(8,128)(2,1)}, bf16[4,2304,768]{2,1,0:T(8,128)(2,1)}, f32[512,768]{1,0:T(8,128)}, bf16[512,768]{1,0:T(8,128)(2,1)}, b...) custom-call(bf16[4608,768]{1,0:T(8,128)(2,1)} %bitcast.61, ...), custom_call_target="tpu_custom_call" | custom-call | tf_op jit(solution)/shard_map/forward_both/pallas_call | solution.py:926
  183.5 44.2 %backward_second.1 = (f32[512,768]{1,0:T(8,128)}, bf16[4,2304,768]{2,1,0:T(8,128)(2,1)}, f32[2,768]{1,0:T(2,128)}, f32[2,768]{1,0:T(2,128)}, f32[4,2,192]{2,1,0:...) custom-call(bf16[512,768]{1,0:T(8,128)(2,1)} %bitcast.71, ...), custom_call_target="tpu_custom_call" | custom-call | tf_op jit(solution)/shard_map/backward_second/pallas_call | solution.py:617
  227.7 1.5 convert_element_type.14
  230.2 5.5 all-to-all-start
  236.5 18.1 %all-to-all-done = bf16[16,2,16,768]{3,2,1,0:T(8,128)(2,1)S(1)} async-done(((bf16[16,2,16,768]{3,2,1,0:T(8,128)(2,1)}), bf16[16,2,16,768]{3,2,1,0:T(8,128)(2,1)S(1)}, u32[]{:S(2)}, u32[]{:S(2)}) %all-to-all-start) | async-done | bytes 786464 | tf_op jit(solution)/shard_map/all_to_all | solution.py:1177
  255.5 44.2 %backward_first.1 = (f32[512,768]{1,0:T(8,128)}, bf16[4,2304,768]{2,1,0:T(8,128)(2,1)}, f32[2,768]{1,0:T(2,128)}, f32[2,768]{1,0:T(2,128)}, f32[4,2,192]{2,1,0:T...) custom-call(bf16[512,768]{1,0:T(8,128)(2,1)} %bitcast.72, ...), custom_call_target="tpu_custom_call" | custom-call | tf_op jit(solution)/shard_map/backward_first/pallas_call | solution.py:617
  299.7 1.5 pad_maximum_fusion.1
  301.2 1.3 pad_maximum_fusion.2
  302.5 2.2 select_reduce_fusion
  304.7 1.3 maximum_bitcast_fusion
  306.0 1.3 pad_maximum_fusion.3
  308.2 12.9 %all_to_all.33 = bf16[2,16,16,768]{3,2,0,1:T(8,128)(2,1)S(1)} all-to-all(bf16[2,16,16,768]{3,2,0,1:T(8,128)(2,1)S(1)} %copy.37), channel_id=1, replica_groups=mesh['clip'=4,'tube'=2,'head'=4] {'tube'}, dimensions={1} | all-to-all | bytes 1572864 | tf_op jit(solution)/shard_map/all_to_all | solution.py:1192
  322.2 188.5 %reduce_grads.1 = bf16[4608,768]{1,0:T(8,128)(2,1)} custom-call(bf16[4,2304,768]{2,1,0:T(8,128)(2,1)} %get-tuple-element.71.refs_0_, bf16[4,2304,768]{2,1,0:T(8,128)(2,1)} %get-tuple-element.72.refs_1_), custom_call_target="tpu_custom_call" | custom-call | tf_op jit(solution)/shard_map/reduce_grads/pallas_call | solution.py:1085
  510.7 3.7 slice.28
  516.6 4.6 fusion
  521.1 53.8 %all-reduce.3.cloned.1.call-done = (f32[768]{0:T(1024)}, f32[2,2,768]{2,1,0:T(2,128)}, f32[2,2,768]{2,1,0:T(2,128)}, f32[2,4,2,192]{3,2,1,0:T(2,128)}, f32[2,768...) async-done(((f32[768]{0:T(1024)}, f32[2,2,768]{2,1,0:T(2,128)}, f32[2,2,768]{2,1,0:T(2,128)}, f32[2,4,2,192]{3,2,1,0:T(2,128)}, f32[2,768]{1,0:T(2,128)}, ...) | async-done | bytes 76816 | tf_op jit(solution)/shard_map/psum | solution.py:1195
  576.2 1.3 dynamic-slice_bitcast_fusion.1
  577.5 3.9 copy.39
  581.4 3.9 copy.51
  (60 shorter events, 16.6 us)
Async XLA Ops:
  8.0 9.6 %copy-start.3 = (bf16[2,192,768]{2,1,0:T(8,128)(2,1)S(1)}, bf16[2,192,768]{2,1,0:T(8,128)(2,1)}, u32[]{:S(2)}) copy-start(bf16[2,192,768]{2,1,0:T(8,128)(2,1)} %param.21) | copy-start | bytes 1769476
  8.0 9.6 %copy-start.2 = (bf16[2,768,768]{2,1,0:T(8,128)(2,1)S(1)}, bf16[2,768,768]{2,1,0:T(8,128)(2,1)}, u32[]{:S(2)}) copy-start(bf16[2,768,768]{2,1,0:T(8,128)(2,1)} %param.25) | copy-start | bytes 7077892
  227.7 8.1 %copy-start.4 = (bf16[2,16,16,128]{3,2,1,0:T(8,128)(2,1)S(1)}, bf16[2,16,16,128]{3,2,1,0:T(8,128)(2,1)}, u32[]{:S(2)}) copy-start(bf16[2,16,16,128]{3,2,1,0:T(8,128)(2,1)} %get-tuple-element.48) | copy-start | bytes 393220
  230.2 24.3 %all-to-all-start = ((bf16[16,2,16,768]{3,2,1,0:T(8,128)(2,1)}), bf16[16,2,16,768]{3,2,1,0:T(8,128)(2,1)S(1)}, u32[]{:S(2)}, u32[]{:S(2)}) async-start(bf16[16,2,16,768]{3,2,1,0:T(8,128)(2,1)} %bitcast.13), calls=%async_computation | async-start | bytes 1572864 | tf_op jit(solution)/shard_map/all_to_all | solution.py:1177
  235.7 339.2 %all-reduce.3.cloned.1.call-start = ((), (), s32[]{:S(2)}) async-start(), calls=%async_computation.4 | async-start | bytes 163840 | tf_op jit(solution)/shard_map/psum | solution.py:1195
  255.5 44.2 %copy-start.7 = (f32[4,1,768]{2,1,0:T(1,128)S(1)}, f32[4,1,768]{2,1,0:T(1,128)}, u32[]{:S(2)}) copy-start(f32[4,1,768]{2,1,0:T(1,128)} %get-tuple-element.78) | copy-start | bytes 36868
  255.5 45.7 %copy-start.8 = (f32[4,2,192]{2,1,0:T(2,128)S(1)}, f32[4,2,192]{2,1,0:T(2,128)}, u32[]{:S(2)}) copy-start(f32[4,2,192]{2,1,0:T(2,128)} %get-tuple-element.74) | copy-start | bytes 18436
  255.5 49.2 %copy-start.14 = (f32[1,768]{1,0:T(1,128)S(1)}, f32[1,768]{1,0:T(1,128)}, u32[]{:S(2)}) copy-start(f32[1,768]{1,0:T(1,128)} %get-tuple-element.76) | copy-start | bytes 9220
  255.5 49.2 %copy-start.15 = (f32[1,768]{1,0:T(1,128)S(1)}, f32[1,768]{1,0:T(1,128)}, u32[]{:S(2)}) copy-start(f32[1,768]{1,0:T(1,128)} %get-tuple-element.80) | copy-start | bytes 9220
  255.5 50.5 %copy-start.9 = (f32[2,768]{1,0:T(2,128)S(1)}, f32[2,768]{1,0:T(2,128)}, u32[]{:S(2)}) copy-start(f32[2,768]{1,0:T(2,128)} %get-tuple-element.68) | copy-start | bytes 18436
  255.5 50.5 %copy-start.10 = (f32[2,768]{1,0:T(2,128)S(1)}, f32[2,768]{1,0:T(2,128)}, u32[]{:S(2)}) copy-start(f32[2,768]{1,0:T(2,128)} %get-tuple-element.70) | copy-start | bytes 18436
  299.7 8.3 %copy-start.1 = (f32[512,768]{1,0:T(8,128)S(1)}, f32[512,768]{1,0:T(8,128)}, u32[]{:S(2)}) copy-start(f32[512,768]{1,0:T(8,128)} %get-tuple-element.66) | copy-start | bytes 4718596
  307.4 270.1 %all-gather.3.cloned.1.call-start = ((), (), s32[]{:S(2)}) async-start(), calls=%async_computation.2 | async-start | bytes 3932160 | tf_op jit(solution)/shard_map/all_gather | solution.py:1172
  307.9 273.5 %all-gather.5.cloned.1.call-start = ((), (), s32[]{:S(2)}) async-start(), calls=%async_computation.3 | async-start | bytes 3932160 | tf_op jit(solution)/shard_map/all_gather | solution.py:1193
  510.6 4.8 copy-start
  581.4 3.9 copy-start.13
  581.4 4.5 copy-start.6
  581.4 5.1 copy-start.5
  581.4 5.7 copy-start.12
  581.4 6.3 %copy-start.11 = (f32[2,768]{1,0:T(2,128)S(1)}, f32[2,768]{1,0:T(2,128)}, u32[]{:S(2)}) copy-start(f32[2,768]{1,0:T(2,128)} %get-tuple-element.160) | copy-start | bytes 18436
Sparse Core Ops, SparseCore 0:
  307.5 267.3 all-reduce.2
Sparse Core Ops, SparseCore 1:
  309.4 70.4 all-gather.2
  381.8 113.3 all-gather.4

commit v4 on v3

--- a/solution.py
+++ b/solution.py
@@ -464,49 +464,47 @@
     y_ref[...] += dot(as_ref[shard, 0], w_ref[shard, sz.down_row : sz.down_row + sz.units, :], NN)
 
 
-def backward_mlp(sz, shard, w_ref, gl_ref, n2_ref, as_ref, du_ref, dn_ref, g_ref, gbup_ref):
-    low = gl_ref[...]
-    grad_active = dot(low, w_ref[shard, sz.down_row : sz.down_row + sz.units, :], NT)
-    du_ref[...] = (grad_active * as_ref[shard, 1].astype(F32)).astype(LOW)
-    gbup_ref[shard] = jnp.sum(du_ref[...].astype(F32), 0, keepdims=True)
-    g_ref[shard, sz.down_row : sz.down_row + sz.units, :] = dot(as_ref[shard, 0], low, TN).astype(LOW)
-    g_ref[shard, sz.up_row : sz.up_row + sz.width, :] = dot(n2_ref[...], du_ref[...], TN).astype(LOW)
-    dn_ref[...] += dot(du_ref[...], w_ref[shard, sz.up_row : sz.up_row + sz.width, :], NT)
-
-
-def norm_back_rows(sz, x_ref, gain, dn_ref, g_ref, out_ref, gain_ref, shift_ref, at_row, sum_ref, low_ref, chunk=128):
-    gain_ref[at_row : at_row + 1, :] = jnp.zeros((1, sz.width), F32)
-    shift_ref[at_row : at_row + 1, :] = jnp.zeros((1, sz.width), F32)
-    if sum_ref is not None:
-        sum_ref[...] = jnp.zeros_like(sum_ref)
+def backward_mlp(sz, w_ref, as_ref, low_ref, n2_ref, du_ref, dn_ref, down_ref, up_ref, sum_row):
+    low = low_ref[...]
+    grad_active = dot(low, w_ref[sz.width : sz.width + sz.units, :], NT)
+    du_ref[...] = (grad_active * as_ref[1].astype(F32)).astype(LOW)
+    sum_row[...] = jnp.sum(du_ref[...].astype(F32), 0, keepdims=True)
+    down_ref[...] = dot(as_ref[0], low, TN).astype(LOW)
+    up_ref[...] = dot(n2_ref[...], du_ref[...], TN).astype(LOW)
+    dn_ref[...] += dot(du_ref[...], w_ref[0 : sz.width, :], NT)
+
+
+def norm_back_rows(sz, x_ref, gain, dn_ref, g_ref, out_ref, gain_row, shift_row, sum_row, low_ref, chunk=128):
+    for row in (gain_row, shift_row, sum_row):
+        if row is not None:
+            row[...] = jnp.zeros_like(row)
 
     @pl.loop(0, sz.rows, step=chunk)
     def _(start):
         at = pl.ds(pl.multiple_of(start, chunk), chunk)
-        normal, inverse = standardize(x_ref[at, :].astype(F32))
+        normal, inverse = standardize(x_ref[at, :])
         dn = dn_ref[at, :]
         dy = dn * gain
         part = inverse * (
             dy - jnp.mean(dy, -1, keepdims=True) - normal * jnp.mean(dy * normal, -1, keepdims=True)
         )
         total = g_ref[at, :].astype(F32) + part
-        out_ref[at, :] = total.astype(out_ref.dtype)
+        out_ref[at, :] = total
         if low_ref is not None:
             low_ref[at, :] = total.astype(LOW)
-        gain_ref[at_row : at_row + 1, :] += jnp.sum(dn * normal, 0, keepdims=True)
-        shift_ref[at_row : at_row + 1, :] += jnp.sum(dn, 0, keepdims=True)
-        if sum_ref is not None:
-            sum_ref[...] += jnp.sum(total, 0, keepdims=True)
-
-
-def backward_attention(sz, shard, w_ref, dml_ref, n_ref, t_ref, p_ref,
-                       do_ref, dq_ref, dk_ref, dv_ref, dn_ref, g_ref, gbqv_ref):
+        gain_row[...] += jnp.sum(dn * normal, 0, keepdims=True)
+        shift_row[...] += jnp.sum(dn, 0, keepdims=True)
+        if sum_row is not None:
+            sum_row[...] += jnp.sum(total, 0, keepdims=True)
+
+
+def backward_attention(sz, w_ref, t_ref, p_ref, dml_ref, n_ref, do_ref, dq_ref, dk_ref, dv_ref, dn_ref, g_ref, query_row, value_row):
     cols, length = sz.columns, sz.length
     low = dml_ref[...]
-    q_ref, k_ref, v_ref, o_ref = (t_ref.at[shard, i] for i in range(4))
-    w_out = w_ref[shard, sz.out_row : sz.out_row + cols, :]
+    q_ref, k_ref, v_ref, o_ref = (t_ref.at[i] for i in range(4))
+    w_out = w_ref[sz.out_row : sz.out_row + cols, :]
     do_ref[...] = dot(low, w_out, NT).astype(LOW)
-    g_ref[shard, sz.out_row : sz.out_row + cols, :] = dot(o_ref[...], low, TN).astype(LOW)
+    g_ref[sz.out_row : sz.out_row + cols, :] = dot(o_ref[...], low, TN).astype(LOW)
     scaled = head_masks(cols, HD**-0.5)
     masks = head_masks(cols, 1.0)
     for seq in range(sz.sequences):
@@ -517,7 +515,7 @@
         dk = jnp.zeros((length, cols), F32)
         dv = jnp.zeros((length, cols), F32)
         for head in range(sz.heads):
-            weights = p_ref[shard, seq * sz.heads + head]
+            weights = p_ref[seq * sz.heads + head]
             grad_head = grad_o * masks[head]
             dp = dot(grad_head, values, NT)
             dv += dot(weights, grad_head, TN)
@@ -529,33 +527,11 @@
         dk_ref[at, :] = dk.astype(LOW)
         dv_ref[at, :] = dv.astype(LOW)
     normed = n_ref[...]
-    gbqv_ref[shard, 0:1, :] = jnp.sum(dq_ref[...].astype(F32), 0, keepdims=True)
-    gbqv_ref[shard, 1:2, :] = jnp.sum(dv_ref[...].astype(F32), 0, keepdims=True)
+    query_row[...] = jnp.sum(dq_ref[...].astype(F32), 0, keepdims=True)
+    value_row[...] = jnp.sum(dv_ref[...].astype(F32), 0, keepdims=True)
     for i, part in enumerate((dq_ref, dk_ref, dv_ref)):
-        g_ref[shard, i * cols : (i + 1) * cols, :] = dot(part[...], normed, TN).astype(LOW)
-        dn_ref[...] += dot(part[...], w_ref[shard, i * cols : (i + 1) * cols, :], NN)
-
-
-def backward_block(sz, up_ref, x_ref, gains_ref, w_ref, n_ref, t_ref, p_ref, m_ref, n2_ref, as_ref,
-                   gl_ref, du_ref, dn_ref, dm_ref, do_ref, dq_ref, dk_ref, dv_ref,
-                   dx_ref, g_ref, ggain_ref, gshift_ref, gbqv_ref, gbout_ref, gbup_ref, gbdown_ref):
-    gl_ref[...] = up_ref[...].astype(LOW)
-    gbdown_ref[...] = jnp.sum(up_ref[...].astype(F32), 0, keepdims=True)
-    dn_ref[...] = jnp.zeros_like(dn_ref)
-
-    @pl.loop(0, sz.shards)
-    def _(shard):
-        backward_mlp(sz, shard, w_ref, gl_ref, n2_ref, as_ref, du_ref, dn_ref, g_ref, gbup_ref)
-
-    norm_back_rows(sz, m_ref, gains_ref[1:2, :], dn_ref, up_ref, dm_ref, ggain_ref, gshift_ref, 1, gbout_ref, gl_ref)
-    dn_ref[...] = jnp.zeros_like(dn_ref)
-
-    @pl.loop(0, sz.shards)
-    def _(shard):
-        backward_attention(sz, shard, w_ref, gl_ref, n_ref, t_ref, p_ref,
-                           do_ref, dq_ref, dk_ref, dv_ref, dn_ref, g_ref, gbqv_ref)
-
-    norm_back_rows(sz, x_ref, gains_ref[0:1, :], dn_ref, dm_ref, dx_ref, ggain_ref, gshift_ref, 0, None, None)
+        g_ref[i * cols : (i + 1) * cols, :] = dot(part[...], normed, TN).astype(LOW)
+        dn_ref[...] += dot(part[...], w_ref[i * cols : (i + 1) * cols, :], NN)
 
 
 def saved_shapes(sz):
@@ -570,57 +546,12 @@
     ]
 
 
-def work_shapes(sz):
-    r, c = sz.rows, sz.columns
-    return [
-        ((r, sz.width), LOW),
-        ((r, sz.units), LOW),
-        ((r, sz.width), F32),
-        ((r, sz.width), F32),
-        ((r, c), LOW),
-        ((r, c), LOW),
-        ((r, c), LOW),
-        ((r, c), LOW),
-    ]
-
-
-def grad_shapes(sz):
-    return [
-        ((sz.shards, sz.block_rows, sz.width), LOW),
-        ((2, sz.width), F32),
-        ((2, sz.width), F32),
-        ((sz.shards, 2, sz.columns), F32),
-        ((1, sz.width), F32),
-        ((sz.shards, 1, sz.units), F32),
-        ((1, sz.width), F32),
-    ]
-
-
 def structs(shapes):
     return [jax.ShapeDtypeStruct(s, d) for s, d in shapes]
 
 
 def vmems(shapes):
     return [pltpu.VMEM(s, d) for s, d in shapes]
-
-
-PARAMS = pltpu.CompilerParams(vmem_limit_bytes=62 * 2**20)
-
-
-def run_backward(sz, up, x, gains, full, saved, name):
-    count = len(grad_shapes(sz))
-    inputs = 4 + len(saved)
-
-    def kernel(*refs):
-        backward_block(sz, *refs[:inputs], *refs[inputs + 1 + count :], *refs[inputs : inputs + 1 + count])
-
-    return pl.pallas_call(
-        kernel,
-        name=name,
-        out_shape=structs([((sz.rows, sz.width), F32)] + grad_shapes(sz)),
-        scratch_shapes=vmems(work_shapes(sz)),
-        compiler_params=PARAMS,
-    )(up, x, gains, full, *saved)
 
 
 class Place:
@@ -663,7 +594,7 @@
 
 class Moves:
     def __init__(self, send_sem, recv_sem):
-        self.send_sem, self.recv_sem, self.count, self.sent = send_sem, recv_sem, 0, []
+        self.send_sem, self.recv_sem, self.count, self.sent = send_sem, recv_sem, 0, {}
 
     def phase(self, copies):
         made = []
@@ -679,7 +610,7 @@
                 src, dst, self.send_sem.at[n], self.recv_sem.at[n], device_id=target, device_id_type=MESH
             )
             copy.start()
-            self.sent.append(copy)
+            self.sent[n] = copy
 
     def arrive(self, made):
         for src, _, landing, target, n in made:
@@ -687,10 +618,15 @@
                 src, landing, self.send_sem.at[n], self.recv_sem.at[n], device_id=target, device_id_type=MESH
             ).wait_recv()
 
+    def left(self, made):
+        for *_, n in made:
+            if n in self.sent:
+                self.sent.pop(n).wait_send()
+
     def finish(self):
-        for copy in self.sent:
+        for copy in self.sent.values():
             copy.wait_send()
-        self.sent = []
+        self.sent = {}
 
 
 PIECES = 3
@@ -958,68 +894,114 @@
     return fulls, saved, out[-2], out[-1]
 
 
+class Line:
+    def __init__(self, place, send_sem, recv_sem, region):
+        self.place, self.send_sem, self.recv_sem, self.region = place, send_sem, recv_sem, region
+        self.steps = place.heads - 1
+
+    def moves(self, step):
+        z, last = self.place.z, self.place.heads - 1
+        return [
+            ((z >= step) & (z < last), z - step, 1, z > step, z - 1 - step, 2 * step),
+            ((z <= last - step) & (z > 0), z + step, -1, z < last - step, z + 1 + step, 2 * step + 1),
+        ]
+
+    def copy(self, block, way, n):
+        return pltpu.make_async_remote_copy(
+            self.region(block),
+            self.region(block),
+            self.send_sem.at[n],
+            self.recv_sem.at[n],
+            device_id=self.place.head(way),
+            device_id_type=MESH,
+        )
+
+    def start(self, step):
+        for sends, block, way, _, _, n in self.moves(step):
+            pl.when(sends)(lambda block=block, way=way, n=n: self.copy(block, way, n).start())
+
+    def arrive(self, step):
+        for _, _, way, gets, block, n in self.moves(step):
+            pl.when(gets)(lambda block=block, way=way, n=n: self.copy(block, way, n).wait_recv())
+
+    def finish(self):
+        for step in range(self.steps):
+            for sends, block, way, _, _, n in self.moves(step):
+                pl.when(sends)(lambda block=block, way=way, n=n: self.copy(block, way, n).wait_send())
+
+
 class Reduction:
-    def __init__(self, place, moves, grads, out, offset, out_row, rows, own, core_buf, first_buf, second_buf, head_buf, local_sem):
+    def __init__(self, place, moves, grads, out, out_row, rows, bufs, final_buf, final_sem):
         q = rows // 8
-        self.q, self.place, self.moves = q, place, moves
-        self.grads, self.out, self.out_row = grads, out, out_row
-        self.own, self.core_buf, self.first_buf, self.second_buf, self.head_buf = own, core_buf, first_buf, second_buf, head_buf
+        self.q, self.place, self.moves, self.grads = q, place, moves, grads
+        self.core_buf, self.first_buf, self.second_buf, self.head_buf = bufs
+        self.final_buf, self.final_sem = final_buf, final_sem
         c, i, j, z, heads = place.core, place.i, place.j, place.z, place.heads
-        cut = lambda ref, start, size: ref.at[:, pl.ds(pl.multiple_of(start * q, q), size * q), :]
-        half = lambda core: grads.at[:, pl.ds(pl.multiple_of(offset + core * 4 * q, q), 4 * q), :]
+        cut = lambda start, size: pl.ds(pl.multiple_of(start * q, q), size * q)
         row = lambda start, size: out.at[pl.ds(pl.multiple_of(out_row + start * q, q), size * q), :]
-        self.load = pltpu.make_async_copy(half(c), own, local_sem)
-        self.core = moves.phase([(half(1 - c), core_buf, core_buf, place.other)])
-        self.first = moves.phase([(cut(own, 2 * (1 - i), 2), first_buf, first_buf, place.first)])
-        self.second = moves.phase([(cut(own, 2 * i + 1 - j, 1), second_buf, second_buf, place.second)])
-        mine = 2 * i + j
-        at = pl.ds(pl.multiple_of(mine * q, q), q)
-        self.mine = at
+        self.kept, self.given = cut(4 * c, 4), cut(4 * (1 - c), 4)
+        self.part, self.subpart = cut(2 * i, 2), cut(j, 1)
+        shards = range(heads)
+        self.core = moves.phase(
+            [(grads.at[s % 2, self.given, :], self.core_buf.at[s], self.core_buf.at[s], place.other) for s in shards]
+        )
+        self.first = moves.phase(
+            [
+                (self.core_buf.at[s, cut(2 * (1 - i), 2), :], self.first_buf.at[s], self.first_buf.at[s], place.first)
+                for s in shards
+            ]
+        )
+        self.second = moves.phase(
+            [(self.first_buf.at[:, cut(1 - j, 1), :], self.second_buf, self.second_buf, place.second)]
+        )
         self.heads = moves.phase(
-            [(own.at[lax.rem(z + d, heads), at, :], head_buf.at[d - 1], head_buf.at[d - 1], place.head(d)) for d in range(1, heads)]
+            [
+                (self.second_buf.at[lax.rem(z + d, heads)], self.head_buf.at[d - 1], self.head_buf.at[d - 1], place.head(d))
+                for d in range(1, heads)
+            ]
         )
-        a = 4 * c
+        a, mine = 4 * c, 2 * i + j
         self.share_second = moves.phase([(row(a + mine, 1), row(a + mine, 1), row(a + 2 * i + 1 - j, 1), place.second)])
         self.share_first = moves.phase([(row(a + 2 * i, 2), row(a + 2 * i, 2), row(a + 2 * (1 - i), 2), place.first)])
         self.share_core = moves.phase([(row(a, 4), row(a, 4), row(4 - a, 4), place.other)])
         self.final_row = row(a + mine, 1)
 
-    def begin(self):
-        self.load.start()
-        self.moves.start(self.core)
-
-    def add(self, buf, start, size):
-        q = self.q
-        shards = self.own.shape[0]
-        at = pl.ds(pl.multiple_of(start * q, q), size * q)
-
-        @pl.loop(0, shards)
+    def give(self, s):
+        self.moves.start([self.core[s]])
+
+    def step_first(self, s):
+        self.moves.arrive([self.core[s]])
+        self.core_buf[s] = self.core_buf[s] + self.grads[s % 2, self.kept, :]
+        self.moves.start([self.first[s]])
+
+    def step_second(self, free_sem=None):
+        self.moves.arrive(self.first)
+
+        @pl.loop(0, self.place.heads)
         def _(s):
-            self.own[s, at, :] = self.own[s, at, :] + buf[s]
-
-    def step_first(self):
-        self.load.wait()
-        self.moves.arrive(self.core)
-        self.add(self.core_buf, 0, 4)
-        self.moves.start(self.first)
-
-    def step_second(self):
-        self.moves.arrive(self.first)
-        self.add(self.first_buf, 2 * self.place.i, 2)
+            self.first_buf[s] = self.first_buf[s] + self.core_buf[s, self.part, :]
+
         self.moves.start(self.second)
+        if free_sem is not None:
+            self.moves.left(self.first)
+            pl.semaphore_signal(free_sem, inc=1, device_id=self.place.other, device_id_type=MESH)
 
     def step_heads(self):
         self.moves.arrive(self.second)
-        self.add(self.second_buf, 2 * self.place.i + self.place.j, 1)
+
+        @pl.loop(0, self.place.heads)
+        def _(s):
+            self.second_buf[s] = self.second_buf[s] + self.first_buf[s, self.subpart, :]
+
         self.moves.start(self.heads)
 
-    def step_share(self, final_buf, sem):
+    def step_share(self):
         self.moves.arrive(self.heads)
-        total = self.own[self.place.z, self.mine, :].astype(F32)
+        total = self.second_buf[self.place.z].astype(F32)
         for d in range(self.place.heads - 1):
             total += self.head_buf[d].astype(F32)
-        final_buf[...] = total.astype(LOW)
-        copy = pltpu.make_async_copy(final_buf, self.final_row, sem)
+        self.final_buf[...] = total.astype(LOW)
+        copy = pltpu.make_async_copy(self.final_buf, self.final_row, self.final_sem)
         copy.start()
         copy.wait()
         self.moves.start(self.share_second)
@@ -1036,75 +1018,378 @@
         self.moves.arrive(self.share_core)
 
 
-def reduce_kernel(heads, block_rows, blocks, *refs):
-    grads, out = refs[:blocks], refs[blocks]
-    own, core_buf, first_buf, second_buf, head_buf, final_buf, send_sem, recv_sem, local_sem, final_sem = refs[blocks + 1 :]
+SMALL_ROWS = 48
+GAIN_ROW, SHIFT_ROW, BOUT_ROW, BDOWN_ROW, BUP_ROW, BQV_ROW = 1, 5, 9, 11, 16, 24
+DOWN, UP, ATTN = 0, 1, 2
+
+
+def backward_kernel(sz, blocks, frame_share, tube_share, *refs):
+    fulls, refs = refs[:blocks], refs[blocks:]
+    saved, refs = [refs[7 * b : 7 * b + 7] for b in range(blocks)], refs[7 * blocks :]
+    (cotangent, result, marks, gains), refs = refs[:4], refs[4:]
+    (out_result, out_tokens, out_grads, out_small), refs = refs[:4], refs[4:]
+    (
+        wm, act, wa, t, p, m, n2, n, x, low, dn, dm, du, do, dq, dk, dv, cot, dx_low, back, res,
+        grads, core_buf, first_buf, second_buf, head_buf, final_buf, small, small_in, small_heads, small_last,
+        send_sem, recv_sem, line_sem, load_sem, copy_sem, final_sem, free_sem,
+    ) = refs
+    heads, width, length = sz.shards, sz.width, sz.length
     place = Place(heads)
     moves = Moves(send_sem, recv_sem)
-    rows = block_rows // PIECES
-    greet(place.peers())
-    work = []
-    for n in range(blocks * PIECES):
-        b, i = blocks - 1 - n // PIECES, PIECES - 1 - n % PIECES
-        work.append(
-            Reduction(
-                place, moves, grads[b], out, i * rows, b * block_rows + i * rows, rows,
-                own.at[n], core_buf.at[n], first_buf.at[n], second_buf.at[n], head_buf.at[n], local_sem.at[n],
+    loads = Saves(copy_sem)
+    yy, z = place.y, place.z
+    tubes = cotangent.shape[1]
+
+    def step_loads(b, kind, s):
+        slot = s % 2
+        if kind == "mlp":
+            pairs = [(fulls[b].at[s, pl.ds(sz.up_row, 2 * width), :], wm.at[slot]), (saved[b][6].at[s], act.at[slot])]
+            base = 0
+        else:
+            pairs = [
+                (fulls[b].at[s, pl.ds(0, sz.up_row), :], wa.at[slot]),
+                (saved[b][2].at[s], t.at[slot]),
+                (saved[b][3].at[s], p.at[slot]),
+            ]
+            base = 4
+        return [
+            pltpu.make_async_copy(src, dst, load_sem.at[base + slot * len(pairs) + i]) for i, (src, dst) in enumerate(pairs)
+        ]
+
+    steps = [(b, kind, s) for b in (1, 0) for kind in ("mlp", "attn") for s in range(heads)]
+
+    def fetch(i):
+        if i < len(steps):
+            for copy in step_loads(*steps[i]):
+                copy.start()
+
+    def ready(i):
+        for copy in step_loads(*steps[i]):
+            copy.wait()
+        fetch(i + 1)
+
+    first_loads = [
+        loads.start(cotangent.at[:, pl.ds(z * tube_share, tube_share)], cot),
+        loads.start(result, res),
+    ]
+    fetch(0)
+    norm_loads = [loads.start(saved[1][4], m), loads.start(saved[1][5], n2)]
+    later_loads = [loads.start(saved[1][1], n), loads.start(saved[1][0], x)]
+    small[...] = jnp.zeros_like(small)
+    greet(place.all_peers())
+
+    red = {}
+    for b in (1, 0):
+        for k in (DOWN, UP, ATTN):
+            base = b * sz.block_rows + (sz.down_row, sz.up_row, 0)[k]
+            red[b, k] = Reduction(
+                place,
+                moves,
+                grads.at[k],
+                out_grads,
+                base,
+                width,
+                (core_buf.at[k], first_buf.at[b, k], second_buf.at[b, k], head_buf.at[b, k]),
+                final_buf.at[b, k],
+                final_sem.at[b * 3 + k],
             )
+    tube_region = lambda block: out_result.at[:, pl.ds(block * tube_share, tube_share)]
+    line = Line(place, line_sem.at[0], line_sem.at[1], tube_region)
+    spread = moves.phase(
+        [
+            (
+                dx_low.at[pl.ds((2 * tz + ty) * frame_share, frame_share)],
+                back.at[:, pl.ds((heads * yy + z) * tube_share, tube_share)],
+                back.at[:, pl.ds((heads * ty + fz) * tube_share, tube_share)],
+                target,
+            )
+            for ty, tz, fz, target in [
+                (yy, lax.rem(z + d, heads), lax.rem(z + heads - d, heads), place.head(d)) for d in range(1, heads)
+            ]
+            + [
+                (1 - yy, lax.rem(z + d, heads), lax.rem(z + heads - d, heads), place.across(d)) for d in range(heads)
+            ]
+        ]
+    )
+
+    for copy in first_loads:
+        copy.wait()
+    own_result = [
+        loads.start(res.at[j], out_result.at[:, z * tube_share + j]) for j in range(tube_share)
+    ]
+    frames = cot.shape[0]
+    for j in range(tube_share):
+        low[j * length : (j + 1) * length, :] = cot[:, j].reshape(length, width)
+    for copy in own_result:
+        copy.wait()
+    line.start(0)
+
+    def row(r, columns=None):
+        return small.at[r : r + 1, :] if columns is None else small.at[r : r + 1, 0:columns]
+
+    def mlp(b, pumps):
+        row(BDOWN_ROW + b)[...] = jnp.sum(low[...].astype(F32), 0, keepdims=True)
+        dn[...] = jnp.zeros_like(dn)
+        for copy in norm_loads:
+            copy.wait()
+        for s in range(heads):
+            ready((1 - b) * 2 * heads + s)
+            for k in (DOWN, UP):
+                if s >= 2:
+                    moves.left([red[b, k].core[s - 2]])
+                elif b == 0:
+                    moves.left([red[1, k].core[s + heads - 2]])
+            backward_mlp(
+                sz, wm.at[s % 2], act.at[s % 2], low, n2, du, dn, grads.at[DOWN, s % 2], grads.at[UP, s % 2],
+                row(BUP_ROW + b * heads + s),
+            )
+            for k in (DOWN, UP):
+                if s == 0 and b == 0:
+                    pl.semaphore_wait(free_sem.at[k], 1)
+                red[b, k].give(s)
+            if s:
+                for k in (DOWN, UP):
+                    red[b, k].step_first(s - 1)
+            pumps[s]()
+        norm_back_rows(
+            sz, m, gains[b, 1:2, :], dn, low, dm, row(GAIN_ROW + 2 * b + 1), row(SHIFT_ROW + 2 * b + 1), row(BOUT_ROW + b), low
         )
-    count = len(work)
-    work[0].begin()
-    for tick in range(count + 6):
-        if tick + 1 < count:
-            work[tick + 1].begin()
-        if tick < count:
-            work[tick].step_first()
-        if 0 <= tick - 1 < count:
-            work[tick - 1].step_second()
-        if 0 <= tick - 2 < count:
-            work[tick - 2].step_heads()
-        if 0 <= tick - 3 < count:
-            work[tick - 3].step_share(final_buf.at[tick - 3], final_sem.at[tick - 3])
-        if 0 <= tick - 4 < count:
-            work[tick - 4].step_share_first()
-        if 0 <= tick - 5 < count:
-            work[tick - 5].step_share_core()
-        if 0 <= tick - 6 < count:
-            work[tick - 6].end()
+        for k in (DOWN, UP):
+            red[b, k].step_first(heads - 1)
+
+    def attention(b, pumps):
+        dn[...] = jnp.zeros_like(dn)
+        for copy in later_loads:
+            copy.wait()
+        for s in range(heads):
+            ready((1 - b) * 2 * heads + heads + s)
+            if s >= 2:
+                moves.left([red[b, ATTN].core[s - 2]])
+            elif b == 0:
+                moves.left([red[1, ATTN].core[s + heads - 2]])
+            r = BQV_ROW + 2 * (b * heads + s)
+            backward_attention(
+                sz, wa.at[s % 2], t.at[s % 2], p.at[s % 2], low, n, do, dq, dk, dv, dn, grads.at[ATTN, s % 2],
+                row(r, sz.columns), row(r + 1, sz.columns),
+            )
+            if s == 0 and b == 0:
+                pl.semaphore_wait(free_sem.at[ATTN], 1)
+            red[b, ATTN].give(s)
+            if s:
+                red[b, ATTN].step_first(s - 1)
+            pumps[s]()
+        norm_back_rows(
+            sz, x, gains[b, 0:1, :], dn, dm, dm, row(GAIN_ROW + 2 * b), row(SHIFT_ROW + 2 * b), None, None
+        )
+
+    def nothing():
+        pass
+
+    def pass_on(step):
+        line.arrive(step)
+        if step + 1 < line.steps:
+            line.start(step + 1)
+
+    def do_all(*actions):
+        def run():
+            for action in actions:
+                action()
+
+        return run
+
+    one = {k: red[1, k] for k in (DOWN, UP, ATTN)}
+    nought = {k: red[0, k] for k in (DOWN, UP, ATTN)}
+
+    mlp(1, [nothing] * heads)
+    norm_loads = [loads.start(saved[0][4], m), loads.start(saved[0][5], n2)]
+    attention(1, [nothing, lambda: pass_on(0), nothing, nothing])
+    later_loads = [loads.start(saved[0][1], n), loads.start(saved[0][0], x)]
+    for j in range(tube_share):
+        dx_low[:, j] = dm[j * length : (j + 1) * length, :].astype(LOW).reshape(frames, length // frames, width)
+    moves.start(spread)
+    mine = loads.start(
+        dx_low.at[pl.ds((2 * z + yy) * frame_share, frame_share)],
+        back.at[:, pl.ds((heads * yy + z) * tube_share, tube_share)],
+    )
+    one[ATTN].step_first(heads - 1)
+    one[DOWN].step_second(free_sem.at[DOWN])
+    one[UP].step_second(free_sem.at[UP])
+    moves.arrive(spread)
+    mine.wait()
+    low[...] = back[...].reshape(sz.rows, width)
+    mlp(
+        0,
+        [
+            lambda: one[DOWN].step_heads(),
+            do_all(lambda: one[ATTN].step_second(free_sem.at[ATTN]), lambda: pass_on(1)),
+            lambda: one[UP].step_heads(),
+            lambda: one[DOWN].step_share(),
+        ],
+    )
+    attention(
+        0,
+        [
+            do_all(lambda: one[ATTN].step_heads(), lambda: one[DOWN].step_share_first()),
+            do_all(lambda: one[UP].step_share(), lambda: one[DOWN].step_share_core()),
+            do_all(lambda: pass_on(2), lambda: one[UP].step_share_first()),
+            do_all(lambda: one[ATTN].step_share(), lambda: one[UP].step_share_core()),
+        ],
+    )
+    mark = marks[...].astype(F32).reshape(sz.rows, 128)[:, 0:1] > 0.5
+    grad = dm[...]
+    row(0)[...] = jnp.sum(jnp.where(mark, grad, 0.0), 0, keepdims=True)
+    back[...] = jnp.where(mark, 0.0, grad).astype(LOW).reshape(back.shape)
+    here, there = pl.ds(yy * tubes, tubes), pl.ds((1 - yy) * tubes, tubes)
+    own_frames = lambda block: out_tokens.at[pl.ds((2 * block + yy) * frame_share, frame_share)]
+    far_frames = lambda block: out_tokens.at[pl.ds((2 * block + 1 - yy) * frame_share, frame_share)]
+    cross = moves.phase([(back.at[:, there], own_frames(z), far_frames(z), place.across(0))])
+    own_line = Line(place, line_sem.at[2], line_sem.at[3], own_frames)
+    far_line = Line(place, line_sem.at[4], line_sem.at[5], far_frames)
+    half = SMALL_ROWS // 2
+    part = pl.ds(pl.multiple_of(place.core * half, half), half)
+    small_steps = [
+        moves.phase([(small, small_in.at[i], small_in.at[i], target)])
+        for i, target in enumerate((place.other, place.first, place.second))
+    ]
+    small_z = moves.phase(
+        [(small.at[part], small_heads.at[d - 1], small_heads.at[d - 1], place.head(d)) for d in range(1, heads)]
+    )
+    far_part = pl.ds(pl.multiple_of((1 - place.core) * half, half), half)
+    small_end = moves.phase([(small_last.at[part], small_last.at[part], small_last.at[far_part], place.other)])
+
+    def add_small(i):
+        moves.arrive(small_steps[i])
+        moves.left(small_steps[i])
+        small[...] += small_in[i]
+        moves.start(small_steps[i + 1] if i + 1 < len(small_steps) else small_z)
+
+    moves.start(cross)
+    own_copy = loads.start(back.at[:, here], own_frames(z))
+    moves.start(small_steps[0])
+    nought[ATTN].step_first(heads - 1)
+    own_copy.wait()
+    own_line.start(0)
+    nought[DOWN].step_second()
+    add_small(0)
+    nought[UP].step_second()
+    moves.arrive(cross)
+    far_line.start(0)
+    add_small(1)
+    nought[DOWN].step_heads()
+    nought[ATTN].step_second()
+    add_small(2)
+    one[ATTN].step_share_first()
+    own_line.arrive(0)
+    own_line.start(1)
+    nought[UP].step_heads()
+    one[UP].end()
+    one[DOWN].end()
+    nought[DOWN].step_share()
+    far_line.arrive(0)
+    far_line.start(1)
+    nought[ATTN].step_heads()
+    one[ATTN].step_share_core()
+    nought[UP].step_share()
+    nought[DOWN].step_share_first()
+    own_line.arrive(1)
+    own_line.start(2)
+    moves.arrive(small_z)
+    total = small[part, :]
+    for d in range(heads - 1):
+        total += small_heads[d]
+    small_last[part, :] = total
+    moves.start(small_end)
+    nought[DOWN].step_share_core()
+    nought[UP].step_share_first()
+    nought[ATTN].step_share()
+    far_line.arrive(1)
+    far_line.start(2)
+    nought[UP].step_share_core()
+    nought[ATTN].step_share_first()
+    moves.arrive(small_end)
+    out_small[...] = small_last[...]
+    nought[ATTN].step_share_core()
+    own_line.arrive(2)
+    far_line.arrive(2)
+    one[ATTN].end()
+    for k in (DOWN, UP, ATTN):
+        nought[k].end()
+    for each in (line, own_line, far_line):
+        each.finish()
     moves.finish()
 
 
-def reduce_grads(heads, grads):
-    blocks = len(grads)
-    _, block_rows, width = grads[0].shape
-    rows = block_rows // PIECES
-    n = blocks * PIECES
-    q = rows // 8
-    count = n * (6 + heads - 1)
-    hbm = pl.BlockSpec(memory_space=pl.ANY)
+def run_backward(sz, blocks, frame_share, tube_share, fulls, saved, cotangent, result, marks, gains):
+    heads, width, rows, cols = sz.shards, sz.width, sz.rows, sz.columns
+    frames, tubes, patches = cotangent.shape[:3]
+    hbm, vmem = pl.BlockSpec(memory_space=pl.ANY), pl.BlockSpec(memory_space=pltpu.VMEM)
+    q = width // 8
+    local = (frame_share, 2 * tubes, patches, width)
+    mixed = (frames, tube_share, patches, width)
+    kinds = 3 * blocks
+    count = kinds * (2 * heads + 4 + heads - 1) + 2 * heads - 1 + 1 + 4 + heads - 1
+    flat = [array for per in saved for array in per]
     return pl.pallas_call(
-        lambda *refs: reduce_kernel(heads, block_rows, blocks, *refs),
-        name="reduce_grads",
-        out_shape=jax.ShapeDtypeStruct((blocks * block_rows, width), LOW),
-        in_specs=[hbm] * blocks,
-        out_specs=hbm,
-        scratch_shapes=[
-            pltpu.VMEM((n, heads, 4 * q, width), LOW),
-            pltpu.VMEM((n, heads, 4 * q, width), LOW),
-            pltpu.VMEM((n, heads, 2 * q, width), LOW),
-            pltpu.VMEM((n, heads, q, width), LOW),
-            pltpu.VMEM((n, heads - 1, q, width), LOW),
-            pltpu.VMEM((n, q, width), LOW),
+        lambda *refs: backward_kernel(sz, blocks, frame_share, tube_share, *refs),
+        name="backward_both",
+        out_shape=structs(
+            [
+                (cotangent.shape, LOW),
+                (cotangent.shape, LOW),
+                ((blocks * sz.block_rows, width), LOW),
+                ((SMALL_ROWS, width), F32),
+            ]
+        ),
+        in_specs=[hbm] * (blocks + len(flat) + 2) + [vmem] * 2,
+        out_specs=[hbm] * 3 + [vmem],
+        scratch_shapes=vmems(
+            [
+                ((2, 2 * width, width), LOW),
+                ((2, 2, rows, sz.units), LOW),
+                ((2, sz.up_row, width), LOW),
+                ((2, 4, rows, cols), LOW),
+                ((2, sz.sequences * sz.heads, sz.length, sz.length), LOW),
+                ((rows, width), F32),
+                ((rows, width), LOW),
+                ((rows, width), LOW),
+                ((rows, width), F32),
+                ((rows, width), LOW),
+                ((rows, width), F32),
+                ((rows, width), F32),
+                ((rows, sz.units), LOW),
+                ((rows, cols), LOW),
+                ((rows, cols), LOW),
+                ((rows, cols), LOW),
+                ((rows, cols), LOW),
+                (mixed, LOW),
+                (mixed, LOW),
+                (local, LOW),
+                (result.shape, LOW),
+                ((3, 2, width, width), LOW),
+                ((3, heads, 4 * q, width), LOW),
+                ((blocks, 3, heads, 2 * q, width), LOW),
+                ((blocks, 3, heads, q, width), LOW),
+                ((blocks, 3, heads - 1, q, width), LOW),
+                ((blocks, 3, q, width), LOW),
+                ((SMALL_ROWS, width), F32),
+                ((3, SMALL_ROWS, width), F32),
+                ((heads - 1, SMALL_ROWS // 2, width), F32),
+                ((SMALL_ROWS, width), F32),
+            ]
+        )
+        + [
             pltpu.SemaphoreType.DMA((count,)),
             pltpu.SemaphoreType.DMA((count,)),
-            pltpu.SemaphoreType.DMA((n,)),
-            pltpu.SemaphoreType.DMA((n,)),
+            pltpu.SemaphoreType.DMA((6, 2 * (heads - 1))),
+            pltpu.SemaphoreType.DMA((10,)),
+            pltpu.SemaphoreType.DMA((24,)),
+            pltpu.SemaphoreType.DMA((kinds,)),
+            pltpu.SemaphoreType.REGULAR((3,)),
         ],
-        compiler_params=pltpu.CompilerParams(collective_id=1, has_side_effects=True, vmem_limit_bytes=60 * 2**20),
-    )(*grads)
-
-
-AXES = ("head", "tube", "clip")
+        compiler_params=pltpu.CompilerParams(
+            collective_id=1, has_side_effects=True, vmem_limit_bytes=63 * 2**20
+        ),
+    )(*fulls, *flat, cotangent, result, marks, gains)
 
 
 def fits_local(arrays, clip_size, tube_size, head_size):
@@ -1168,51 +1453,30 @@
         b_out[:, None],
         b_down[:, None],
     )
-    output = output.reshape(tube_share, frames, patches, width).transpose(1, 0, 2, 3)
-    output = lax.all_gather(output, "head", axis=1, tiled=True)[None]
-
-    def tubes_to_frames(array):
-        order = array.reshape(tube_share, heads, tube_size, frame_share, patches, width)
-        order = order.transpose(2, 1, 3, 0, 4, 5).reshape(frames, tube_share, patches, width)
-        return lax.all_to_all(order, ("tube", "head"), 0, 1, tiled=True).reshape(rows, width)
-
-    masked = mark_frames[..., :1].reshape(rows, 1) > 0.5
-    upstream = lax.dynamic_slice_in_dim(cotangent[0], head * tube_share, tube_share, 1)
-    upstream = upstream.transpose(1, 0, 2, 3).reshape(rows, width)
-    grad_second, grads_second, *small_second = run_backward(
-        sz, upstream, saved[1][0], norm_gains[1], full[1], saved[1][1:], "backward_second"
-    )
-    grad_first = tubes_to_frames(grad_second.astype(LOW))
-    grad_initial, grads_first, *small_first = run_backward(
-        sz, grad_first, saved[0][0], norm_gains[0], full[0], saved[0][1:], "backward_first"
-    )
-    grad_embed = jnp.sum(jnp.where(masked, grad_initial, 0.0), 0)
-    grad_tokens = jnp.where(masked, 0.0, grad_initial).astype(LOW)
-    grad_tokens = grad_tokens.reshape(frame_share, tube_size * tubes, patches, width)
-    grad_tokens = lax.all_to_all(grad_tokens, "tube", 1, 0, tiled=True)
-    grad_tokens = lax.all_gather(grad_tokens, "head", axis=0, tiled=True)[None]
-    small = [jnp.stack(two) for two in zip(small_first, small_second)]
-    small = lax.psum((grad_embed, *small), AXES)
-    embed_grad, gain_grad, shift_grad, bqv_grad, bout_grad, bup_grad, bdown_grad = small
-    bqv_grad = lax.dynamic_index_in_dim(bqv_grad, head, 1, False)
-    bup_grad = lax.dynamic_index_in_dim(bup_grad, head, 1, False).reshape(blocks, units)
-    whole = reduce_grads(heads, [grads_first, grads_second]).astype(F32)
+    output, grad_tokens, whole, small = run_backward(
+        sz, blocks, frame_share, tube_share, full, saved, cotangent[0], output, mark_frames, norm_gains
+    )
+    rows_of = lambda start, size: small[start : start + size]
+    bup_grad = rows_of(BUP_ROW, blocks * heads).reshape(blocks, heads, units)
+    bqv_grad = rows_of(BQV_ROW, 2 * blocks * heads)[:, :columns].reshape(blocks, heads, 2, columns)
+    of_head = lambda array: lax.dynamic_index_in_dim(array, head, 1, False)
+    whole = whole.astype(F32)
     whole = whole.reshape(blocks, sz.block_rows, width)
     qkv_grad = whole[:, : sz.out_row].reshape(blocks, 3, columns, width).transpose(0, 3, 1, 2)
     return (
-        output,
-        grad_tokens,
-        embed_grad,
-        gain_grad,
-        shift_grad,
+        output[None],
+        grad_tokens[None],
+        small[0],
+        rows_of(GAIN_ROW, 2 * blocks).reshape(blocks, 2, width),
+        rows_of(SHIFT_ROW, 2 * blocks).reshape(blocks, 2, width),
         qkv_grad,
-        bqv_grad,
+        of_head(bqv_grad),
         whole[:, sz.out_row : sz.up_row],
-        bout_grad[:, 0],
+        rows_of(BOUT_ROW, blocks),
         whole[:, sz.up_row : sz.down_row],
-        bup_grad,
+        of_head(bup_grad),
         whole[:, sz.down_row :],
-        bdown_grad[:, 0],
+        rows_of(BDOWN_ROW, blocks),
     )
 
 

time: 598 us -> 424 us (0.71)
  the two profiles are of different devices: /device:TPU:1 before, /device:TPU:9 now
where the time goes in v4:
time: 424 us; the launch traced here: 416 us
  Pallas kernels  385 us (91%)
  local copies, waits for them, and re-layouts  23 us (5%)
  other arithmetic  6.41 us (2%)
    pallas_call x1, Pallas kernels, run_backward(): pl.pallas_call(lambda *refs: backward_kernel(sz, blocks, frame_share, tub...  228 us
    pallas_call x1, Pallas kernels, run_forward(): pl.pallas_call(lambda *refs: forward_kernel(sz, blocks, frame_share, tube...  158 us

profile of v4, /device:TPU:9, one launch (start us, length us, event | category | flops | bytes accessed | tf_op | source)
XLA Modules:
  0.0 415.8 jit_solution(6089049414340313018)
XLA Ops:
  0.6 0.0 copy-start.2
  0.7 0.0 copy-start.4
  0.7 0.0 copy-start.5
  0.7 6.4 %pad_maximum_fusion = bf16[2,2304,768]{2,1,0:T(8,128)(2,1)} fusion(bf16[2,768,768]{2,1,0:T(8,128)(2,1)} %param.25, bf16[2,768,768]{2,1,0:T(8,128)(2,1)} %param.23, bf16[2,192,768]{2,1,0:T(8,128)(2,1)} %param.21, bf16[2,576,768]{2,1,0:T(8,128)(2,1)} %bitcast.29), kind=kLoop, calls=%fused_computation | loop fusion | flops 28311552 | bytes 14155776 | tf_op jit(solution)/shard_map/concatenate | solution.py:1436
  7.1 1.1 broadcast_in_dim.20.refs_2_
  8.2 0.6 broadcast_in_dim.22.refs_8_
  8.8 0.0 copy-done.5
  8.8 0.6 broadcast_in_dim.23.refs_9_
  9.4 0.6 reshape.60.refs_3_
  10.1 0.6 broadcast_in_dim.21.refs_5_
  10.6 157.6 %forward_both.1 = (bf16[4,2304,768]{2,1,0:T(8,128)(2,1)}, bf16[4,2304,768]{2,1,0:T(8,128)(2,1)}, f32[512,768]{1,0:T(8,128)}, bf16[512,768]{1,0:T(8,128)(2,1)}, b...) custom-call(bf16[4608,768]{1,0:T(8,128)(2,1)} %bitcast.23, ...), custom_call_target="tpu_custom_call" | custom-call | tf_op jit(solution)/shard_map/forward_both/pallas_call | solution.py:862
  168.2 227.9 %backward_both.1 = (bf16[16,8,16,768]{3,2,1,0:T(8,128)(2,1)}, bf16[16,8,16,768]{3,2,1,0:T(8,128)(2,1)}, bf16[4608,768]{1,0:T(8,128)(2,1)}, f32[48,768]{1,0:T(8,128)}) custom-call(bf16[4,2304,768]{2,1,0:T(8,128)(2,1)} %get-tuple-element.35.refs_0_, bf16[4,2304,768]{2,1,0:T(8,128)(2,1)} %get-tuple-element.36.refs_1_, f32[512,768]{1,0:T(8,128)} %get-tuple-element.37.refs_2_, ...), custom_call_target="tpu_custom_call" | custom-call | tf_op jit(solution)/shard_map/backward_both/pallas_call | solution.py:1332
  396.1 7.1 %fusion = (f32[2,768,768]{2,1,0:T(8,128)}, f32[2,768,768]{2,1,0:T(8,128)}) fusion(bf16[2,2304,768]{2,1,0:T(8,128)(2,1)} %bitcast.20), kind=kLoop, calls=%fused_computation.6 | loop fusion | bytes 18874368 | tf_op jit(solution)/shard_map/slice | solution.py:1478
  403.2 2.1 slice.46
  405.3 1.1 slice.47
  406.4 0.6 copy.29
  407.0 0.6 dynamic-slice_bitcast_fusion
  407.7 0.6 reshape.61
  408.3 0.6 reshape.62
  408.9 0.6 fusion.1
  409.5 0.6 slice_reduce_fusion
  410.1 3.8 copy.32
  413.9 0.0 copy-done.1
  413.9 1.7 copy.33
  (18 shorter events, 0.1 us)
Async XLA Ops:
  0.6 6.5 %copy-start.2 = (s32[1,16,8,16]{3,2,1,0:T(8,128)S(1)}, s32[1,16,8,16]{3,2,1,0:T(8,128)}, u32[]{:S(2)}) copy-start(s32[1,16,8,16]{3,2,1,0:T(8,128)} %param.15) | copy-start | bytes 24580
  0.7 7.6 %copy-start.4 = (f32[2,768]{1,0:T(2,128)S(1)}, f32[2,768]{1,0:T(2,128)}, u32[]{:S(2)}) copy-start(f32[2,768]{1,0:T(2,128)} %param.22) | copy-start | bytes 18436
  0.7 8.2 %copy-start.5 = (f32[2,768]{1,0:T(2,128)S(1)}, f32[2,768]{1,0:T(2,128)}, u32[]{:S(2)}) copy-start(f32[2,768]{1,0:T(2,128)} %param.26) | copy-start | bytes 18436
  0.7 8.8 %copy-start.7 = (f32[2,2,192]{2,1,0:T(2,128)S(1)}, f32[2,2,192]{2,1,0:T(2,128)}, u32[]{:S(2)}) copy-start(f32[2,2,192]{2,1,0:T(2,128)} %param.20) | copy-start | bytes 9220
  0.7 9.4 %copy-start.6 = (f32[768]{0:T(1024)S(1)}, f32[768]{0:T(1024)}, u32[]{:S(2)}) copy-start(f32[768]{0:T(1024)} %param.16) | copy-start | bytes 9220
  396.1 7.1 %copy-start = (bf16[4608,768]{1,0:T(8,128)(2,1)S(1)}, bf16[4608,768]{1,0:T(8,128)(2,1)}, u32[]{:S(2)}) copy-start(bf16[4608,768]{1,0:T(8,128)(2,1)} %get-tuple-element.56) | copy-start | bytes 21233668
  403.2 3.2 copy-start.3
  405.3 8.6 %copy-start.1 = (bf16[16,8,16,768]{3,2,1,0:T(8,128)(2,1)S(1)}, bf16[16,8,16,768]{3,2,1,0:T(8,128)(2,1)}, u32[]{:S(2)}) copy-start(bf16[16,8,16,768]{3,2,1,0:T(8,128)(2,1)} %get-tuple-element.54) | copy-start | bytes 9437188

commit v5 on v4

--- a/solution.py
+++ b/solution.py
@@ -1,3 +1,5 @@
+import functools
+
 import jax
 import jax.numpy as jnp
 from jax import lax
@@ -376,6 +378,43 @@
         bdown_grad,
     )
 
+
+DOWN, UP, ATTN = range(3)
+SEND, PASS, FIRST_INPUT, SECOND_INPUT, SPREAD, RESULT, ATTEND, MIDDLE, EXPAND, CONTRACT = range(10)
+FORWARD_ORDER = (
+    (SEND, 0), (PASS, 0, 0), (SEND, 1), (FIRST_INPUT,), (PASS, 0, 1), (PASS, 1, 0), (SEND, 2), (PASS, 1, 1),
+    (PASS, 0, 2), (PASS, 0, 3), (PASS, 1, 2), (PASS, 2, 0), (SEND, 3), (PASS, 1, 3), (ATTEND, 0, 0), (ATTEND, 0, 1),
+    (ATTEND, 0, 2), (PASS, 2, 1), (ATTEND, 0, 3), (MIDDLE, 0), (PASS, 3, 0), (SEND, 4), (PASS, 2, 2), (PASS, 3, 1),
+    (PASS, 2, 3), (EXPAND, 0, 0), (PASS, 4, 0), (SEND, 5), (EXPAND, 0, 1), (EXPAND, 0, 2), (EXPAND, 0, 3),
+    (PASS, 3, 2), (PASS, 4, 1), (PASS, 5, 0), (SEND, 6), (PASS, 3, 3), (CONTRACT, 0, 0), (CONTRACT, 0, 1),
+    (CONTRACT, 0, 2), (CONTRACT, 0, 3), (SPREAD,), (PASS, 5, 1), (PASS, 4, 2), (PASS, 4, 3), (PASS, 6, 0),
+    (SECOND_INPUT,), (ATTEND, 1, 0), (PASS, 6, 1), (PASS, 5, 2), (ATTEND, 1, 1), (ATTEND, 1, 2), (PASS, 5, 3),
+    (ATTEND, 1, 3), (MIDDLE, 1), (EXPAND, 1, 0), (PASS, 6, 2), (EXPAND, 1, 1), (EXPAND, 1, 2), (EXPAND, 1, 3),
+    (PASS, 6, 3), (CONTRACT, 1, 0), (CONTRACT, 1, 1), (CONTRACT, 1, 2), (CONTRACT, 1, 3), (RESULT,),
+)
+MLP_BACK, MLP_NORM, ATTN_BACK, ATTN_NORM, UPSTREAM, RESULT_LINE, OWN_LINE, FAR_START, FAR_LINE, SMALL = range(10)
+ADD_CORE, ADD_FIRST, ADD_SECOND, ADD_HEADS, SHARE_FIRST, SHARE_CORE, ARRIVED = range(10, 17)
+BACKWARD_ORDER = (
+    (MLP_BACK, 1, 0), (MLP_BACK, 1, 1), (ADD_CORE, 1, DOWN, 0), (ADD_CORE, 1, UP, 0), (MLP_BACK, 1, 2),
+    (ADD_CORE, 1, UP, 1), (ADD_CORE, 1, DOWN, 1), (MLP_BACK, 1, 3), (ADD_CORE, 1, DOWN, 2), (ADD_CORE, 1, UP, 2),
+    (MLP_NORM, 1), (RESULT_LINE, 0), (ATTN_BACK, 1, 0), (ATTN_BACK, 1, 1), (ADD_CORE, 1, DOWN, 3),
+    (ADD_CORE, 1, ATTN, 0), (ATTN_BACK, 1, 2), (ADD_CORE, 1, ATTN, 1), (ATTN_BACK, 1, 3), (ADD_CORE, 1, UP, 3),
+    (ATTN_NORM, 1), (RESULT_LINE, 1), (ADD_FIRST, 1, UP), (ADD_FIRST, 1, DOWN), (ADD_CORE, 1, ATTN, 3),
+    (ADD_SECOND, 1, UP), (ADD_CORE, 1, ATTN, 2), (UPSTREAM,), (MLP_BACK, 0, 0), (MLP_BACK, 0, 1),
+    (ADD_CORE, 0, DOWN, 0), (ADD_CORE, 0, UP, 0), (MLP_BACK, 0, 2), (ADD_SECOND, 1, DOWN), (ADD_CORE, 0, DOWN, 1),
+    (ADD_FIRST, 1, ATTN), (ADD_CORE, 0, UP, 1), (MLP_BACK, 0, 3), (MLP_NORM, 0), (ATTN_BACK, 0, 0), (ATTN_BACK, 0, 1),
+    (ADD_CORE, 0, ATTN, 0), (ADD_SECOND, 1, ATTN), (ATTN_BACK, 0, 2), (ADD_CORE, 0, ATTN, 1), (ATTN_BACK, 0, 3),
+    (ATTN_NORM, 0), (ADD_CORE, 0, DOWN, 2), (FAR_START,), (ADD_CORE, 0, DOWN, 3), (ADD_CORE, 0, UP, 3),
+    (ADD_HEADS, 1, ATTN), (ADD_CORE, 0, ATTN, 3), (OWN_LINE, 0), (FAR_LINE, 0), (ADD_CORE, 0, UP, 2),
+    (ADD_FIRST, 0, DOWN), (SHARE_FIRST, 1, ATTN), (ADD_SECOND, 0, DOWN), (ADD_FIRST, 0, UP), (ADD_CORE, 0, ATTN, 2),
+    (SHARE_CORE, 1, ATTN), (FAR_LINE, 1), (ADD_HEADS, 1, DOWN), (SMALL, 0), (ADD_HEADS, 1, UP), (ADD_FIRST, 0, ATTN),
+    (ADD_SECOND, 0, UP), (ADD_HEADS, 0, DOWN), (FAR_LINE, 2), (SHARE_FIRST, 1, UP), (SMALL, 1), (ADD_SECOND, 0, ATTN),
+    (SHARE_FIRST, 1, DOWN), (SMALL, 2), (SHARE_FIRST, 0, DOWN), (ADD_HEADS, 0, UP), (SHARE_FIRST, 0, UP),
+    (SHARE_CORE, 0, DOWN), (SHARE_CORE, 1, DOWN), (OWN_LINE, 1), (ADD_HEADS, 0, ATTN), (RESULT_LINE, 2),
+    (SHARE_CORE, 1, UP), (SHARE_FIRST, 0, ATTN), (SHARE_CORE, 0, UP), (ARRIVED, 0, DOWN), (ARRIVED, 1, ATTN),
+    (SMALL, 3), (SHARE_CORE, 0, ATTN), (ARRIVED, 0, UP), (ARRIVED, 0, ATTN), (ARRIVED, 1, UP), (ARRIVED, 1, DOWN),
+    (SMALL, 4), (OWN_LINE, 2),
+)
 
 GELU_A = 0.7978845608028654
 GELU_B = 0.044715
@@ -565,6 +604,7 @@
         self.other = (1 - c + 2 * x, y, self.z)
         self.i = (1 - c) * x + c * y
         self.j = (1 - c) * y + c * x
+        self.along_x = (c + 2 * (1 - x), y, self.z)
 
     def head(self, step):
         return (self.clip, self.y, lax.rem(self.z + step + self.heads, self.heads))
@@ -572,17 +612,11 @@
     def across(self, step):
         return (self.clip, 1 - self.y, lax.rem(self.z + step + self.heads, self.heads))
 
-    def peers(self):
-        return [self.first, self.second, self.other] + [self.head(d) for d in range(1, self.heads)]
-
     def clip_peers(self):
         return [self.head(d) for d in range(1, self.heads)] + [self.across(d) for d in range(self.heads)]
 
     def all_peers(self):
-        return [
-            (self.first[0] * (1 - self.core) + self.second[0] * self.core, self.y, self.z),
-            self.other,
-        ] + self.clip_peers()
+        return [self.along_x, self.other] + self.clip_peers()
 
 
 def greet(peers):
@@ -629,10 +663,17 @@
         self.sent = {}
 
 
-PIECES = 3
-
-
-def gather_phases(place, moves, shard, full, base, offset, rows):
+def piece_list(sz, blocks):
+    out = []
+    for b in range(blocks):
+        for kind, start in ((ATTN, 0), (UP, sz.up_row), (DOWN, sz.down_row)):
+            parts = 2 if (b, kind) == (0, ATTN) else 1
+            size = sz.width // parts
+            out += [(b, kind, start + i * size, size) for i in range(parts)]
+    return out
+
+
+def gather_phases(place, moves, full, offset, rows):
     q = rows // 8
     c, i, j, z, heads = place.core, place.i, place.j, place.z, place.heads
 
@@ -646,11 +687,10 @@
     near = 4 * c + 2 * j + (1 - i)
     pair = 4 * c + 2 * j
     pair_far = 4 * c + 2 * (1 - j)
-    src = shard.at[pl.ds(pl.multiple_of(base + offset + mine * q, q), q), :]
     steps = range(1, heads)
     return [
         moves.phase(
-            [(src, at(full, z, mine, 1), at(full, lax.rem(z + heads - d, heads), mine, 1), place.head(d)) for d in steps]
+            [(at(full, z, mine, 1), at(full, z, mine, 1), at(full, lax.rem(z + heads - d, heads), mine, 1), place.head(d)) for d in steps]
         ),
         moves.phase(
             [(at(full, other(d), mine, 1), at(full, other(d), mine, 1), at(full, other(d), near, 1), place.first) for d in steps]
@@ -676,7 +716,7 @@
 
 
 def forward_kernel(sz, blocks, frame_share, tube_share, *refs):
-    (shard, tokens, marks, b_qv, b_up, embed, gains, shifts, b_out, b_down), refs = refs[:10], refs[10:]
+    (w_qkv, w_out, w_up, w_down, tokens, marks, b_qv, b_up, embed, gains, shifts, b_out, b_down), refs = refs[:13], refs[13:]
     fulls, refs = refs[:blocks], refs[blocks:]
     saved, refs = [refs[7 * b : 7 * b + 7] for b in range(blocks)], refs[7 * blocks :]
     (result, frame_marks), refs = refs[:2], refs[2:]
@@ -688,7 +728,11 @@
     place = Place(heads)
     moves = Moves(send_sem, recv_sem)
     local, saves = Saves(local_sem), Saves(save_sem)
-    rows = block_rows // PIECES
+
+    def settle(copies):
+        for copy in copies:
+            copy.wait()
+
     yy, z = place.y, place.z
     tubes = tokens.shape[1]
     greet(place.all_peers())
@@ -723,19 +767,29 @@
             ]
         ]
     )
-    work = [
-        gather_phases(place, moves, shard, w[b], b * block_rows, i * rows, rows)
-        for b in range(blocks)
-        for i in range(PIECES)
-    ]
+    pieces = piece_list(sz, blocks)
+    work = [gather_phases(place, moves, w[b], start, size) for b, _, start, size in pieces]
     moves.start(exchange)
-    moves.start(work[0][0])
+    own_parts = {}
+    for b in range(blocks):
+        mine = w[b].at[z]
+        own_parts[b, ATTN] = [
+            local.start(w_qkv.at[b], mine.at[pl.ds(0, sz.out_row)]),
+            local.start(w_out.at[b], mine.at[pl.ds(sz.out_row, sz.columns)]),
+        ]
+        own_parts[b, UP] = [local.start(w_up.at[b], mine.at[pl.ds(sz.up_row, sz.width)])]
+        own_parts[b, DOWN] = [local.start(w_down.at[b], mine.at[pl.ds(sz.down_row, sz.units)])]
+
+    def begin_piece(piece):
+        b, kind, _, _ = pieces[piece]
+        settle(own_parts.pop((b, kind), ()))
+        moves.start(work[piece][0])
     owns = [
         local.start(tokens.at[owned], frames.at[:, here]),
         local.start(marks.at[owned], frame_marks.at[:, here]),
         local.start(b_qv, bqv.at[z]),
         local.start(b_up, bup.at[z]),
-    ] + [local.start(shard.at[pl.ds(b * block_rows, block_rows), :], w[b].at[z]) for b in range(blocks)]
+    ]
 
     def save(b, index, src, part=None):
         dst = saved[b][index]
@@ -743,127 +797,104 @@
 
     def begin_block(b):
         norm_rows(sz, x, gains[b, 0:1, :], shifts[b, 0:1, :], n)
-        m[...] = x[...] + b_out[b]
+        m[...] = x[...] + b_out[b : b + 1, :]
         return [save(b, 0, x), save(b, 1, n)]
 
-    def attention(b, low, high):
-        @pl.loop(low, high)
-        def _(s):
-            forward_attention(sz, s, w[b], bqv[s, 2 * b : 2 * b + 1, :], bqv[s, 2 * b + 1 : 2 * b + 2, :], n, t, p, m)
-
-        at = pl.ds(low, high - low)
-        return [save(b, 2, t.at[at], at), save(b, 3, p.at[at], at)]
+    def attention(b, s):
+        forward_attention(sz, s, w[b], bqv[s, b, 0:1, :], bqv[s, b, 1:2, :], n, t, p, m)
+        return [save(b, 2, t.at[s], s), save(b, 3, p.at[s], s)]
 
     def middle(b):
         norm_rows(sz, m, gains[b, 1:2, :], shifts[b, 1:2, :], n2)
-        y[...] = m[...] + b_down[b]
+        y[...] = m[...] + b_down[b : b + 1, :]
         return [save(b, 4, m), save(b, 5, n2)]
 
-    def up(b, low, high):
-        @pl.loop(low, high)
-        def _(s):
-            forward_up(sz, s, w[b], bup[s, b : b + 1, :], n2, act)
-
-        at = pl.ds(low, high - low)
-        return [save(b, 6, act.at[at], at)]
-
-    def down(b):
-        @pl.loop(0, heads)
-        def _(s):
-            forward_down(sz, s, w[b], act, y)
+    def up(b, s):
+        forward_up(sz, s, w[b], bup[s, b : b + 1, :], n2, act)
+        return [save(b, 6, act.at[s], s)]
+
+    def down(b, s):
+        forward_down(sz, s, w[b], act, y)
 
     def keep(piece):
-        b, i = piece // PIECES, piece % PIECES
-        at = pl.ds(i * rows, rows)
+        b, _, start, size = pieces[piece]
+        at = pl.ds(start, size)
         return [saves.start(w[b].at[:, at], fulls[b].at[:, at])]
 
-    def arrived(piece):
-        moves.arrive(work[piece][3])
-        return keep(piece)
-
-    def settle(copies):
-        for copy in copies:
-            copy.wait()
-
-    half = heads // 2
-    kept = []
-    early = []
-    for tick in range(6):
-        moves.arrive(work[tick][0])
-        if tick + 1 < 6:
-            moves.start(work[tick + 1][0])
-        moves.start(work[tick][1])
-        if tick:
-            moves.arrive(work[tick - 1][2])
-            moves.start(work[tick - 1][3])
-        if tick == 0:
-            settle(owns)
-            moves.arrive(exchange)
-            tok = frames[...].astype(F32).reshape(sz.rows, sz.width)
-            mark = frame_marks[...].astype(F32).reshape(sz.rows, 128)[:, 0:1]
-            x[...] = jnp.where(mark > 0.5, embed[...], tok)
-            early += begin_block(0)
-        if tick == 2:
-            kept += arrived(0)
-            early += attention(0, 0, half)
-        if tick == 3:
-            kept += arrived(1)
-            early += middle(0)
-            early += up(0, 0, half)
-        if tick == 4:
-            kept += arrived(2)
-            down(0)
-            y_low[...] = y[...].astype(LOW).reshape(y_low.shape)
-            moves.start(spread)
-            mine = local.start(
-                y_low.at[:, pl.ds((heads * yy + z) * tube_share, tube_share)],
-                second.at[pl.ds((2 * z + yy) * frame_share, frame_share)],
-            )
-        if tick == 5:
-            kept += arrived(3)
-            kept += attention(1, 0, half)
-        moves.arrive(work[tick][1])
-        moves.start(work[tick][2])
-        if tick == 2:
-            early += attention(0, half, heads)
-        if tick == 3:
-            early += up(0, half, heads)
-        if tick == 4:
-            moves.arrive(spread)
-            mine.wait()
-            settle(early)
-            for j in range(tube_share):
-                x[j * length : (j + 1) * length, :] = second[:, j].astype(F32).reshape(length, sz.width)
-            kept += begin_block(1)
-        if tick == 5:
-            kept += attention(1, half, heads)
-    kept += middle(1)
-    kept += arrived(4)
-    kept += up(1, 0, heads)
-    moves.arrive(work[5][2])
-    moves.start(work[5][3])
-    kept += arrived(5)
-    down(1)
+    kept, early = [], []
+    wide = [None] * blocks
+
+    def first_input():
+        settle(owns)
+        moves.arrive(exchange)
+        tok = frames[...].astype(F32).reshape(sz.rows, sz.width)
+        mark = frame_marks[...].astype(F32).reshape(sz.rows, 128)[:, 0:1]
+        x[...] = jnp.where(mark > 0.5, embed[...].reshape(1, sz.width), tok)
+        early.extend(begin_block(0))
+
+    def second_input():
+        moves.arrive(spread)
+        wide[1].wait()
+        settle(early)
+        for j in range(tube_share):
+            x[j * length : (j + 1) * length, :] = second[:, j].astype(F32).reshape(length, sz.width)
+        kept.extend(begin_block(1))
+
+    def spread_first():
+        y_low[...] = y[...].astype(LOW).reshape(y_low.shape)
+        moves.start(spread)
+        wide[1] = local.start(
+            y_low.at[:, pl.ds((heads * yy + z) * tube_share, tube_share)],
+            second.at[pl.ds((2 * z + yy) * frame_share, frame_share)],
+        )
+
+    def finish_second():
+        for j in range(tube_share):
+            at = slice(j * length, (j + 1) * length)
+            second[:, j] = y[at, :].astype(LOW).reshape(second.shape[0], second.shape[2], sz.width)
+        kept.append(saves.start(second, result))
+
+    def advance(piece, phase):
+        moves.arrive(work[piece][phase])
+        if phase < 3:
+            moves.start(work[piece][phase + 1])
+        else:
+            kept.extend(keep(piece))
+
+    steps = {(FIRST_INPUT,): first_input, (SPREAD,): spread_first, (SECOND_INPUT,): second_input, (RESULT,): finish_second}
+    for piece in range(len(work)):
+        steps[SEND, piece] = functools.partial(begin_piece, piece)
+        for phase in range(4):
+            steps[PASS, piece, phase] = functools.partial(advance, piece, phase)
+    for b in range(blocks):
+        held = kept if b else early
+        run = lambda f, *args, held=held: held.extend(f(*args) or ())
+        steps[MIDDLE, b] = functools.partial(run, middle, b)
+        for s in range(heads):
+            steps[ATTEND, b, s] = functools.partial(run, attention, b, s)
+            steps[EXPAND, b, s] = functools.partial(run, up, b, s)
+            steps[CONTRACT, b, s] = functools.partial(run, down, b, s)
+    for step in FORWARD_ORDER:
+        steps[step]()
     moves.finish()
-    y_low[...] = y[...].astype(LOW).reshape(y_low.shape)
-    kept.append(saves.start(y_low, result))
     settle(kept)
 
 
-def run_forward(sz, blocks, frame_share, tube_share, shard, tokens, marks, b_qv, b_up, embed, gains, shifts, b_out, b_down):
+def run_forward(sz, blocks, frame_share, tube_share, weights, tokens, marks, b_qv, b_up, embed, gains, shifts, b_out, b_down):
     heads, width, rows = sz.shards, sz.width, sz.rows
     tubes, patches = 2 * tokens.shape[1], tokens.shape[2]
     frames = tokens.shape[0]
     saved = [((rows, width), F32)] + saved_shapes(sz)
     whole_frames = (frame_share, tubes, patches)
-    count = blocks * PIECES * 4 * (heads - 1) + 2 + 2 * (heads - 1) + 2 * heads - 1
+    count = len(piece_list(sz, blocks)) * 4 * (heads - 1) + 2 + 2 * (heads - 1) + 2 * heads - 1
     hbm, vmem = pl.BlockSpec(memory_space=pl.ANY), pl.BlockSpec(memory_space=pltpu.VMEM)
     full = ((heads, sz.block_rows, width), LOW)
+    mixed = (frames, tube_share, patches, width)
     out = pl.pallas_call(
         lambda *refs: forward_kernel(sz, blocks, frame_share, tube_share, *refs),
         name="forward_both",
-        out_shape=structs([full] * blocks + saved * blocks + [(whole_frames + (width,), LOW), (whole_frames + (128,), LOW)]),
-        in_specs=[hbm] * 5 + [vmem] * 5,
+        out_shape=structs([full] * blocks + saved * blocks + [(mixed, LOW), (whole_frames + (128,), LOW)]),
+        in_specs=[hbm] * 8 + [vmem] * 5,
         out_specs=[hbm] * (blocks + 7 * blocks + 1) + [vmem],
         scratch_shapes=vmems(
             [full] * blocks
@@ -876,27 +907,28 @@
             + [
                 ((rows, width), F32),
                 (whole_frames + (width,), LOW),
-                ((frames, tube_share, patches, width), LOW),
+                (mixed, LOW),
             ]
         )
         + [
             pltpu.SemaphoreType.DMA((count,)),
             pltpu.SemaphoreType.DMA((count,)),
-            pltpu.SemaphoreType.DMA((8,)),
-            pltpu.SemaphoreType.DMA((32,)),
+            pltpu.SemaphoreType.DMA((16,)),
+            pltpu.SemaphoreType.DMA((64,)),
         ],
         compiler_params=pltpu.CompilerParams(
             collective_id=0, has_side_effects=True, vmem_limit_bytes=62 * 2**20
         ),
-    )(shard, tokens, marks, b_qv, b_up, embed, gains, shifts, b_out, b_down)
+    )(*weights, tokens, marks, b_qv, b_up, embed, gains, shifts, b_out, b_down)
     fulls, out = out[:blocks], out[blocks:]
     saved = [out[7 * b : 7 * b + 7] for b in range(blocks)]
     return fulls, saved, out[-2], out[-1]
 
 
 class Line:
-    def __init__(self, place, send_sem, recv_sem, region):
+    def __init__(self, place, send_sem, recv_sem, region, own=None):
         self.place, self.send_sem, self.recv_sem, self.region = place, send_sem, recv_sem, region
+        self.own = own
         self.steps = place.heads - 1
 
     def moves(self, step):
@@ -908,7 +940,7 @@
 
     def copy(self, block, way, n):
         return pltpu.make_async_remote_copy(
-            self.region(block),
+            self.own if n < 2 and self.own is not None else self.region(block),
             self.region(block),
             self.send_sem.at[n],
             self.recv_sem.at[n],
@@ -946,13 +978,10 @@
             [(grads.at[s % 2, self.given, :], self.core_buf.at[s], self.core_buf.at[s], place.other) for s in shards]
         )
         self.first = moves.phase(
-            [
-                (self.core_buf.at[s, cut(2 * (1 - i), 2), :], self.first_buf.at[s], self.first_buf.at[s], place.first)
-                for s in shards
-            ]
+            [(self.core_buf.at[s, cut(2 * (1 - i), 2), :], self.first_buf.at[s], self.first_buf.at[s], place.first) for s in shards]
         )
         self.second = moves.phase(
-            [(self.first_buf.at[:, cut(1 - j, 1), :], self.second_buf, self.second_buf, place.second)]
+            [(self.first_buf.at[s, cut(1 - j, 1), :], self.second_buf.at[s], self.second_buf.at[s], place.second) for s in shards]
         )
         self.heads = moves.phase(
             [
@@ -961,10 +990,10 @@
             ]
         )
         a, mine = 4 * c, 2 * i + j
-        self.share_second = moves.phase([(row(a + mine, 1), row(a + mine, 1), row(a + 2 * i + 1 - j, 1), place.second)])
+        self.share_second = moves.phase([(final_buf, row(a + mine, 1), row(a + 2 * i + 1 - j, 1), place.second)])
         self.share_first = moves.phase([(row(a + 2 * i, 2), row(a + 2 * i, 2), row(a + 2 * (1 - i), 2), place.first)])
         self.share_core = moves.phase([(row(a, 4), row(a, 4), row(4 - a, 4), place.other)])
-        self.final_row = row(a + mine, 1)
+        self.keep = pltpu.make_async_copy(final_buf, row(a + mine, 1), final_sem)
 
     def give(self, s):
         self.moves.start([self.core[s]])
@@ -975,24 +1004,18 @@
         self.moves.start([self.first[s]])
 
     def step_second(self, free_sem=None):
-        self.moves.arrive(self.first)
-
-        @pl.loop(0, self.place.heads)
-        def _(s):
+        for s in range(self.place.heads):
+            self.moves.arrive([self.first[s]])
             self.first_buf[s] = self.first_buf[s] + self.core_buf[s, self.part, :]
-
-        self.moves.start(self.second)
+            self.moves.start([self.second[s]])
         if free_sem is not None:
             self.moves.left(self.first)
             pl.semaphore_signal(free_sem, inc=1, device_id=self.place.other, device_id_type=MESH)
 
     def step_heads(self):
-        self.moves.arrive(self.second)
-
-        @pl.loop(0, self.place.heads)
-        def _(s):
+        for s in range(self.place.heads):
+            self.moves.arrive([self.second[s]])
             self.second_buf[s] = self.second_buf[s] + self.first_buf[s, self.subpart, :]
-
         self.moves.start(self.heads)
 
     def step_share(self):
@@ -1001,12 +1024,11 @@
         for d in range(self.place.heads - 1):
             total += self.head_buf[d].astype(F32)
         self.final_buf[...] = total.astype(LOW)
-        copy = pltpu.make_async_copy(self.final_buf, self.final_row, self.final_sem)
-        copy.start()
-        copy.wait()
+        self.keep.start()
         self.moves.start(self.share_second)
 
     def step_share_first(self):
+        self.keep.wait()
         self.moves.arrive(self.share_second)
         self.moves.start(self.share_first)
 
@@ -1020,7 +1042,6 @@
 
 SMALL_ROWS = 48
 GAIN_ROW, SHIFT_ROW, BOUT_ROW, BDOWN_ROW, BUP_ROW, BQV_ROW = 1, 5, 9, 11, 16, 24
-DOWN, UP, ATTN = 0, 1, 2
 
 
 def backward_kernel(sz, blocks, frame_share, tube_share, *refs):
@@ -1029,7 +1050,7 @@
     (cotangent, result, marks, gains), refs = refs[:4], refs[4:]
     (out_result, out_tokens, out_grads, out_small), refs = refs[:4], refs[4:]
     (
-        wm, act, wa, t, p, m, n2, n, x, low, dn, dm, du, do, dq, dk, dv, cot, dx_low, back, res,
+        wm, act, wa, t, p, m, n2, n, x, low, dn, dm, du, do, dq, dk, dv, cot, dx_low, back,
         grads, core_buf, first_buf, second_buf, head_buf, final_buf, small, small_in, small_heads, small_last,
         send_sem, recv_sem, line_sem, load_sem, copy_sem, final_sem, free_sem,
     ) = refs
@@ -1042,7 +1063,7 @@
 
     def step_loads(b, kind, s):
         slot = s % 2
-        if kind == "mlp":
+        if kind == MLP_BACK:
             pairs = [(fulls[b].at[s, pl.ds(sz.up_row, 2 * width), :], wm.at[slot]), (saved[b][6].at[s], act.at[slot])]
             base = 0
         else:
@@ -1056,7 +1077,7 @@
             pltpu.make_async_copy(src, dst, load_sem.at[base + slot * len(pairs) + i]) for i, (src, dst) in enumerate(pairs)
         ]
 
-    steps = [(b, kind, s) for b in (1, 0) for kind in ("mlp", "attn") for s in range(heads)]
+    steps = [(b, kind, s) for b in (1, 0) for kind in (MLP_BACK, ATTN_BACK) for s in range(heads)]
 
     def fetch(i):
         if i < len(steps):
@@ -1068,13 +1089,10 @@
             copy.wait()
         fetch(i + 1)
 
-    first_loads = [
-        loads.start(cotangent.at[:, pl.ds(z * tube_share, tube_share)], cot),
-        loads.start(result, res),
-    ]
+    first_load = loads.start(cotangent.at[:, pl.ds(z * tube_share, tube_share)], cot)
     fetch(0)
-    norm_loads = [loads.start(saved[1][4], m), loads.start(saved[1][5], n2)]
-    later_loads = [loads.start(saved[1][1], n), loads.start(saved[1][0], x)]
+    norm_loads = {1: [loads.start(saved[1][4], m), loads.start(saved[1][5], n2)]}
+    later_loads = {1: [loads.start(saved[1][1], n), loads.start(saved[1][0], x)]}
     small[...] = jnp.zeros_like(small)
     greet(place.all_peers())
 
@@ -1094,7 +1112,7 @@
                 final_sem.at[b * 3 + k],
             )
     tube_region = lambda block: out_result.at[:, pl.ds(block * tube_share, tube_share)]
-    line = Line(place, line_sem.at[0], line_sem.at[1], tube_region)
+    line = Line(place, line_sem.at[0], line_sem.at[1], tube_region, result)
     spread = moves.phase(
         [
             (
@@ -1112,141 +1130,111 @@
         ]
     )
 
-    for copy in first_loads:
-        copy.wait()
-    own_result = [
-        loads.start(res.at[j], out_result.at[:, z * tube_share + j]) for j in range(tube_share)
-    ]
+    line.start(0)
+    first_load.wait()
     frames = cot.shape[0]
     for j in range(tube_share):
         low[j * length : (j + 1) * length, :] = cot[:, j].reshape(length, width)
-    for copy in own_result:
-        copy.wait()
-    line.start(0)
+    own_result = loads.start(result, tube_region(z))
 
     def row(r, columns=None):
         return small.at[r : r + 1, :] if columns is None else small.at[r : r + 1, 0:columns]
 
-    def mlp(b, pumps):
-        row(BDOWN_ROW + b)[...] = jnp.sum(low[...].astype(F32), 0, keepdims=True)
-        dn[...] = jnp.zeros_like(dn)
-        for copy in norm_loads:
-            copy.wait()
-        for s in range(heads):
-            ready((1 - b) * 2 * heads + s)
-            for k in (DOWN, UP):
-                if s >= 2:
-                    moves.left([red[b, k].core[s - 2]])
-                elif b == 0:
-                    moves.left([red[1, k].core[s + heads - 2]])
-            backward_mlp(
-                sz, wm.at[s % 2], act.at[s % 2], low, n2, du, dn, grads.at[DOWN, s % 2], grads.at[UP, s % 2],
-                row(BUP_ROW + b * heads + s),
-            )
-            for k in (DOWN, UP):
-                if s == 0 and b == 0:
-                    pl.semaphore_wait(free_sem.at[k], 1)
-                red[b, k].give(s)
-            if s:
-                for k in (DOWN, UP):
-                    red[b, k].step_first(s - 1)
-            pumps[s]()
+    def mlp(b, s):
+        if s == 0:
+            row(BDOWN_ROW + b)[...] = jnp.sum(low[...].astype(F32), 0, keepdims=True)
+            dn[...] = jnp.zeros_like(dn)
+            for copy in norm_loads[b]:
+                copy.wait()
+        ready((1 - b) * 2 * heads + s)
+        for k in (DOWN, UP):
+            if s >= 2:
+                moves.left([red[b, k].core[s - 2]])
+            elif b == 0:
+                moves.left([red[1, k].core[s + heads - 2]])
+        backward_mlp(
+            sz, wm.at[s % 2], act.at[s % 2], low, n2, du, dn, grads.at[DOWN, s % 2], grads.at[UP, s % 2],
+            row(BUP_ROW + b * heads + s),
+        )
+        for k in (DOWN, UP):
+            if s == 0 and b == 0:
+                pl.semaphore_wait(free_sem.at[k], 1)
+            red[b, k].give(s)
+
+    def mlp_norm(b):
         norm_back_rows(
             sz, m, gains[b, 1:2, :], dn, low, dm, row(GAIN_ROW + 2 * b + 1), row(SHIFT_ROW + 2 * b + 1), row(BOUT_ROW + b), low
         )
-        for k in (DOWN, UP):
-            red[b, k].step_first(heads - 1)
-
-    def attention(b, pumps):
-        dn[...] = jnp.zeros_like(dn)
-        for copy in later_loads:
-            copy.wait()
-        for s in range(heads):
-            ready((1 - b) * 2 * heads + heads + s)
-            if s >= 2:
-                moves.left([red[b, ATTN].core[s - 2]])
-            elif b == 0:
-                moves.left([red[1, ATTN].core[s + heads - 2]])
-            r = BQV_ROW + 2 * (b * heads + s)
-            backward_attention(
-                sz, wa.at[s % 2], t.at[s % 2], p.at[s % 2], low, n, do, dq, dk, dv, dn, grads.at[ATTN, s % 2],
-                row(r, sz.columns), row(r + 1, sz.columns),
-            )
-            if s == 0 and b == 0:
-                pl.semaphore_wait(free_sem.at[ATTN], 1)
-            red[b, ATTN].give(s)
-            if s:
-                red[b, ATTN].step_first(s - 1)
-            pumps[s]()
+        if b:
+            norm_loads[0] = [loads.start(saved[0][4], m), loads.start(saved[0][5], n2)]
+
+    def attention(b, s):
+        if s == 0:
+            dn[...] = jnp.zeros_like(dn)
+            for copy in later_loads[b]:
+                copy.wait()
+        ready((1 - b) * 2 * heads + heads + s)
+        if s >= 2:
+            moves.left([red[b, ATTN].core[s - 2]])
+        elif b == 0:
+            moves.left([red[1, ATTN].core[s + heads - 2]])
+        r = BQV_ROW + 2 * (b * heads + s)
+        backward_attention(
+            sz, wa.at[s % 2], t.at[s % 2], p.at[s % 2], low, n, do, dq, dk, dv, dn, grads.at[ATTN, s % 2],
+            row(r, sz.columns), row(r + 1, sz.columns),
+        )
+        if s == 0 and b == 0:
+            pl.semaphore_wait(free_sem.at[ATTN], 1)
+        red[b, ATTN].give(s)
+
+    own_spread = []
+
+    def attention_norm(b):
         norm_back_rows(
             sz, x, gains[b, 0:1, :], dn, dm, dm, row(GAIN_ROW + 2 * b), row(SHIFT_ROW + 2 * b), None, None
         )
-
-    def nothing():
-        pass
-
-    def pass_on(step):
-        line.arrive(step)
-        if step + 1 < line.steps:
-            line.start(step + 1)
-
-    def do_all(*actions):
-        def run():
-            for action in actions:
-                action()
-
-        return run
-
-    one = {k: red[1, k] for k in (DOWN, UP, ATTN)}
-    nought = {k: red[0, k] for k in (DOWN, UP, ATTN)}
-
-    mlp(1, [nothing] * heads)
-    norm_loads = [loads.start(saved[0][4], m), loads.start(saved[0][5], n2)]
-    attention(1, [nothing, lambda: pass_on(0), nothing, nothing])
-    later_loads = [loads.start(saved[0][1], n), loads.start(saved[0][0], x)]
-    for j in range(tube_share):
-        dx_low[:, j] = dm[j * length : (j + 1) * length, :].astype(LOW).reshape(frames, length // frames, width)
-    moves.start(spread)
-    mine = loads.start(
-        dx_low.at[pl.ds((2 * z + yy) * frame_share, frame_share)],
-        back.at[:, pl.ds((heads * yy + z) * tube_share, tube_share)],
-    )
-    one[ATTN].step_first(heads - 1)
-    one[DOWN].step_second(free_sem.at[DOWN])
-    one[UP].step_second(free_sem.at[UP])
-    moves.arrive(spread)
-    mine.wait()
-    low[...] = back[...].reshape(sz.rows, width)
-    mlp(
-        0,
-        [
-            lambda: one[DOWN].step_heads(),
-            do_all(lambda: one[ATTN].step_second(free_sem.at[ATTN]), lambda: pass_on(1)),
-            lambda: one[UP].step_heads(),
-            lambda: one[DOWN].step_share(),
-        ],
-    )
-    attention(
-        0,
-        [
-            do_all(lambda: one[ATTN].step_heads(), lambda: one[DOWN].step_share_first()),
-            do_all(lambda: one[UP].step_share(), lambda: one[DOWN].step_share_core()),
-            do_all(lambda: pass_on(2), lambda: one[UP].step_share_first()),
-            do_all(lambda: one[ATTN].step_share(), lambda: one[UP].step_share_core()),
-        ],
-    )
-    mark = marks[...].astype(F32).reshape(sz.rows, 128)[:, 0:1] > 0.5
-    grad = dm[...]
-    row(0)[...] = jnp.sum(jnp.where(mark, grad, 0.0), 0, keepdims=True)
-    back[...] = jnp.where(mark, 0.0, grad).astype(LOW).reshape(back.shape)
+        if b:
+            later_loads[0] = [loads.start(saved[0][1], n), loads.start(saved[0][0], x)]
+            for j in range(tube_share):
+                dx_low[:, j] = dm[j * length : (j + 1) * length, :].astype(LOW).reshape(frames, length // frames, width)
+            moves.start(spread)
+            own_spread.append(
+                loads.start(
+                    dx_low.at[pl.ds((2 * z + yy) * frame_share, frame_share)],
+                    back.at[:, pl.ds((heads * yy + z) * tube_share, tube_share)],
+                )
+            )
+            return
+        mark = marks[...].astype(F32).reshape(sz.rows, 128)[:, 0:1] > 0.5
+        grad = dm[...]
+        row(0)[...] = jnp.sum(jnp.where(mark, grad, 0.0), 0, keepdims=True)
+        back[...] = jnp.where(mark, 0.0, grad).astype(LOW).reshape(back.shape)
+        moves.start(cross)
+        own_copy = loads.start(back.at[:, here], own_frames(z))
+        moves.start(small_steps[0])
+        own_copy.wait()
+        own_line.start(0)
+
+    def second_upstream():
+        moves.arrive(spread)
+        for copy in own_spread:
+            copy.wait()
+        low[...] = back[...].reshape(sz.rows, width)
+
     here, there = pl.ds(yy * tubes, tubes), pl.ds((1 - yy) * tubes, tubes)
     own_frames = lambda block: out_tokens.at[pl.ds((2 * block + yy) * frame_share, frame_share)]
     far_frames = lambda block: out_tokens.at[pl.ds((2 * block + 1 - yy) * frame_share, frame_share)]
     cross = moves.phase([(back.at[:, there], own_frames(z), far_frames(z), place.across(0))])
     own_line = Line(place, line_sem.at[2], line_sem.at[3], own_frames)
     far_line = Line(place, line_sem.at[4], line_sem.at[5], far_frames)
+
+    def start_far():
+        moves.arrive(cross)
+        far_line.start(0)
+
     half = SMALL_ROWS // 2
     part = pl.ds(pl.multiple_of(place.core * half, half), half)
+    far_part = pl.ds(pl.multiple_of((1 - place.core) * half, half), half)
     small_steps = [
         moves.phase([(small, small_in.at[i], small_in.at[i], target)])
         for i, target in enumerate((place.other, place.first, place.second))
@@ -1254,7 +1242,6 @@
     small_z = moves.phase(
         [(small.at[part], small_heads.at[d - 1], small_heads.at[d - 1], place.head(d)) for d in range(1, heads)]
     )
-    far_part = pl.ds(pl.multiple_of((1 - place.core) * half, half), half)
     small_end = moves.phase([(small_last.at[part], small_last.at[part], small_last.at[far_part], place.other)])
 
     def add_small(i):
@@ -1263,57 +1250,48 @@
         small[...] += small_in[i]
         moves.start(small_steps[i + 1] if i + 1 < len(small_steps) else small_z)
 
-    moves.start(cross)
-    own_copy = loads.start(back.at[:, here], own_frames(z))
-    moves.start(small_steps[0])
-    nought[ATTN].step_first(heads - 1)
-    own_copy.wait()
-    own_line.start(0)
-    nought[DOWN].step_second()
-    add_small(0)
-    nought[UP].step_second()
-    moves.arrive(cross)
-    far_line.start(0)
-    add_small(1)
-    nought[DOWN].step_heads()
-    nought[ATTN].step_second()
-    add_small(2)
-    one[ATTN].step_share_first()
-    own_line.arrive(0)
-    own_line.start(1)
-    nought[UP].step_heads()
-    one[UP].end()
-    one[DOWN].end()
-    nought[DOWN].step_share()
-    far_line.arrive(0)
-    far_line.start(1)
-    nought[ATTN].step_heads()
-    one[ATTN].step_share_core()
-    nought[UP].step_share()
-    nought[DOWN].step_share_first()
-    own_line.arrive(1)
-    own_line.start(2)
-    moves.arrive(small_z)
-    total = small[part, :]
-    for d in range(heads - 1):
-        total += small_heads[d]
-    small_last[part, :] = total
-    moves.start(small_end)
-    nought[DOWN].step_share_core()
-    nought[UP].step_share_first()
-    nought[ATTN].step_share()
-    far_line.arrive(1)
-    far_line.start(2)
-    nought[UP].step_share_core()
-    nought[ATTN].step_share_first()
-    moves.arrive(small_end)
-    out_small[...] = small_last[...]
-    nought[ATTN].step_share_core()
-    own_line.arrive(2)
-    far_line.arrive(2)
-    one[ATTN].end()
-    for k in (DOWN, UP, ATTN):
-        nought[k].end()
+    def add_small_heads():
+        moves.arrive(small_z)
+        total = small[part, :]
+        for d in range(heads - 1):
+            total += small_heads[d]
+        small_last[part, :] = total
+        moves.start(small_end)
+
+    def end_small():
+        moves.arrive(small_end)
+        out_small[...] = small_last[...]
+
+    def pass_on(way, step):
+        way.arrive(step)
+        if step + 1 < way.steps:
+            way.start(step + 1)
+
+    todo = {(UPSTREAM,): second_upstream, (FAR_START,): start_far, (SMALL, 3): add_small_heads, (SMALL, 4): end_small}
+    for i in range(3):
+        todo[SMALL, i] = functools.partial(add_small, i)
+    for name, way in ((RESULT_LINE, line), (OWN_LINE, own_line), (FAR_LINE, far_line)):
+        for step in range(way.steps):
+            todo[name, step] = functools.partial(pass_on, way, step)
+    for b in range(blocks):
+        todo[MLP_NORM, b] = functools.partial(mlp_norm, b)
+        todo[ATTN_NORM, b] = functools.partial(attention_norm, b)
+        for s in range(heads):
+            todo[MLP_BACK, b, s] = functools.partial(mlp, b, s)
+            todo[ATTN_BACK, b, s] = functools.partial(attention, b, s)
+        for k in (DOWN, UP, ATTN):
+            each = red[b, k]
+            for s in range(heads):
+                todo[ADD_CORE, b, k, s] = functools.partial(each.step_first, s)
+            todo[ADD_FIRST, b, k] = functools.partial(each.step_second, free_sem.at[k] if b else None)
+            todo[ADD_SECOND, b, k] = each.step_heads
+            todo[ADD_HEADS, b, k] = each.step_share
+            todo[SHARE_FIRST, b, k] = each.step_share_first
+            todo[SHARE_CORE, b, k] = each.step_share_core
+            todo[ARRIVED, b, k] = each.end
+    for step in BACKWARD_ORDER:
+        todo[step]()
+    own_result.wait()
     for each in (line, own_line, far_line):
         each.finish()
     moves.finish()
@@ -1327,7 +1305,7 @@
     local = (frame_share, 2 * tubes, patches, width)
     mixed = (frames, tube_share, patches, width)
     kinds = 3 * blocks
-    count = kinds * (2 * heads + 4 + heads - 1) + 2 * heads - 1 + 1 + 4 + heads - 1
+    count = kinds * (3 * heads + 3 + heads - 1) + 2 * heads - 1 + 1 + 4 + heads - 1
     flat = [array for per in saved for array in per]
     return pl.pallas_call(
         lambda *refs: backward_kernel(sz, blocks, frame_share, tube_share, *refs),
@@ -1364,7 +1342,6 @@
                 (mixed, LOW),
                 (mixed, LOW),
                 (local, LOW),
-                (result.shape, LOW),
                 ((3, 2, width, width), LOW),
                 ((3, heads, 4 * q, width), LOW),
                 ((blocks, 3, heads, 2 * q, width), LOW),
@@ -1433,25 +1410,22 @@
     rows = frame_share * tube_size * tubes * patches
     sz = Sizes(rows, width, heads, columns, units, rows // frame_share)
 
-    shard = jnp.concatenate(
-        [w_qkv.transpose(0, 2, 3, 1).reshape(blocks, 3 * columns, width), w_out, w_up, w_down], 1
-    ).reshape(blocks * sz.block_rows, width)
     marks = jnp.broadcast_to(token_mask[0][..., None], (frames, tubes, patches, 128)).astype(LOW)
     full, saved, output, mark_frames = run_forward(
         sz,
         blocks,
         frame_share,
         tube_share,
-        shard,
+        (w_qkv.transpose(0, 2, 3, 1).reshape(blocks, 3 * columns, width), w_out, w_up, w_down),
         tokens[0],
         marks,
-        b_qv.reshape(2 * blocks, columns),
+        b_qv,
         b_up,
-        mask_embed[None],
+        mask_embed,
         norm_gains,
         norm_shifts,
-        b_out[:, None],
-        b_down[:, None],
+        b_out,
+        b_down,
     )
     output, grad_tokens, whole, small = run_backward(
         sz, blocks, frame_share, tube_share, full, saved, cotangent[0], output, mark_frames, norm_gains

time: 424 us -> 363 us (0.86)
  the two profiles are of different devices: /device:TPU:9 before, /device:TPU:25 now
where the time goes in v5:
time: 363 us; the launch traced here: 356 us
  Pallas kernels  334 us (92%)
  local copies, waits for them, and re-layouts  19.8 us (5%)
    pallas_call x1, Pallas kernels, run_backward(): pl.pallas_call(lambda *refs: backward_kernel(sz, blocks, frame_share, tub...  196 us
    pallas_call x1, Pallas kernels, run_forward(): pl.pallas_call(lambda *refs: forward_kernel(sz, blocks, frame_share, tube...  138 us

profile of v5, /device:TPU:25, one launch (start us, length us, event | category | flops | bytes accessed | tf_op | source)
XLA Modules:
  0.0 355.7 jit_solution(13727093680049341635)
XLA Ops:
  0.6 0.8 convert_bitcast_fusion
  1.5 1.1 broadcast_in_dim.11.refs_5_
  2.6 138.1 %forward_both.1 = (bf16[4,2304,768]{2,1,0:T(8,128)(2,1)}, bf16[4,2304,768]{2,1,0:T(8,128)(2,1)}, f32[512,768]{1,0:T(8,128)}, bf16[512,768]{1,0:T(8,128)(2,1)}, b...) custom-call(bf16[2,576,768]{2,1,0:T(8,128)(2,1)} %bitcast.27, ...), custom_call_target="tpu_custom_call" | custom-call | tf_op jit(solution)/shard_map/forward_both/pallas_call | solution.py:893
  140.7 196.0 %backward_both.1 = (bf16[16,8,16,768]{3,2,1,0:T(8,128)(2,1)}, bf16[16,8,16,768]{3,2,1,0:T(8,128)(2,1)}, bf16[4608,768]{1,0:T(8,128)(2,1)}, f32[48,768]{1,0:T(8,128)}) custom-call(bf16[4,2304,768]{2,1,0:T(8,128)(2,1)} %get-tuple-element.35.refs_0_, bf16[4,2304,768]{2,1,0:T(8,128)(2,1)} %get-tuple-element.36.refs_1_, f32[512,768]{1,0:T(8,128)} %get-tuple-element.37.refs_2_, ...), custom_call_target="tpu_custom_call" | custom-call | tf_op jit(solution)/shard_map/backward_both/pallas_call | solution.py:1310
  336.8 0.0 copy-start
  336.8 7.1 %fusion = (f32[2,768,768]{2,1,0:T(8,128)}, f32[2,768,768]{2,1,0:T(8,128)}) fusion(bf16[2,2304,768]{2,1,0:T(8,128)(2,1)} %bitcast.19), kind=kLoop, calls=%fused_computation.5 | loop fusion | bytes 18874368 | tf_op jit(solution)/shard_map/slice | solution.py:1452
  343.9 0.0 copy-done
  343.9 0.0 copy-start.3
  343.9 0.0 copy-start.2
  343.9 2.1 slice.46
  345.9 1.1 slice.47
  347.0 0.0 copy-done.3
  347.1 0.6 copy.29
  347.7 0.6 dynamic-slice_bitcast_fusion
  348.3 0.6 reshape.53
  348.9 0.6 reshape.54
  349.5 0.6 fusion.1
  350.1 0.6 slice_reduce_fusion
  350.7 0.0 copy-done.2
  350.7 0.0 copy-start.1
  350.7 1.7 copy.32
  352.4 1.4 copy-done.1
  353.8 1.7 copy.33
  (6 shorter events, 0.1 us)
Async XLA Ops:
  336.8 7.1 %copy-start = (bf16[4608,768]{1,0:T(8,128)(2,1)S(1)}, bf16[4608,768]{1,0:T(8,128)(2,1)}, u32[]{:S(2)}) copy-start(bf16[4608,768]{1,0:T(8,128)(2,1)} %get-tuple-element.56) | copy-start | bytes 21233668
  343.9 3.2 copy-start.3
  343.9 6.9 %copy-start.2 = (bf16[16,8,16,768]{3,2,1,0:T(8,128)(2,1)S(1)}, bf16[16,8,16,768]{3,2,1,0:T(8,128)(2,1)}, u32[]{:S(2)}) copy-start(bf16[16,8,16,768]{3,2,1,0:T(8,128)(2,1)} %get-tuple-element.53) | copy-start | bytes 9437188
  350.7 3.0 copy-start.1

commit v6 on v5

--- a/solution.py
+++ b/solution.py
@@ -380,7 +380,7 @@
 
 
 DOWN, UP, ATTN = range(3)
-SEND, PASS, FIRST_INPUT, SECOND_INPUT, SPREAD, RESULT, ATTEND, MIDDLE, EXPAND, CONTRACT = range(10)
+SEND, PASS, FIRST_INPUT, SECOND_INPUT, SPREAD, ATTEND, MIDDLE, EXPAND, CONTRACT = range(9)
 FORWARD_ORDER = (
     (SEND, 0), (PASS, 0, 0), (SEND, 1), (FIRST_INPUT,), (PASS, 0, 1), (PASS, 1, 0), (SEND, 2), (PASS, 1, 1),
     (PASS, 0, 2), (PASS, 0, 3), (PASS, 1, 2), (PASS, 2, 0), (SEND, 3), (PASS, 1, 3), (ATTEND, 0, 0), (ATTEND, 0, 1),
@@ -390,30 +390,33 @@
     (CONTRACT, 0, 2), (CONTRACT, 0, 3), (SPREAD,), (PASS, 5, 1), (PASS, 4, 2), (PASS, 4, 3), (PASS, 6, 0),
     (SECOND_INPUT,), (ATTEND, 1, 0), (PASS, 6, 1), (PASS, 5, 2), (ATTEND, 1, 1), (ATTEND, 1, 2), (PASS, 5, 3),
     (ATTEND, 1, 3), (MIDDLE, 1), (EXPAND, 1, 0), (PASS, 6, 2), (EXPAND, 1, 1), (EXPAND, 1, 2), (EXPAND, 1, 3),
-    (PASS, 6, 3), (CONTRACT, 1, 0), (CONTRACT, 1, 1), (CONTRACT, 1, 2), (CONTRACT, 1, 3), (RESULT,),
+    (PASS, 6, 3),
 )
 MLP_BACK, MLP_NORM, ATTN_BACK, ATTN_NORM, UPSTREAM, RESULT_LINE, OWN_LINE, FAR_START, FAR_LINE, SMALL = range(10)
-ADD_CORE, ADD_FIRST, ADD_SECOND, ADD_HEADS, SHARE_FIRST, SHARE_CORE, ARRIVED = range(10, 17)
+ADD_CORE, ADD_FIRST, ADD_SECOND, PASS_HEADS, ADD_HEADS, SHARE_FIRST, SHARE_CORE, ARRIVED, MLP_START, SEND_RESULT = range(10, 20)
 BACKWARD_ORDER = (
-    (MLP_BACK, 1, 0), (MLP_BACK, 1, 1), (ADD_CORE, 1, DOWN, 0), (ADD_CORE, 1, UP, 0), (MLP_BACK, 1, 2),
-    (ADD_CORE, 1, UP, 1), (ADD_CORE, 1, DOWN, 1), (MLP_BACK, 1, 3), (ADD_CORE, 1, DOWN, 2), (ADD_CORE, 1, UP, 2),
-    (MLP_NORM, 1), (RESULT_LINE, 0), (ATTN_BACK, 1, 0), (ATTN_BACK, 1, 1), (ADD_CORE, 1, DOWN, 3),
-    (ADD_CORE, 1, ATTN, 0), (ATTN_BACK, 1, 2), (ADD_CORE, 1, ATTN, 1), (ATTN_BACK, 1, 3), (ADD_CORE, 1, UP, 3),
-    (ATTN_NORM, 1), (RESULT_LINE, 1), (ADD_FIRST, 1, UP), (ADD_FIRST, 1, DOWN), (ADD_CORE, 1, ATTN, 3),
-    (ADD_SECOND, 1, UP), (ADD_CORE, 1, ATTN, 2), (UPSTREAM,), (MLP_BACK, 0, 0), (MLP_BACK, 0, 1),
-    (ADD_CORE, 0, DOWN, 0), (ADD_CORE, 0, UP, 0), (MLP_BACK, 0, 2), (ADD_SECOND, 1, DOWN), (ADD_CORE, 0, DOWN, 1),
-    (ADD_FIRST, 1, ATTN), (ADD_CORE, 0, UP, 1), (MLP_BACK, 0, 3), (MLP_NORM, 0), (ATTN_BACK, 0, 0), (ATTN_BACK, 0, 1),
-    (ADD_CORE, 0, ATTN, 0), (ADD_SECOND, 1, ATTN), (ATTN_BACK, 0, 2), (ADD_CORE, 0, ATTN, 1), (ATTN_BACK, 0, 3),
-    (ATTN_NORM, 0), (ADD_CORE, 0, DOWN, 2), (FAR_START,), (ADD_CORE, 0, DOWN, 3), (ADD_CORE, 0, UP, 3),
-    (ADD_HEADS, 1, ATTN), (ADD_CORE, 0, ATTN, 3), (OWN_LINE, 0), (FAR_LINE, 0), (ADD_CORE, 0, UP, 2),
-    (ADD_FIRST, 0, DOWN), (SHARE_FIRST, 1, ATTN), (ADD_SECOND, 0, DOWN), (ADD_FIRST, 0, UP), (ADD_CORE, 0, ATTN, 2),
-    (SHARE_CORE, 1, ATTN), (FAR_LINE, 1), (ADD_HEADS, 1, DOWN), (SMALL, 0), (ADD_HEADS, 1, UP), (ADD_FIRST, 0, ATTN),
-    (ADD_SECOND, 0, UP), (ADD_HEADS, 0, DOWN), (FAR_LINE, 2), (SHARE_FIRST, 1, UP), (SMALL, 1), (ADD_SECOND, 0, ATTN),
-    (SHARE_FIRST, 1, DOWN), (SMALL, 2), (SHARE_FIRST, 0, DOWN), (ADD_HEADS, 0, UP), (SHARE_FIRST, 0, UP),
-    (SHARE_CORE, 0, DOWN), (SHARE_CORE, 1, DOWN), (OWN_LINE, 1), (ADD_HEADS, 0, ATTN), (RESULT_LINE, 2),
-    (SHARE_CORE, 1, UP), (SHARE_FIRST, 0, ATTN), (SHARE_CORE, 0, UP), (ARRIVED, 0, DOWN), (ARRIVED, 1, ATTN),
-    (SMALL, 3), (SHARE_CORE, 0, ATTN), (ARRIVED, 0, UP), (ARRIVED, 0, ATTN), (ARRIVED, 1, UP), (ARRIVED, 1, DOWN),
-    (SMALL, 4), (OWN_LINE, 2),
+    (MLP_START,), (MLP_BACK, 1, 0), (ADD_CORE, 1, DOWN, 0), (MLP_BACK, 1, 1), (ADD_CORE, 1, UP, 0), (MLP_BACK, 1, 2),
+    (ADD_CORE, 1, UP, 1), (ADD_CORE, 1, DOWN, 1), (MLP_BACK, 1, 3), (SEND_RESULT,), (ADD_CORE, 1, DOWN, 2),
+    (ADD_CORE, 1, UP, 2), (MLP_NORM, 1), (ADD_CORE, 1, DOWN, 3), (ATTN_BACK, 1, 0), (ADD_CORE, 1, UP, 3),
+    (ATTN_BACK, 1, 1), (ADD_CORE, 1, ATTN, 0), (ATTN_BACK, 1, 2), (ADD_FIRST, 1, UP), (ADD_CORE, 1, ATTN, 1),
+    (ATTN_BACK, 1, 3), (ATTN_NORM, 1), (ADD_CORE, 1, ATTN, 3), (ADD_SECOND, 1, UP), (ADD_CORE, 1, ATTN, 2),
+    (RESULT_LINE, 0), (ADD_FIRST, 1, DOWN), (UPSTREAM,), (ADD_FIRST, 1, ATTN), (MLP_BACK, 0, 0), (MLP_BACK, 0, 1),
+    (ADD_SECOND, 1, DOWN), (ADD_CORE, 0, DOWN, 0), (ADD_CORE, 0, UP, 0), (MLP_BACK, 0, 2), (ADD_CORE, 0, UP, 1),
+    (PASS_HEADS, 1, UP, 1), (ADD_CORE, 0, DOWN, 1), (MLP_BACK, 0, 3), (ADD_CORE, 0, UP, 2), (MLP_NORM, 0),
+    (PASS_HEADS, 1, DOWN, 1), (ADD_SECOND, 1, ATTN), (RESULT_LINE, 1), (ATTN_BACK, 0, 0), (ADD_CORE, 0, UP, 3),
+    (ADD_CORE, 0, DOWN, 2), (ATTN_BACK, 0, 1), (ADD_CORE, 0, ATTN, 0), (ATTN_BACK, 0, 2), (ADD_CORE, 0, DOWN, 3),
+    (ADD_CORE, 0, ATTN, 1), (PASS_HEADS, 1, ATTN, 1), (PASS_HEADS, 1, DOWN, 2), (ATTN_BACK, 0, 3), (ATTN_NORM, 0),
+    (PASS_HEADS, 1, ATTN, 2), (ADD_FIRST, 0, UP), (ADD_FIRST, 0, DOWN), (ADD_CORE, 0, ATTN, 2),
+    (ADD_CORE, 0, ATTN, 3), (FAR_START,), (OWN_LINE, 0), (PASS_HEADS, 1, UP, 2), (SMALL, 0), (ADD_SECOND, 0, UP),
+    (RESULT_LINE, 2), (FAR_LINE, 0), (ADD_SECOND, 0, DOWN), (ADD_FIRST, 0, ATTN), (PASS_HEADS, 0, UP, 1),
+    (ADD_HEADS, 1, UP), (ADD_HEADS, 1, ATTN), (ADD_SECOND, 0, ATTN), (OWN_LINE, 1), (SMALL, 1), (SHARE_FIRST, 1, UP),
+    (SHARE_FIRST, 1, ATTN), (ADD_HEADS, 1, DOWN), (PASS_HEADS, 0, DOWN, 1), (PASS_HEADS, 0, UP, 2),
+    (PASS_HEADS, 0, ATTN, 1), (PASS_HEADS, 0, DOWN, 2), (SHARE_FIRST, 1, DOWN), (ADD_HEADS, 0, UP), (SMALL, 2),
+    (ADD_HEADS, 0, DOWN), (SHARE_FIRST, 0, UP), (PASS_HEADS, 0, ATTN, 2), (FAR_LINE, 1), (SHARE_CORE, 1, DOWN),
+    (SHARE_FIRST, 0, DOWN), (SHARE_CORE, 1, UP), (ADD_HEADS, 0, ATTN), (ARRIVED, 1, DOWN), (SHARE_CORE, 1, ATTN),
+    (SHARE_CORE, 0, UP), (SHARE_CORE, 0, DOWN), (SHARE_FIRST, 0, ATTN), (OWN_LINE, 2), (ARRIVED, 1, ATTN),
+    (ARRIVED, 0, DOWN), (ARRIVED, 0, UP), (FAR_LINE, 2), (SMALL, 3), (ARRIVED, 1, UP), (SHARE_CORE, 0, ATTN),
+    (SMALL, 4), (ARRIVED, 0, ATTN),
 )
 
 GELU_A = 0.7978845608028654
@@ -508,7 +511,8 @@
     grad_active = dot(low, w_ref[sz.width : sz.width + sz.units, :], NT)
     du_ref[...] = (grad_active * as_ref[1].astype(F32)).astype(LOW)
     sum_row[...] = jnp.sum(du_ref[...].astype(F32), 0, keepdims=True)
-    down_ref[...] = dot(as_ref[0], low, TN).astype(LOW)
+    if down_ref is not None:
+        down_ref[...] = dot(as_ref[0], low, TN).astype(LOW)
     up_ref[...] = dot(n2_ref[...], du_ref[...], TN).astype(LOW)
     dn_ref[...] += dot(du_ref[...], w_ref[0 : sz.width, :], NT)
 
@@ -630,6 +634,15 @@
     def __init__(self, send_sem, recv_sem):
         self.send_sem, self.recv_sem, self.count, self.sent = send_sem, recv_sem, 0, {}
 
+    def reserve(self):
+        self.count += 1
+        return self.count - 1
+
+    def one(self, n, src, dst, target):
+        return pltpu.make_async_remote_copy(
+            src, dst, self.send_sem.at[n], self.recv_sem.at[n], device_id=target, device_id_type=MESH
+        )
+
     def phase(self, copies):
         made = []
         for src, dst, landing, target in copies:
@@ -719,7 +732,7 @@
     (w_qkv, w_out, w_up, w_down, tokens, marks, b_qv, b_up, embed, gains, shifts, b_out, b_down), refs = refs[:13], refs[13:]
     fulls, refs = refs[:blocks], refs[blocks:]
     saved, refs = [refs[7 * b : 7 * b + 7] for b in range(blocks)], refs[7 * blocks :]
-    (result, frame_marks), refs = refs[:2], refs[2:]
+    (frame_marks,), refs = refs[:1], refs[1:]
     w = refs[:blocks]
     (
         frames, bqv, bup, x, n, t, p, m, n2, act, y, y_low, second, send_sem, recv_sem, local_sem, save_sem,
@@ -848,12 +861,6 @@
             second.at[pl.ds((2 * z + yy) * frame_share, frame_share)],
         )
 
-    def finish_second():
-        for j in range(tube_share):
-            at = slice(j * length, (j + 1) * length)
-            second[:, j] = y[at, :].astype(LOW).reshape(second.shape[0], second.shape[2], sz.width)
-        kept.append(saves.start(second, result))
-
     def advance(piece, phase):
         moves.arrive(work[piece][phase])
         if phase < 3:
@@ -861,7 +868,7 @@
         else:
             kept.extend(keep(piece))
 
-    steps = {(FIRST_INPUT,): first_input, (SPREAD,): spread_first, (SECOND_INPUT,): second_input, (RESULT,): finish_second}
+    steps = {(FIRST_INPUT,): first_input, (SPREAD,): spread_first, (SECOND_INPUT,): second_input}
     for piece in range(len(work)):
         steps[SEND, piece] = functools.partial(begin_piece, piece)
         for phase in range(4):
@@ -893,9 +900,9 @@
     out = pl.pallas_call(
         lambda *refs: forward_kernel(sz, blocks, frame_share, tube_share, *refs),
         name="forward_both",
-        out_shape=structs([full] * blocks + saved * blocks + [(mixed, LOW), (whole_frames + (128,), LOW)]),
+        out_shape=structs([full] * blocks + saved * blocks + [(whole_frames + (128,), LOW)]),
         in_specs=[hbm] * 8 + [vmem] * 5,
-        out_specs=[hbm] * (blocks + 7 * blocks + 1) + [vmem],
+        out_specs=[hbm] * (blocks + 7 * blocks) + [vmem],
         scratch_shapes=vmems(
             [full] * blocks
             + [
@@ -922,7 +929,7 @@
     )(*weights, tokens, marks, b_qv, b_up, embed, gains, shifts, b_out, b_down)
     fulls, out = out[:blocks], out[blocks:]
     saved = [out[7 * b : 7 * b + 7] for b in range(blocks)]
-    return fulls, saved, out[-2], out[-1]
+    return fulls, saved, out[-1]
 
 
 class Line:
@@ -983,12 +990,8 @@
         self.second = moves.phase(
             [(self.first_buf.at[s, cut(1 - j, 1), :], self.second_buf.at[s], self.second_buf.at[s], place.second) for s in shards]
         )
-        self.heads = moves.phase(
-            [
-                (self.second_buf.at[lax.rem(z + d, heads)], self.head_buf.at[d - 1], self.head_buf.at[d - 1], place.head(d))
-                for d in range(1, heads)
-            ]
-        )
+        self.to_right = moves.reserve()
+        self.to_left = moves.reserve()
         a, mine = 4 * c, 2 * i + j
         self.share_second = moves.phase([(final_buf, row(a + mine, 1), row(a + 2 * i + 1 - j, 1), place.second)])
         self.share_first = moves.phase([(row(a + 2 * i, 2), row(a + 2 * i, 2), row(a + 2 * (1 - i), 2), place.first)])
@@ -1016,16 +1019,70 @@
         for s in range(self.place.heads):
             self.moves.arrive([self.second[s]])
             self.second_buf[s] = self.second_buf[s] + self.first_buf[s, self.subpart, :]
-        self.moves.start(self.heads)
+        last = self.place.heads - 1
+        pl.when(self.place.z == 0)(functools.partial(self.send_right, 0))
+        pl.when(self.place.z == last)(functools.partial(self.send_left, last))
+
+    def right_copy(self, z):
+        return self.moves.one(
+            self.to_right, self.second_buf.at[z + 1 :], self.head_buf.at[z + 2 :], self.place.head(1)
+        )
+
+    def left_copy(self, z):
+        return self.moves.one(self.to_left, self.second_buf.at[:z], self.head_buf.at[:z], self.place.head(-1))
+
+    def send_right(self, z):
+        self.right_copy(z).start()
+
+    def send_left(self, z):
+        self.left_copy(z).start()
+
+    def from_left(self, z):
+        self.right_copy(z - 1).wait_recv()
+        for s in range(z + 1, self.place.heads):
+            self.second_buf[s] = self.second_buf[s] + self.head_buf[s + 1]
+        if z < self.place.heads - 1:
+            self.send_right(z)
+
+    def from_right(self, z):
+        self.left_copy(z + 1).wait_recv()
+        for s in range(z):
+            self.second_buf[s] = self.second_buf[s] + self.head_buf[s]
+        if z > 0:
+            self.send_left(z)
+
+    def step_pass(self, hop):
+        heads = self.place.heads
+        pl.when(self.place.z == hop)(functools.partial(self.from_left, hop))
+        pl.when(self.place.z == heads - 1 - hop)(functools.partial(self.from_right, heads - 1 - hop))
 
     def step_share(self):
-        self.moves.arrive(self.heads)
-        total = self.second_buf[self.place.z].astype(F32)
-        for d in range(self.place.heads - 1):
-            total += self.head_buf[d].astype(F32)
-        self.final_buf[...] = total.astype(LOW)
+        z, last = self.place.z, self.place.heads - 1
+        self.step_pass(last)
+
+        @pl.when(z == 0)
+        def _():
+            self.final_buf[...] = self.second_buf[0] + self.head_buf[0]
+
+        @pl.when(z == last)
+        def _():
+            self.final_buf[...] = self.second_buf[last] + self.head_buf[last + 1]
+
+        @pl.when((z > 0) & (z < last))
+        def _():
+            total = self.second_buf[z].astype(F32) + self.head_buf[z].astype(F32)
+            self.final_buf[...] = (total + self.head_buf[z + 1].astype(F32)).astype(LOW)
+
         self.keep.start()
         self.moves.start(self.share_second)
+
+    def finish(self):
+        last = self.place.heads - 1
+        for z in range(last + 1):
+            if z < last:
+                pl.when(self.place.z == z)(lambda z=z: self.right_copy(z).wait_send())
+            if z > 0:
+                pl.when(self.place.z == z)(lambda z=z: self.left_copy(z).wait_send())
 
     def step_share_first(self):
         self.keep.wait()
@@ -1047,10 +1104,10 @@
 def backward_kernel(sz, blocks, frame_share, tube_share, *refs):
     fulls, refs = refs[:blocks], refs[blocks:]
     saved, refs = [refs[7 * b : 7 * b + 7] for b in range(blocks)], refs[7 * blocks :]
-    (cotangent, result, marks, gains), refs = refs[:4], refs[4:]
+    (cotangent, marks, gains, b_down), refs = refs[:4], refs[4:]
     (out_result, out_tokens, out_grads, out_small), refs = refs[:4], refs[4:]
     (
-        wm, act, wa, t, p, m, n2, n, x, low, dn, dm, du, do, dq, dk, dv, cot, dx_low, back,
+        wm, act, wa, t, p, m, n2, n, x, low, dn, dm, du, do, dq, dk, dv, cot, dx_low, back, result,
         grads, core_buf, first_buf, second_buf, head_buf, final_buf, small, small_in, small_heads, small_last,
         send_sem, recv_sem, line_sem, load_sem, copy_sem, final_sem, free_sem,
     ) = refs
@@ -1130,36 +1187,58 @@
         ]
     )
 
-    line.start(0)
     first_load.wait()
     frames = cot.shape[0]
     for j in range(tube_share):
         low[j * length : (j + 1) * length, :] = cot[:, j].reshape(length, width)
-    own_result = loads.start(result, tube_region(z))
+    own_result = []
+
+    def send_result():
+        for j in range(tube_share):
+            at = slice(j * length, (j + 1) * length)
+            result[:, j] = dm[at, :].astype(LOW).reshape(frames, length // frames, width)
+        line.start(0)
+        own_result.append(loads.start(result, tube_region(z)))
+
+    def mlp_start():
+        begin_mlp(1)
+        grads[DOWN, 0] = dot(act[0, 0], low[...], TN).astype(LOW)
+        red[1, DOWN].give(0)
 
     def row(r, columns=None):
         return small.at[r : r + 1, :] if columns is None else small.at[r : r + 1, 0:columns]
 
+    def begin_mlp(b):
+        row(BDOWN_ROW + b)[...] = jnp.sum(low[...].astype(F32), 0, keepdims=True)
+        dn[...] = jnp.zeros_like(dn)
+        for copy in norm_loads[b]:
+            copy.wait()
+        if b:
+            dm[...] = m[...] + b_down[b : b + 1, :]
+        ready((1 - b) * 2 * heads)
+
     def mlp(b, s):
-        if s == 0:
-            row(BDOWN_ROW + b)[...] = jnp.sum(low[...].astype(F32), 0, keepdims=True)
-            dn[...] = jnp.zeros_like(dn)
-            for copy in norm_loads[b]:
-                copy.wait()
-        ready((1 - b) * 2 * heads + s)
+        if s:
+            ready((1 - b) * 2 * heads + s)
+        elif b == 0:
+            begin_mlp(b)
         for k in (DOWN, UP):
             if s >= 2:
                 moves.left([red[b, k].core[s - 2]])
             elif b == 0:
                 moves.left([red[1, k].core[s + heads - 2]])
+        first = (b, s) == (1, 0)
+        slot = s % 2
         backward_mlp(
-            sz, wm.at[s % 2], act.at[s % 2], low, n2, du, dn, grads.at[DOWN, s % 2], grads.at[UP, s % 2],
+            sz, wm.at[slot], act.at[slot], low, n2, du, dn, None if first else grads.at[DOWN, slot], grads.at[UP, slot],
             row(BUP_ROW + b * heads + s),
         )
-        for k in (DOWN, UP):
+        for k in (UP,) if first else (DOWN, UP):
             if s == 0 and b == 0:
                 pl.semaphore_wait(free_sem.at[k], 1)
             red[b, k].give(s)
+        if b:
+            dm[...] += dot(act[slot, 0], wm[slot, width : width + sz.units, :], NN)
 
     def mlp_norm(b):
         norm_back_rows(
@@ -1267,7 +1346,7 @@
         if step + 1 < way.steps:
             way.start(step + 1)
 
-    todo = {(UPSTREAM,): second_upstream, (FAR_START,): start_far, (SMALL, 3): add_small_heads, (SMALL, 4): end_small}
+    todo = {(UPSTREAM,): second_upstream, (MLP_START,): mlp_start, (SEND_RESULT,): send_result, (FAR_START,): start_far, (SMALL, 3): add_small_heads, (SMALL, 4): end_small}
     for i in range(3):
         todo[SMALL, i] = functools.partial(add_small, i)
     for name, way in ((RESULT_LINE, line), (OWN_LINE, own_line), (FAR_LINE, far_line)):
@@ -1285,19 +1364,22 @@
                 todo[ADD_CORE, b, k, s] = functools.partial(each.step_first, s)
             todo[ADD_FIRST, b, k] = functools.partial(each.step_second, free_sem.at[k] if b else None)
             todo[ADD_SECOND, b, k] = each.step_heads
+            for hop in range(1, heads - 1):
+                todo[PASS_HEADS, b, k, hop] = functools.partial(each.step_pass, hop)
             todo[ADD_HEADS, b, k] = each.step_share
             todo[SHARE_FIRST, b, k] = each.step_share_first
             todo[SHARE_CORE, b, k] = each.step_share_core
             todo[ARRIVED, b, k] = each.end
     for step in BACKWARD_ORDER:
         todo[step]()
-    own_result.wait()
-    for each in (line, own_line, far_line):
+    for copy in own_result:
+        copy.wait()
+    for each in (line, own_line, far_line, *red.values()):
         each.finish()
     moves.finish()
 
 
-def run_backward(sz, blocks, frame_share, tube_share, fulls, saved, cotangent, result, marks, gains):
+def run_backward(sz, blocks, frame_share, tube_share, fulls, saved, cotangent, marks, gains, b_down):
     heads, width, rows, cols = sz.shards, sz.width, sz.rows, sz.columns
     frames, tubes, patches = cotangent.shape[:3]
     hbm, vmem = pl.BlockSpec(memory_space=pl.ANY), pl.BlockSpec(memory_space=pltpu.VMEM)
@@ -1305,7 +1387,7 @@
     local = (frame_share, 2 * tubes, patches, width)
     mixed = (frames, tube_share, patches, width)
     kinds = 3 * blocks
-    count = kinds * (3 * heads + 3 + heads - 1) + 2 * heads - 1 + 1 + 4 + heads - 1
+    count = kinds * (3 * heads + 3 + 2) + 2 * heads - 1 + 1 + 4 + heads - 1
     flat = [array for per in saved for array in per]
     return pl.pallas_call(
         lambda *refs: backward_kernel(sz, blocks, frame_share, tube_share, *refs),
@@ -1318,7 +1400,7 @@
                 ((SMALL_ROWS, width), F32),
             ]
         ),
-        in_specs=[hbm] * (blocks + len(flat) + 2) + [vmem] * 2,
+        in_specs=[hbm] * (blocks + len(flat) + 1) + [vmem] * 3,
         out_specs=[hbm] * 3 + [vmem],
         scratch_shapes=vmems(
             [
@@ -1342,11 +1424,12 @@
                 (mixed, LOW),
                 (mixed, LOW),
                 (local, LOW),
+                (mixed, LOW),
                 ((3, 2, width, width), LOW),
                 ((3, heads, 4 * q, width), LOW),
                 ((blocks, 3, heads, 2 * q, width), LOW),
                 ((blocks, 3, heads, q, width), LOW),
-                ((blocks, 3, heads - 1, q, width), LOW),
+                ((blocks, 3, heads + 1, q, width), LOW),
                 ((blocks, 3, q, width), LOW),
                 ((SMALL_ROWS, width), F32),
                 ((3, SMALL_ROWS, width), F32),
@@ -1366,7 +1449,91 @@
         compiler_params=pltpu.CompilerParams(
             collective_id=1, has_side_effects=True, vmem_limit_bytes=63 * 2**20
         ),
-    )(*fulls, *flat, cotangent, result, marks, gains)
+    )(*fulls, *flat, cotangent, marks, gains, b_down)
+
+
+def finish(sz, blocks, output, tokens, whole, small):
+    heads, width, cols, units = sz.shards, sz.width, sz.columns, sz.units
+    parts = 4
+
+    def kernel(o_in, t_in, a_in, c_in, u_in, d_in, small, o_out, t_out, embed, gain, shift, a, bqv, c, bout, u, bup, d, bdown):
+        for src, dst in ((o_in, o_out), (t_in, t_out)):
+            dst[...] = src[...]
+        for src, dst in ((a_in, a), (c_in, c), (u_in, u), (d_in, d)):
+            dst[...] = src[...].astype(F32)
+
+        @pl.when((pl.program_id(0) == 0) & (pl.program_id(1) == 0))
+        def _():
+            head = lax.axis_index("head")
+            embed[...] = small[0:1, :]
+            for b in range(blocks):
+                for norm in range(2):
+                    gain[b, norm : norm + 1, :] = small[GAIN_ROW + 2 * b + norm : GAIN_ROW + 2 * b + norm + 1, :]
+                    shift[b, norm : norm + 1, :] = small[SHIFT_ROW + 2 * b + norm : SHIFT_ROW + 2 * b + norm + 1, :]
+                bout[b : b + 1, :] = small[BOUT_ROW + b : BOUT_ROW + b + 1, :]
+                bdown[b : b + 1, :] = small[BDOWN_ROW + b : BDOWN_ROW + b + 1, :]
+                bup[b : b + 1, :] = small[pl.ds(BUP_ROW + b * heads + head, 1), :]
+                for i in range(2):
+                    bqv[b, i : i + 1, :] = small[pl.ds(BQV_ROW + 2 * (b * heads + head) + i, 1), 0:cols]
+
+    def rows(size, first):
+        return pl.BlockSpec((1, size // parts, width), lambda b, i: (b, first * parts // size + i, 0))
+
+    def kept(*shape):
+        return pl.BlockSpec(shape, lambda b, i: (0,) * len(shape))
+
+    share = output.shape[0] // (blocks * parts)
+    cut = pl.BlockSpec((share,) + output.shape[1:], lambda b, i: (b * parts + i, 0, 0, 0))
+    pair, triple = (blocks, width), (blocks, 2, width)
+    sizes = (3 * cols, cols, width, units)
+    shapes = [(output.shape, LOW), (output.shape, LOW)] + [
+        (s, F32)
+        for s in (
+            (1, width),
+            triple,
+            triple,
+            (blocks, sizes[0], width),
+            (blocks, 2, cols),
+            (blocks, sizes[1], width),
+            pair,
+            (blocks, sizes[2], width),
+            pair,
+            (blocks, sizes[3], width),
+            pair,
+        )
+    ]
+    out = [rows(size, 0) for size in sizes]
+    return pl.pallas_call(
+        kernel,
+        name="finish",
+        grid=(blocks, parts),
+        out_shape=structs(shapes),
+        in_specs=[
+            cut,
+            cut,
+            rows(sizes[0], 0),
+            rows(sizes[1], sz.out_row),
+            rows(sizes[2], sz.up_row),
+            rows(sizes[3], sz.down_row),
+            kept(SMALL_ROWS, width),
+        ],
+        out_specs=[
+            cut,
+            cut,
+            kept(1, width),
+            kept(*triple),
+            kept(*triple),
+            out[0],
+            kept(blocks, 2, cols),
+            out[1],
+            kept(*pair),
+            out[2],
+            kept(*pair),
+            out[3],
+            kept(*pair),
+        ],
+        compiler_params=pltpu.CompilerParams(vmem_limit_bytes=62 * 2**20),
+    )(output, tokens, whole, whole, whole, whole, small)
 
 
 def fits_local(arrays, clip_size, tube_size, head_size):
@@ -1411,7 +1578,7 @@
     sz = Sizes(rows, width, heads, columns, units, rows // frame_share)
 
     marks = jnp.broadcast_to(token_mask[0][..., None], (frames, tubes, patches, 128)).astype(LOW)
-    full, saved, output, mark_frames = run_forward(
+    full, saved, mark_frames = run_forward(
         sz,
         blocks,
         frame_share,
@@ -1428,29 +1595,25 @@
         b_down,
     )
     output, grad_tokens, whole, small = run_backward(
-        sz, blocks, frame_share, tube_share, full, saved, cotangent[0], output, mark_frames, norm_gains
-    )
-    rows_of = lambda start, size: small[start : start + size]
-    bup_grad = rows_of(BUP_ROW, blocks * heads).reshape(blocks, heads, units)
-    bqv_grad = rows_of(BQV_ROW, 2 * blocks * heads)[:, :columns].reshape(blocks, heads, 2, columns)
-    of_head = lambda array: lax.dynamic_index_in_dim(array, head, 1, False)
-    whole = whole.astype(F32)
-    whole = whole.reshape(blocks, sz.block_rows, width)
-    qkv_grad = whole[:, : sz.out_row].reshape(blocks, 3, columns, width).transpose(0, 3, 1, 2)
+        sz, blocks, frame_share, tube_share, full, saved, cotangent[0], mark_frames, norm_gains, b_down
+    )
+    out = finish(sz, blocks, output, grad_tokens, whole.reshape(blocks, sz.block_rows, width), small)
+    output, grad_tokens, embed, gains, shifts, qkv_grad, bqv, out_grad, bout, up_grad, bup, down_grad, bdown = out
+    qkv_grad = qkv_grad.reshape(blocks, 3, columns, width).transpose(0, 3, 1, 2)
     return (
         output[None],
         grad_tokens[None],
-        small[0],
-        rows_of(GAIN_ROW, 2 * blocks).reshape(blocks, 2, width),
-        rows_of(SHIFT_ROW, 2 * blocks).reshape(blocks, 2, width),
+        embed.reshape(width),
+        gains,
+        shifts,
         qkv_grad,
-        of_head(bqv_grad),
-        whole[:, sz.out_row : sz.up_row],
-        rows_of(BOUT_ROW, blocks),
-        whole[:, sz.up_row : sz.down_row],
-        of_head(bup_grad),
-        whole[:, sz.down_row :],
-        rows_of(BDOWN_ROW, blocks),
+        bqv,
+        out_grad,
+        bout,
+        up_grad,
+        bup,
+        down_grad,
+        bdown,
     )
 
 

time: 363 us -> 353 us (0.972)
  the two profiles are of different devices: /device:TPU:25 before, /device:TPU:1 now
where the time goes in v6:
time: 353 us; the launch traced here: 346 us
  Pallas kernels  342 us (97%)
    pallas_call x1, Pallas kernels, run_backward(): pl.pallas_call(lambda *refs: backward_kernel(sz, blocks, frame_share, tub...  193 us
    pallas_call x1, Pallas kernels, run_forward(): pl.pallas_call(lambda *refs: forward_kernel(sz, blocks, frame_share, tube...  136 us
    pallas_call x1, Pallas kernels, finish(): pl.pallas_call(kernel, name='finish', grid=(blocks, parts), out_shape=str...  13.3 us

profile of v6, /device:TPU:1, one launch (start us, length us, event | category | flops | bytes accessed | tf_op | source)
XLA Modules:
  0.0 345.8 jit_solution(9689864826843336727)
XLA Ops:
  0.6 0.8 convert_bitcast_fusion
  1.5 1.1 broadcast_in_dim.11.refs_5_
  2.6 135.9 %forward_both.1 = (bf16[4,2304,768]{2,1,0:T(8,128)(2,1)}, bf16[4,2304,768]{2,1,0:T(8,128)(2,1)}, f32[512,768]{1,0:T(8,128)}, bf16[512,768]{1,0:T(8,128)(2,1)}, b...) custom-call(bf16[2,576,768]{2,1,0:T(8,128)(2,1)} %bitcast.19, ...), custom_call_target="tpu_custom_call" | custom-call | tf_op jit(solution)/shard_map/forward_both/pallas_call | solution.py:900
  138.5 192.5 %backward_both.1 = (bf16[16,8,16,768]{3,2,1,0:T(8,128)(2,1)}, bf16[16,8,16,768]{3,2,1,0:T(8,128)(2,1)}, bf16[4608,768]{1,0:T(8,128)(2,1)}, f32[48,768]{1,0:T(8,128)}) custom-call(bf16[4,2304,768]{2,1,0:T(8,128)(2,1)} %get-tuple-element.47.refs_0_, bf16[4,2304,768]{2,1,0:T(8,128)(2,1)} %get-tuple-element.48.refs_1_, f32[512,768]{1,0:T(8,128)} %get-tuple-element.49.refs_2_, ...), custom_call_target="tpu_custom_call" | custom-call | tf_op jit(solution)/shard_map/backward_both/pallas_call | solution.py:1392
  331.0 13.3 %finish.1 = (bf16[16,8,16,768]{3,2,1,0:T(8,128)(2,1)}, bf16[16,8,16,768]{3,2,1,0:T(8,128)(2,1)}, f32[1,768]{1,0:T(1,128)}, f32[2,2,768]{2,1,0:T(2,128)}, f32[2,2...) custom-call(bf16[16,8,16,768]{3,2,1,0:T(8,128)(2,1)} %get-tuple-elem, ...), custom_call_target="tpu_custom_call" | custom-call | tf_op jit(solution)/shard_map/finish/pallas_call | solution.py:1506
  344.3 1.3 reduce

commit v7 on v6

--- a/solution.py
+++ b/solution.py
@@ -717,6 +717,17 @@
     ]
 
 
+def masked_rows(rows, marks_ref):
+    patches = marks_ref.shape[-1]
+    marks = marks_ref[...].astype(F32).reshape(rows // patches, patches).astype(LOW)
+    group = lax.div(lax.broadcasted_iota(jnp.int32, (rows, rows // patches), 0), patches)
+    spread = (group == lax.broadcasted_iota(jnp.int32, (rows, rows // patches), 1)).astype(F32).astype(LOW)
+    wide = dot(spread, marks, NN)
+    lane = lax.broadcasted_iota(jnp.int32, (rows, patches), 1)
+    mine = lane == lax.rem(lax.broadcasted_iota(jnp.int32, (rows, patches), 0), patches)
+    return jnp.sum(jnp.where(mine, wide, 0.0), -1, keepdims=True) > 0.5
+
+
 class Saves:
     def __init__(self, sem):
         self.sem, self.count = sem, 0
@@ -841,8 +852,7 @@
         settle(owns)
         moves.arrive(exchange)
         tok = frames[...].astype(F32).reshape(sz.rows, sz.width)
-        mark = frame_marks[...].astype(F32).reshape(sz.rows, 128)[:, 0:1]
-        x[...] = jnp.where(mark > 0.5, embed[...].reshape(1, sz.width), tok)
+        x[...] = jnp.where(masked_rows(sz.rows, frame_marks), embed[...].reshape(1, sz.width), tok)
         early.extend(begin_block(0))
 
     def second_input():
@@ -900,7 +910,7 @@
     out = pl.pallas_call(
         lambda *refs: forward_kernel(sz, blocks, frame_share, tube_share, *refs),
         name="forward_both",
-        out_shape=structs([full] * blocks + saved * blocks + [(whole_frames + (128,), LOW)]),
+        out_shape=structs([full] * blocks + saved * blocks + [(whole_frames, jnp.int32)]),
         in_specs=[hbm] * 8 + [vmem] * 5,
         out_specs=[hbm] * (blocks + 7 * blocks) + [vmem],
         scratch_shapes=vmems(
@@ -1284,7 +1294,7 @@
                 )
             )
             return
-        mark = marks[...].astype(F32).reshape(sz.rows, 128)[:, 0:1] > 0.5
+        mark = masked_rows(sz.rows, marks)
         grad = dm[...]
         row(0)[...] = jnp.sum(jnp.where(mark, grad, 0.0), 0, keepdims=True)
         back[...] = jnp.where(mark, 0.0, grad).astype(LOW).reshape(back.shape)
@@ -1465,7 +1475,7 @@
         @pl.when((pl.program_id(0) == 0) & (pl.program_id(1) == 0))
         def _():
             head = lax.axis_index("head")
-            embed[...] = small[0:1, :]
+            embed[...] = small[0, :]
             for b in range(blocks):
                 for norm in range(2):
                     gain[b, norm : norm + 1, :] = small[GAIN_ROW + 2 * b + norm : GAIN_ROW + 2 * b + norm + 1, :]
@@ -1489,7 +1499,7 @@
     shapes = [(output.shape, LOW), (output.shape, LOW)] + [
         (s, F32)
         for s in (
-            (1, width),
+            (width,),
             triple,
             triple,
             (blocks, sizes[0], width),
@@ -1520,7 +1530,7 @@
         out_specs=[
             cut,
             cut,
-            kept(1, width),
+            kept(width),
             kept(*triple),
             kept(*triple),
             out[0],
@@ -1577,7 +1587,6 @@
     rows = frame_share * tube_size * tubes * patches
     sz = Sizes(rows, width, heads, columns, units, rows // frame_share)
 
-    marks = jnp.broadcast_to(token_mask[0][..., None], (frames, tubes, patches, 128)).astype(LOW)
     full, saved, mark_frames = run_forward(
         sz,
         blocks,
@@ -1585,7 +1594,7 @@
         tube_share,
         (w_qkv.transpose(0, 2, 3, 1).reshape(blocks, 3 * columns, width), w_out, w_up, w_down),
         tokens[0],
-        marks,
+        token_mask[0],
         b_qv,
         b_up,
         mask_embed,
@@ -1603,7 +1612,7 @@
     return (
         output[None],
         grad_tokens[None],
-        embed.reshape(width),
+        embed,
         gains,
         shifts,
         qkv_grad,

time: 353 us -> 351 us (level)
  no operation moved by 1% of the time
where the time goes in v7:
time: 351 us; the launch traced here: 344 us
  Pallas kernels  343 us (98%)
    pallas_call x1, Pallas kernels, run_backward(): pl.pallas_call(lambda *refs: backward_kernel(sz, blocks, frame_share, tub...  193 us
    pallas_call x1, Pallas kernels, run_forward(): pl.pallas_call(lambda *refs: forward_kernel(sz, blocks, frame_share, tube...  137 us
    pallas_call x1, Pallas kernels, finish(): pl.pallas_call(kernel, name='finish', grid=(blocks, parts), out_shape=str...  13.3 us

profile of v7, /device:TPU:1, one launch (start us, length us, event | category | flops | bytes accessed | tf_op | source)
XLA Modules:
  0.0 344.2 jit_solution(2247092187768589914)
XLA Ops:
  0.6 136.5 %forward_both.1 = (bf16[4,2304,768]{2,1,0:T(8,128)(2,1)}, bf16[4,2304,768]{2,1,0:T(8,128)(2,1)}, f32[512,768]{1,0:T(8,128)}, bf16[512,768]{1,0:T(8,128)(2,1)}, b...) custom-call(bf16[2,576,768]{2,1,0:T(8,128)(2,1)} %bitcast.18, ...), custom_call_target="tpu_custom_call" | custom-call | tf_op jit(solution)/shard_map/forward_both/pallas_call | solution.py:910
  137.2 193.5 %backward_both.1 = (bf16[16,8,16,768]{3,2,1,0:T(8,128)(2,1)}, bf16[16,8,16,768]{3,2,1,0:T(8,128)(2,1)}, bf16[4608,768]{1,0:T(8,128)(2,1)}, f32[48,768]{1,0:T(8,128)}) custom-call(bf16[4,2304,768]{2,1,0:T(8,128)(2,1)} %get-tuple-element.47.refs_0_, bf16[4,2304,768]{2,1,0:T(8,128)(2,1)} %get-tuple-element.48.refs_1_, f32[512,768]{1,0:T(8,128)} %get-tuple-element.49.refs_2_, ...), custom_call_target="tpu_custom_call" | custom-call | tf_op jit(solution)/shard_map/backward_both/pallas_call | solution.py:1402
  330.7 13.3 %finish.1 = (bf16[16,8,16,768]{3,2,1,0:T(8,128)(2,1)}, bf16[16,8,16,768]{3,2,1,0:T(8,128)(2,1)}, f32[768]{0:T(1024)}, f32[2,2,768]{2,1,0:T(2,128)}, f32[2,2,768]...) custom-call(bf16[16,8,16,768]{3,2,1,0:T(8,128)(2,1)} %get-tuple-elem, ...), custom_call_target="tpu_custom_call" | custom-call | tf_op jit(solution)/shard_map/finish/pallas_call | solution.py:1516

commit v8 on v7

--- a/solution.py
+++ b/solution.py
@@ -396,27 +396,27 @@
 ADD_CORE, ADD_FIRST, ADD_SECOND, PASS_HEADS, ADD_HEADS, SHARE_FIRST, SHARE_CORE, ARRIVED, MLP_START, SEND_RESULT = range(10, 20)
 BACKWARD_ORDER = (
     (MLP_START,), (MLP_BACK, 1, 0), (ADD_CORE, 1, DOWN, 0), (MLP_BACK, 1, 1), (ADD_CORE, 1, UP, 0), (MLP_BACK, 1, 2),
-    (ADD_CORE, 1, UP, 1), (ADD_CORE, 1, DOWN, 1), (MLP_BACK, 1, 3), (SEND_RESULT,), (ADD_CORE, 1, DOWN, 2),
-    (ADD_CORE, 1, UP, 2), (MLP_NORM, 1), (ADD_CORE, 1, DOWN, 3), (ATTN_BACK, 1, 0), (ADD_CORE, 1, UP, 3),
-    (ATTN_BACK, 1, 1), (ADD_CORE, 1, ATTN, 0), (ATTN_BACK, 1, 2), (ADD_FIRST, 1, UP), (ADD_CORE, 1, ATTN, 1),
-    (ATTN_BACK, 1, 3), (ATTN_NORM, 1), (ADD_CORE, 1, ATTN, 3), (ADD_SECOND, 1, UP), (ADD_CORE, 1, ATTN, 2),
-    (RESULT_LINE, 0), (ADD_FIRST, 1, DOWN), (UPSTREAM,), (ADD_FIRST, 1, ATTN), (MLP_BACK, 0, 0), (MLP_BACK, 0, 1),
-    (ADD_SECOND, 1, DOWN), (ADD_CORE, 0, DOWN, 0), (ADD_CORE, 0, UP, 0), (MLP_BACK, 0, 2), (ADD_CORE, 0, UP, 1),
-    (PASS_HEADS, 1, UP, 1), (ADD_CORE, 0, DOWN, 1), (MLP_BACK, 0, 3), (ADD_CORE, 0, UP, 2), (MLP_NORM, 0),
-    (PASS_HEADS, 1, DOWN, 1), (ADD_SECOND, 1, ATTN), (RESULT_LINE, 1), (ATTN_BACK, 0, 0), (ADD_CORE, 0, UP, 3),
-    (ADD_CORE, 0, DOWN, 2), (ATTN_BACK, 0, 1), (ADD_CORE, 0, ATTN, 0), (ATTN_BACK, 0, 2), (ADD_CORE, 0, DOWN, 3),
-    (ADD_CORE, 0, ATTN, 1), (PASS_HEADS, 1, ATTN, 1), (PASS_HEADS, 1, DOWN, 2), (ATTN_BACK, 0, 3), (ATTN_NORM, 0),
-    (PASS_HEADS, 1, ATTN, 2), (ADD_FIRST, 0, UP), (ADD_FIRST, 0, DOWN), (ADD_CORE, 0, ATTN, 2),
-    (ADD_CORE, 0, ATTN, 3), (FAR_START,), (OWN_LINE, 0), (PASS_HEADS, 1, UP, 2), (SMALL, 0), (ADD_SECOND, 0, UP),
-    (RESULT_LINE, 2), (FAR_LINE, 0), (ADD_SECOND, 0, DOWN), (ADD_FIRST, 0, ATTN), (PASS_HEADS, 0, UP, 1),
-    (ADD_HEADS, 1, UP), (ADD_HEADS, 1, ATTN), (ADD_SECOND, 0, ATTN), (OWN_LINE, 1), (SMALL, 1), (SHARE_FIRST, 1, UP),
-    (SHARE_FIRST, 1, ATTN), (ADD_HEADS, 1, DOWN), (PASS_HEADS, 0, DOWN, 1), (PASS_HEADS, 0, UP, 2),
-    (PASS_HEADS, 0, ATTN, 1), (PASS_HEADS, 0, DOWN, 2), (SHARE_FIRST, 1, DOWN), (ADD_HEADS, 0, UP), (SMALL, 2),
-    (ADD_HEADS, 0, DOWN), (SHARE_FIRST, 0, UP), (PASS_HEADS, 0, ATTN, 2), (FAR_LINE, 1), (SHARE_CORE, 1, DOWN),
-    (SHARE_FIRST, 0, DOWN), (SHARE_CORE, 1, UP), (ADD_HEADS, 0, ATTN), (ARRIVED, 1, DOWN), (SHARE_CORE, 1, ATTN),
-    (SHARE_CORE, 0, UP), (SHARE_CORE, 0, DOWN), (SHARE_FIRST, 0, ATTN), (OWN_LINE, 2), (ARRIVED, 1, ATTN),
-    (ARRIVED, 0, DOWN), (ARRIVED, 0, UP), (FAR_LINE, 2), (SMALL, 3), (ARRIVED, 1, UP), (SHARE_CORE, 0, ATTN),
-    (SMALL, 4), (ARRIVED, 0, ATTN),
+    (ADD_CORE, 1, DOWN, 1), (ADD_CORE, 1, UP, 1), (MLP_BACK, 1, 3), (ADD_CORE, 1, UP, 2), (ADD_CORE, 1, DOWN, 2),
+    (SEND_RESULT,), (MLP_NORM, 1), (ATTN_BACK, 1, 0), (ADD_CORE, 1, UP, 3), (ADD_CORE, 1, DOWN, 3), (ATTN_BACK, 1, 1),
+    (ADD_CORE, 1, ATTN, 0), (ATTN_BACK, 1, 2), (ADD_CORE, 1, ATTN, 1), (ATTN_BACK, 1, 3), (ADD_CORE, 1, ATTN, 2),
+    (ATTN_NORM, 1), (ADD_CORE, 1, ATTN, 3), (RESULT_LINE, 0), (ADD_FIRST, 1, DOWN), (ADD_FIRST, 1, ATTN),
+    (ADD_FIRST, 1, UP), (UPSTREAM,), (MLP_BACK, 0, 0), (MLP_BACK, 0, 1), (ADD_SECOND, 1, DOWN),
+    (ADD_CORE, 0, DOWN, 0), (ADD_CORE, 0, UP, 0), (MLP_BACK, 0, 2), (ADD_CORE, 0, DOWN, 1), (ADD_SECOND, 1, ATTN),
+    (ADD_CORE, 0, UP, 1), (MLP_BACK, 0, 3), (MLP_NORM, 0), (ATTN_BACK, 0, 0), (ADD_CORE, 0, UP, 3),
+    (ADD_SECOND, 1, UP), (PASS_HEADS, 1, DOWN, 1), (ADD_CORE, 0, DOWN, 2), (ADD_CORE, 0, UP, 2), (RESULT_LINE, 1),
+    (ADD_CORE, 0, DOWN, 3), (ATTN_BACK, 0, 1), (ADD_CORE, 0, ATTN, 0), (ATTN_BACK, 0, 2), (PASS_HEADS, 1, ATTN, 1),
+    (ADD_CORE, 0, ATTN, 1), (ATTN_BACK, 0, 3), (PASS_HEADS, 1, UP, 1), (ATTN_NORM, 0), (ADD_FIRST, 0, UP),
+    (ADD_CORE, 0, ATTN, 2), (PASS_HEADS, 1, ATTN, 2), (PASS_HEADS, 1, DOWN, 2), (FAR_START,), (ADD_CORE, 0, ATTN, 3),
+    (OWN_LINE, 0), (ADD_FIRST, 0, DOWN), (PASS_HEADS, 1, UP, 2), (ADD_SECOND, 0, UP), (SMALL, 0),
+    (ADD_HEADS, 1, ATTN), (ADD_FIRST, 0, ATTN), (FAR_LINE, 0), (ADD_SECOND, 0, DOWN), (SHARE_FIRST, 1, ATTN),
+    (PASS_HEADS, 0, UP, 1), (OWN_LINE, 1), (ADD_HEADS, 1, DOWN), (ADD_SECOND, 0, ATTN), (ADD_HEADS, 1, UP),
+    (PASS_HEADS, 0, DOWN, 1), (SHARE_FIRST, 1, DOWN), (PASS_HEADS, 0, UP, 2), (SMALL, 1), (SHARE_FIRST, 1, UP),
+    (PASS_HEADS, 0, ATTN, 1), (PASS_HEADS, 0, DOWN, 2), (SMALL, 2), (ADD_HEADS, 0, UP), (ADD_HEADS, 0, DOWN),
+    (SHARE_CORE, 1, ATTN), (OWN_LINE, 2), (SHARE_FIRST, 0, UP), (PASS_HEADS, 0, ATTN, 2), (SHARE_FIRST, 0, DOWN),
+    (SHARE_CORE, 1, DOWN), (FAR_LINE, 1), (ADD_HEADS, 0, ATTN), (SMALL, 3), (SHARE_FIRST, 0, ATTN),
+    (SHARE_CORE, 1, UP), (SHARE_CORE, 0, DOWN), (ARRIVED, 1, DOWN), (SMALL, 4), (ARRIVED, 1, UP), (ARRIVED, 1, ATTN),
+    (SHARE_CORE, 0, UP), (SHARE_CORE, 0, ATTN), (ARRIVED, 0, DOWN), (ARRIVED, 0, UP), (FAR_LINE, 2), (RESULT_LINE, 2),
+    (ARRIVED, 0, ATTN),
 )
 
 GELU_A = 0.7978845608028654

time: 351 us -> 353 us (level)
  no operation moved by 1% of the time
where the time goes in v8:
time: 353 us; the launch traced here: 346 us
  Pallas kernels  345 us (98%)
    pallas_call x1, Pallas kernels, run_backward(): pl.pallas_call(lambda *refs: backward_kernel(sz, blocks, frame_share, tub...  195 us
    pallas_call x1, Pallas kernels, run_forward(): pl.pallas_call(lambda *refs: forward_kernel(sz, blocks, frame_share, tube...  137 us
    pallas_call x1, Pallas kernels, finish(): pl.pallas_call(kernel, name='finish', grid=(blocks, parts), out_shape=str...  13.3 us

profile of v8, /device:TPU:1, one launch (start us, length us, event | category | flops | bytes accessed | tf_op | source)
XLA Modules:
  0.0 345.9 jit_solution(17346713097618941477)
XLA Ops:
  0.6 136.5 %forward_both.1 = (bf16[4,2304,768]{2,1,0:T(8,128)(2,1)}, bf16[4,2304,768]{2,1,0:T(8,128)(2,1)}, f32[512,768]{1,0:T(8,128)}, bf16[512,768]{1,0:T(8,128)(2,1)}, b...) custom-call(bf16[2,576,768]{2,1,0:T(8,128)(2,1)} %bitcast.18, ...), custom_call_target="tpu_custom_call" | custom-call | tf_op jit(solution)/shard_map/forward_both/pallas_call | solution.py:910
  137.2 195.1 %backward_both.1 = (bf16[16,8,16,768]{3,2,1,0:T(8,128)(2,1)}, bf16[16,8,16,768]{3,2,1,0:T(8,128)(2,1)}, bf16[4608,768]{1,0:T(8,128)(2,1)}, f32[48,768]{1,0:T(8,128)}) custom-call(bf16[4,2304,768]{2,1,0:T(8,128)(2,1)} %get-tuple-element.47.refs_0_, bf16[4,2304,768]{2,1,0:T(8,128)(2,1)} %get-tuple-element.48.refs_1_, f32[512,768]{1,0:T(8,128)} %get-tuple-element.49.refs_2_, ...), custom_call_target="tpu_custom_call" | custom-call | tf_op jit(solution)/shard_map/backward_both/pallas_call | solution.py:1402
  332.4 13.3 %finish.1 = (bf16[16,8,16,768]{3,2,1,0:T(8,128)(2,1)}, bf16[16,8,16,768]{3,2,1,0:T(8,128)(2,1)}, f32[768]{0:T(1024)}, f32[2,2,768]{2,1,0:T(2,128)}, f32[2,2,768]...) custom-call(bf16[16,8,16,768]{3,2,1,0:T(8,128)(2,1)} %get-tuple-elem, ...), custom_call_target="tpu_custom_call" | custom-call | tf_op jit(solution)/shard_map/finish/pallas_call | solution.py:1516
